TPU v7x, 128 devices: a whole 4x4x4 slice. The times are simulated.
128 devices in a mesh: tile: 16 (over x_lo, y, core), sample: 8 (over z, x_hi).
Axes of the slice: x: 4 (x_hi: 2, x_lo: 2; x = x_hi * 2 + x_lo), y: 4, z: 4, core: 2. Of those that a mesh axis runs over, the one named last changes fastest.
Arguments:
- pair: bfloat16 [256, 256, 128], P('tile', 'sample'), may hold values from -30 to 30
- pair_mask: int32 [256, 256], P('tile', 'sample'), may hold values 0 or 1
- tri_in_w: bfloat16 [128, 512], replicated, may hold values from -0.5 to 0.5
- tri_gate_w: bfloat16 [128, 128], replicated, may hold values from -0.5 to 0.5
- tri_out_w: bfloat16 [128, 128], replicated, may hold values from -0.5 to 0.5
- bias_w: bfloat16 [128, 16], replicated, may hold values from -0.5 to 0.5
- atom_feats: bfloat16 [2048, 128], P('tile'), may hold values from -6 to 6
- atom_to_token: int32 [2048], P('tile'), may hold values from 0 to 255, never falling along the last dimension, each value on 1 to 24 neighbouring positions
- atom_w: bfloat16 [128, 768], replicated, may hold values from -0.5 to 0.5
- tokens: bfloat16 [256, 256, 768], P(('tile', 'sample')), may hold values from -40 to 40
- attention_input_weight: bfloat16 [768, 3072], replicated, may hold values from -2 to 2
- attention_output_weight: bfloat16 [768, 768], replicated, may hold values from -0.21875 to 0.21875
- cot_pair: bfloat16 [256, 256, 128], P('tile', 'sample'), may hold values from -6 to 6
- token_output_cotangent: bfloat16 [256, 256, 768], P(('tile', 'sample')), may hold values from -6 to 6
Outputs:
- pair_next: float32 [256, 256, 128], P('tile', 'sample')
- token_output_rows: float32 [256, 256, 768], P(('tile', 'sample'))
- grad_pair: float32 [256, 256, 128], P('tile', 'sample')
- grad_tokens: float32 [256, 256, 768], P(('tile', 'sample'))
- grad_tri_in_w: float32 [128, 512], replicated
- grad_tri_gate_w: float32 [128, 128], replicated
- grad_tri_out_w: float32 [128, 128], replicated
- grad_bias_w: float32 [128, 16], replicated
- grad_atom_w: float32 [128, 768], replicated
- attention_input_weight_gradient: float32 [768, 3072], replicated
- attention_output_weight_gradient: float32 [768, 768], replicated
Inputs may be any that keep to these rules, and one draw needn't show every extreme that they name: `atom_to_token`: atoms are in order of their tokens; every token has 1 to 24 atoms.
All inputs are finite; a program needn't handle non-finite values. No bound on the sum of `pair_mask` on one device may be relied on, other than what follows from the above.
Results may differ from a plain program's by a relative error of at most 0.034.
Values may be sent and summed in bfloat16 or wider, within the bound.
A program may use at most 128 MiB of HBM per device.

v0:
```python
import functools
import math

import jax
import jax.numpy as jnp
from jax import lax
from jax.experimental import pallas as pl
from jax.experimental.pallas import tpu as pltpu
from jax.sharding import PartitionSpec as P

EPSILON = 1e-05
N_TILE = 16
N_SAMPLE = 8
N_CHIP = 8
MESH = pl.DeviceIdType.MESH
BF16 = jnp.bfloat16
F32 = jnp.float32
HIGHEST = lax.Precision.HIGHEST


def enter(t, s):
    barrier = pltpu.get_barrier_semaphore()
    for k in range(1, N_SAMPLE):
        pl.semaphore_signal(
            barrier, inc=1, device_id=(t, lax.rem(s + k, N_SAMPLE)), device_id_type=MESH
        )
    for k in range(1, N_TILE):
        pl.semaphore_signal(
            barrier, inc=1, device_id=(lax.rem(t + k, N_TILE), s), device_id_type=MESH
        )
    pl.semaphore_wait(barrier, N_SAMPLE + N_TILE - 2)


def wait_bytes(ref, sem):
    pltpu.make_async_copy(ref, ref, sem).wait()


def send(src, dst, send_sem, recv_sem, t, s):
    pltpu.make_async_remote_copy(
        src, dst, send_sem, recv_sem, device_id=(t, s), device_id_type=MESH
    ).start()


def exchange_kernel(x, out, mid, send_sem, recv_sem, local_sem):
    t, s = lax.axis_index("tile"), lax.axis_index("sample")
    enter(t, s)
    for k in range(1, N_SAMPLE):
        d = lax.rem(s + k, N_SAMPLE)
        send(x.at[:, d], mid.at[:, s], send_sem.at[0], recv_sem.at[0], t, d)
    own = pltpu.make_async_copy(x.at[:, s], mid.at[:, s], local_sem)
    own.start()
    own.wait()
    wait_bytes(mid.at[:, pl.ds(0, N_SAMPLE - 1)], recv_sem.at[0])
    for k in range(1, N_TILE):
        d = lax.rem(t + k, N_TILE)
        send(mid.at[d], out.at[t], send_sem.at[1], recv_sem.at[1], d, s)
    own = pltpu.make_async_copy(mid.at[t], out.at[t], local_sem)
    own.start()
    own.wait()
    wait_bytes(out.at[pl.ds(0, N_TILE - 1)], recv_sem.at[1])
    wait_bytes(mid.at[:, pl.ds(0, N_SAMPLE - 1)], send_sem.at[0])
    wait_bytes(out.at[pl.ds(0, N_TILE - 1)], send_sem.at[1])


def exchange(x, collective_id):
    return pl.pallas_call(
        exchange_kernel,
        out_shape=jax.ShapeDtypeStruct(x.shape, x.dtype),
        in_specs=[pl.BlockSpec(memory_space=pltpu.VMEM)],
        out_specs=pl.BlockSpec(memory_space=pltpu.VMEM),
        scratch_shapes=[
            pltpu.VMEM(x.shape, x.dtype),
            pltpu.SemaphoreType.DMA((2,)),
            pltpu.SemaphoreType.DMA((2,)),
            pltpu.SemaphoreType.DMA,
        ],
        compiler_params=pltpu.CompilerParams(
            collective_id=collective_id, has_side_effects=True, vmem_limit_bytes=32 << 20
        ),
    )(x)


def dot(a, b):
    return jnp.dot(a, b, preferred_element_type=F32)


def dot_t(a, b):
    return lax.dot_general(a, b, (((1,), (1,)), ((), ())), preferred_element_type=F32)


def t_dot(a, b):
    return lax.dot_general(a, b, (((0,), (0,)), ((), ())), preferred_element_type=F32)


HEAD = 48
GROUP = 4
LANES = 32


def place_lanes(parts, first):
    group_of = lax.broadcasted_iota(jnp.int32, parts[0].shape, 1) // LANES
    result = None
    for i in range(4):
        shift = (i - first) % 4 * LANES
        moved = pltpu.roll(parts[i], shift, 1) if shift else parts[i]
        result = moved if result is None else jnp.where(group_of == i, moved, result)
    return result


def panel_of(arrived, first, step, panel):
    for part in range(4):
        rows = [
            arrived[part, pl.ds(first + s * (step // 8), 16, stride=step), :] for s in range(8)
        ]
        for i in range(4):
            for half in range(2):
                panel[half, pl.ds(part * 4 + i, 16, stride=16), :] = place_lanes(
                    rows[half * 4 : half * 4 + 4], i
                )


def blocks_of(panel, store):
    for half in range(2):
        for part in range(4):
            rows = [panel[half, pl.ds(part * 4 + i, 16, stride=16), :] for i in range(4)]
            for q in range(4):
                store(half * 4 + q, pl.ds(part * 128, 128), place_lanes(rows, q))


def split_lanes(values, ref):
    for part in range(ref.shape[0]):
        ref[part] = values[:, part * 128 : part * 128 + 128]


def joined(ref):
    return jnp.concatenate([ref[0], ref[1]], axis=1)


def norm_rows(values, axis):
    centered = values - jnp.mean(values, axis=axis, keepdims=True)
    inverse = lax.rsqrt(jnp.mean(centered * centered, axis=axis, keepdims=True) + EPSILON)
    return centered * inverse, inverse


def sigmoid(values):
    return 1.0 / (1.0 + jnp.exp(-values))


def pair_forward_kernel(
    pair,
    mask,
    in_w_t,
    gate_w,
    out_w,
    bias_w_t,
    feats,
    atoms,
    pair_next,
    bias,
    left,
    right,
    product,
    every_feat,
    every_atom,
    x1,
    mid,
    mid_rows,
    x2,
    arrived,
    arrived_rows,
    panel,
    x3,
    back,
    back_rows,
    x4,
    packed,
    mine,
    send_sem,
    recv_sem,
):
    t, s = lax.axis_index("tile"), lax.axis_index("sample")
    m, c = t // 2, lax.rem(t, 2)
    barrier = pltpu.get_barrier_semaphore()
    tile_peers = [lax.rem(t + k, N_TILE) for k in range(1, N_TILE)]
    sample_peers = [lax.rem(s + k, N_SAMPLE) for k in range(1, N_SAMPLE)]
    for d in sample_peers:
        pl.semaphore_signal(barrier, inc=1, device_id=(t, d), device_id_type=MESH)
    for d in tile_peers:
        pl.semaphore_signal(barrier, inc=1, device_id=(d, s), device_id_type=MESH)

    normed_z = norm_rows(pair[...].astype(F32), 1)[0].astype(BF16)

    def project(block):
        return dot_t(in_w_t[pl.ds(block * 128, 128), :], normed_z)

    for side in range(2):
        value = (sigmoid(project(2 * side)) * project(2 * side + 1) * mask[...]).astype(BF16)
        for d in range(N_SAMPLE):
            x1[d, side] = value[d * 16 : d * 16 + 16]
    pl.semaphore_wait(barrier, N_SAMPLE + N_TILE - 2)
    for d in sample_peers:
        send(x1.at[d], mid.at[s], send_sem.at[0], recv_sem.at[0], t, d)
    for d in tile_peers:
        send(feats, every_feat.at[t], send_sem.at[1], recv_sem.at[1], d, s)
        send(atoms, every_atom.at[t], send_sem.at[2], recv_sem.at[2], d, s)
    every_feat[t] = feats[...]
    every_atom[t] = atoms[...]
    mid[s] = x1[s]
    tri_gate = sigmoid(dot(normed_z, gate_w[...]))
    wait_bytes(mid.at[pl.ds(0, N_SAMPLE - 1)], recv_sem.at[0])
    split_lanes(mid[...].reshape(256, 512).astype(F32), mid_rows)
    for d in range(N_TILE):
        for part in range(4):
            x2[d, :, pl.ds(part * 128, 128)] = mid_rows[part, pl.ds(d, 16, stride=16), :].astype(
                BF16
            )
    for d in tile_peers:
        send(x2.at[d], arrived.at[t], send_sem.at[3], recv_sem.at[3], d, s)
    arrived[t] = x2[t]
    wait_bytes(arrived.at[pl.ds(0, N_TILE - 1)], recv_sem.at[3])
    split_lanes(arrived[...].reshape(256, 512).astype(F32), arrived_rows)
    panel_of(arrived_rows, 0, 16, panel)
    left[...] = joined(panel).astype(BF16)
    panel_of(arrived_rows, 1, 16, panel)
    right[...] = joined(panel).astype(BF16)
    x3[...] = dot_t(left[...], right[...]).astype(BF16).reshape(N_TILE, 16, 256)
    for d in tile_peers:
        send(x3.at[d], back.at[t], send_sem.at[4], recv_sem.at[4], d, s)
    back[t] = x3[t]
    wait_bytes(back.at[pl.ds(0, N_TILE - 1)], recv_sem.at[4])
    split_lanes(back[...].reshape(256, 256).astype(F32), back_rows)

    def store(d, lanes, rows):
        x4[d, :, lanes] = rows.astype(BF16)

    blocks_of(back_rows, store)
    for d in sample_peers:
        send(x4.at[d], product.at[s], send_sem.at[5], recv_sem.at[5], t, d)
    product[s] = x4[s]
    wait_bytes(product.at[pl.ds(0, N_SAMPLE - 1)], recv_sem.at[5])
    normed_p = norm_rows(product[...].reshape(128, 512).astype(F32), 0)[0].astype(BF16)
    linear = t_dot(normed_p, out_w[...])
    following = pair[...].astype(F32) + tri_gate * linear
    pair_next[...] = following
    normed_n = norm_rows(following, 1)[0].astype(BF16)
    head_rows = dot_t(bias_w_t[...], normed_n)
    split_lanes(head_rows, packed)
    for part in range(4):
        rows = [packed[part, pl.ds(h, 4, stride=4), :] for h in range(4)]
        for i in range(4):
            mine[:, part * 4 + i] = place_lanes(rows, i)
    bias[m, c, s] = mine[...].astype(BF16)

    own = bias.at[m, c, s]
    for d in sample_peers:
        send(own, own, send_sem.at[6], recv_sem.at[6], t, d)
    wait_bytes(bias.at[m, c, pl.ds(0, N_SAMPLE - 1)], recv_sem.at[6])
    block = bias.at[m, c]
    other = m * 2 + 1 - c
    for k in range(1, N_CHIP):
        send(block, block, send_sem.at[7], recv_sem.at[7 + k], lax.rem(m + k, N_CHIP) * 2 + c, s)
    send(block, block, send_sem.at[8], recv_sem.at[7], other, s)
    for k in range(1, N_CHIP):
        came = bias.at[lax.rem(m + N_CHIP - k, N_CHIP), c]
        wait_bytes(came, recv_sem.at[7 + k])
        send(came, came, send_sem.at[8], recv_sem.at[7], other, s)
    wait_bytes(bias.at[:, 0], recv_sem.at[7])
    wait_bytes(every_feat.at[pl.ds(0, N_TILE - 1)], recv_sem.at[1])
    wait_bytes(every_atom.at[pl.ds(0, N_TILE - 1)], recv_sem.at[2])
    wait_bytes(mid.at[pl.ds(0, N_SAMPLE - 1)], send_sem.at[0])
    wait_bytes(every_feat.at[pl.ds(0, N_TILE - 1)], send_sem.at[1])
    wait_bytes(every_atom.at[pl.ds(0, N_TILE - 1)], send_sem.at[2])
    wait_bytes(arrived.at[pl.ds(0, N_TILE - 1)], send_sem.at[3])
    wait_bytes(back.at[pl.ds(0, N_TILE - 1)], send_sem.at[4])
    wait_bytes(product.at[pl.ds(0, N_SAMPLE - 1)], send_sem.at[5])
    wait_bytes(bias.at[m, c, pl.ds(0, N_SAMPLE - 1)], send_sem.at[6])
    wait_bytes(bias.at[pl.ds(0, N_CHIP - 1), 0], send_sem.at[7])
    wait_bytes(bias.at[:, 0], send_sem.at[8])


def pair_forward(pair, mask, in_w_t, gate_w, out_w, bias_w_t, feats, atoms, collective_id):
    vmem = pl.BlockSpec(memory_space=pltpu.VMEM)
    return pl.pallas_call(
        pair_forward_kernel,
        out_shape=[
            jax.ShapeDtypeStruct(pair.shape, F32),
            jax.ShapeDtypeStruct((N_CHIP, 2, N_SAMPLE, 4, 16, 128), BF16),
            jax.ShapeDtypeStruct((256, 256), BF16),
            jax.ShapeDtypeStruct((256, 256), BF16),
            jax.ShapeDtypeStruct((N_SAMPLE, 16, 512), BF16),
            jax.ShapeDtypeStruct((N_TILE,) + feats.shape, feats.dtype),
            jax.ShapeDtypeStruct((N_TILE,) + atoms.shape, atoms.dtype),
        ],
        in_specs=[vmem] * 8,
        out_specs=[vmem] * 7,
        scratch_shapes=[
            pltpu.VMEM((N_SAMPLE, 2, 16, 512), BF16),
            pltpu.VMEM((N_SAMPLE, 2, 16, 512), BF16),
            pltpu.VMEM((4, 256, 128), F32),
            pltpu.VMEM((N_TILE, 16, 512), BF16),
            pltpu.VMEM((N_TILE, 16, 512), BF16),
            pltpu.VMEM((4, 256, 128), F32),
            pltpu.VMEM((2, 256, 128), F32),
            pltpu.VMEM((N_TILE, 16, 256), BF16),
            pltpu.VMEM((N_TILE, 16, 256), BF16),
            pltpu.VMEM((2, 256, 128), F32),
            pltpu.VMEM((N_SAMPLE, 16, 512), BF16),
            pltpu.VMEM((4, 16, 128), F32),
            pltpu.VMEM((4, 16, 128), F32),
            pltpu.SemaphoreType.DMA((9,)),
            pltpu.SemaphoreType.DMA((15,)),
        ],
        compiler_params=pltpu.CompilerParams(
            collective_id=collective_id, has_side_effects=True, vmem_limit_bytes=40 << 20
        ),
    )(pair, mask, in_w_t, gate_w, out_w, bias_w_t, feats, atoms)


def scatter_sum_kernel(x, out, pair_sum, by_chip, by_sample, send_sem, recv_sem):
    t, s = lax.axis_index("tile"), lax.axis_index("sample")
    m, c = t // 2, lax.rem(t, 2)
    enter(t, s)
    for k in range(1, N_CHIP + 1):
        d = lax.rem(m + k, N_CHIP)
        send(x.at[d, 1 - c], pair_sum.at[d], send_sem.at[0], recv_sem.at[k], m * 2 + 1 - c, s)
    for k in range(1, N_CHIP + 1):
        d = lax.rem(m + k, N_CHIP)
        wait_bytes(pair_sum.at[d], recv_sem.at[k])
        pair_sum[d] = (pair_sum[d].astype(F32) + x[d, c].astype(F32)).astype(x.dtype)
        if k < N_CHIP:
            send(
                pair_sum.at[d],
                by_chip.at[k - 1],
                send_sem.at[1],
                recv_sem.at[N_CHIP + k],
                d * 2 + c,
                s,
            )
    total = pair_sum[m].astype(F32)
    for k in range(1, N_CHIP):
        wait_bytes(by_chip.at[k - 1], recv_sem.at[N_CHIP + k])
        total = total + by_chip[k - 1].astype(F32)
    pair_sum[m] = total.astype(x.dtype)
    for k in range(1, N_SAMPLE):
        d = lax.rem(s + k, N_SAMPLE)
        send(pair_sum.at[m, d], by_sample.at[k - 1], send_sem.at[2], recv_sem.at[0], t, d)
    wait_bytes(by_sample, recv_sem.at[0])
    out[...] = pair_sum[m, s].astype(F32) + jnp.sum(by_sample[...].astype(F32), axis=0)
    wait_bytes(pair_sum, send_sem.at[0])
    wait_bytes(by_chip, send_sem.at[1])
    wait_bytes(by_sample, send_sem.at[2])


def scatter_sum(x, collective_id):
    block = x.shape[3:]
    return pl.pallas_call(
        scatter_sum_kernel,
        out_shape=jax.ShapeDtypeStruct(block, F32),
        in_specs=[pl.BlockSpec(memory_space=pltpu.VMEM)],
        out_specs=pl.BlockSpec(memory_space=pltpu.VMEM),
        scratch_shapes=[
            pltpu.VMEM((N_CHIP, N_SAMPLE) + block, x.dtype),
            pltpu.VMEM((N_CHIP - 1, N_SAMPLE) + block, x.dtype),
            pltpu.VMEM((N_SAMPLE - 1,) + block, x.dtype),
            pltpu.SemaphoreType.DMA((3,)),
            pltpu.SemaphoreType.DMA((2 * N_CHIP,)),
        ],
        compiler_params=pltpu.CompilerParams(
            collective_id=collective_id, has_side_effects=True, vmem_limit_bytes=32 << 20
        ),
    )(x)


def attention_kernel(q, k, v, gate, up, bias, gated, d_every, d_bias, bias_rows, bias_total):
    tokens = bias_rows.shape[1]
    scale = 1.0 / math.sqrt(HEAD)
    group_of = lax.broadcasted_iota(jnp.int32, (tokens, 128), 1) // LANES

    for half in range(2):
        parts = [
            bias[:, :, half * 4 + i, 0].reshape(tokens, 128).astype(F32) for i in range(4)
        ]
        for h in range(GROUP):
            row = parts[0] if h == 0 else pltpu.roll(parts[0], (-h) % 4 * LANES, 1)
            for i in range(1, 4):
                shift = (i - h) % 4 * LANES
                moved = pltpu.roll(parts[i], shift, 1) if shift else parts[i]
                row = jnp.where(group_of == i, moved, row)
            bias_rows[h, :, pl.ds(half * 128, 128)] = row

    @pl.loop(0, GROUP)
    def _(h):
        rows = pl.ds(pl.multiple_of(h * HEAD, 16), HEAD)
        for sample in range(2):
            columns = pl.ds(sample * tokens, tokens)
            qh, kh, vh = q[rows, columns], k[rows, columns], v[rows, columns]
            scores = t_dot(qh, kh) * scale + bias_rows[h]
            weights = jnp.exp(scores - jnp.max(scores, axis=1, keepdims=True))
            probs = weights * (1.0 / jnp.sum(weights, axis=1, keepdims=True))
            probs_b = probs.astype(BF16)
            attended = dot_t(vh, probs_b)
            gate_h, up_h = gate[rows, columns], up[rows, columns]
            gated[rows, columns] = (gate_h * attended).astype(BF16)
            d_att = (up_h * gate_h).astype(BF16)
            d_every[1, rows, columns] = (up_h * attended * gate_h * (1.0 - gate_h)).astype(BF16)
            d_probs = t_dot(d_att, vh)
            inner = jnp.sum(probs * d_probs, axis=1, keepdims=True)
            d_scores = probs * (d_probs - inner)
            d_scores_b = d_scores.astype(BF16)
            d_every[0, rows, columns] = (dot_t(kh, d_scores_b) * scale).astype(BF16)
            d_every[2, rows, columns] = (dot(qh, d_scores_b) * scale).astype(BF16)
            d_every[3, rows, columns] = dot(d_att, probs_b).astype(BF16)
            if sample == 0:
                bias_total[h] = d_scores
            else:
                bias_total[h] = bias_total[h] + d_scores

    for half in range(2):
        parts = [bias_total[h, :, pl.ds(half * 128, 128)] for h in range(GROUP)]
        for i in range(4):
            row = parts[0] if i == 0 else pltpu.roll(parts[0], (-i) % 4 * LANES, 1)
            for h in range(1, GROUP):
                shift = (h - i) % 4 * LANES
                moved = pltpu.roll(parts[h], shift, 1) if shift else parts[h]
                row = jnp.where(group_of == h, moved, row)
            d_bias[:, :, half * 4 + i, 0] = row.astype(BF16).reshape(N_CHIP, 2, 16, 128)


def attention(q, k, v, gate, up, bias):
    width, columns = q.shape
    tokens = columns // 2
    block = GROUP * HEAD
    feature = pl.BlockSpec((block, columns), lambda i: (i, 0))
    of_bias = pl.BlockSpec((N_CHIP, 2, N_SAMPLE, 1, 16, 128), lambda i: (0, 0, 0, i, 0, 0))
    return pl.pallas_call(
        attention_kernel,
        grid=(width // block,),
        in_specs=[feature] * 5 + [of_bias],
        out_specs=[feature, pl.BlockSpec((4, block, columns), lambda i: (0, i, 0)), of_bias],
        out_shape=[
            jax.ShapeDtypeStruct((width, columns), BF16),
            jax.ShapeDtypeStruct((4, width, columns), BF16),
            jax.ShapeDtypeStruct(bias.shape, BF16),
        ],
        scratch_shapes=[
            pltpu.VMEM((GROUP, tokens, tokens), F32),
            pltpu.VMEM((GROUP, tokens, tokens), F32),
        ],
        compiler_params=pltpu.CompilerParams(vmem_limit_bytes=40 << 20),
    )(q, k, v, gate, up, bias)


QUARTER = 208
PADDED = 256
WIDTH = 640


def reduce_kernel(
    left_in,
    right_in,
    left_out,
    right_out,
    small,
    in_sum,
    out_sum,
    small_sum,
    full,
    other,
    mine,
    theirs,
    from_core,
    part1,
    sum1,
    part2,
    sum2,
    part3,
    sum3,
    send_sem,
    recv_sem,
):
    t, s = lax.axis_index("tile"), lax.axis_index("sample")
    core = lax.rem(t, 2)
    place = [lax.rem(s, 2) * 2 + t // 8, lax.rem(t // 2, 4), s // 2]

    def device(where, c):
        return (lax.rem(where[0], 2) * 8 + where[1] * 2 + c, where[2] * 2 + where[0] // 2)

    def peer(axis, k):
        where = list(place)
        where[axis] = lax.rem(place[axis] + k, 4)
        return where[axis], device(where, core)

    partner = device(place, 1 - core)
    barrier = pltpu.get_barrier_semaphore()
    others = [partner] + [peer(axis, k)[1] for axis in range(3) for k in range(1, 4)]
    for to in others:
        pl.semaphore_signal(barrier, inc=1, device_id=to, device_id_type=MESH)

    def form(g, c, target):
        wide = pl.ds(pl.multiple_of(g * 1024 + c * 512, 512), 512)
        narrow = pl.ds(pl.multiple_of(g * 256 + c * 128, 128), 128)
        chunk = pl.ds(pl.multiple_of(g * WIDTH, 128), WIDTH)

        @pl.loop(0, 4)
        def _(a):
            rows = pl.ds(pl.multiple_of(a * 192, 64), 192)
            target[g, a, pl.ds(0, 192), pl.ds(0, 512)] = dot_t(
                left_in[rows, :], right_in[wide, :]
            ).astype(BF16)
            target[g, a, pl.ds(0, 192), pl.ds(512, 128)] = jnp.dot(
                left_out[rows, :], right_out[:, narrow], preferred_element_type=F32
            ).astype(BF16)
            target[g, a, pl.ds(192, 16), :] = small[
                pl.ds(pl.multiple_of(c * 64 + a * 16, 16), 16), chunk
            ]

    def add(count, store, *terms):
        @pl.loop(0, count)
        def _(r):
            rows = pl.ds(pl.multiple_of(r * 16, 16), 16)
            total = terms[0](rows).astype(F32)
            for term in terms[1:]:
                total = total + term(rows).astype(F32)
            store(rows, total.astype(BF16))

    for g in range(3):
        form(g, 1 - core, theirs)
        if g == 0:
            pl.semaphore_wait(barrier, len(others))
        send(theirs.at[g], from_core.at[g], send_sem.at[0], recv_sem.at[g, 0], *partner)
    for g in range(3):
        form(g, core, mine)
        wait_bytes(from_core.at[g], recv_sem.at[g, 0])
        for a in range(4):

            def put(rows, total, g=g, a=a):
                mine[g, a, rows, :] = total

            add(
                QUARTER // 16,
                put,
                lambda rows, g=g, a=a: mine[g, a, rows, :],
                lambda rows, g=g, a=a: from_core[g, a, rows, :],
            )
        for k in range(1, 4):
            d, to = peer(g, k)
            send(mine.at[g, d], part1.at[g, k - 1], send_sem.at[1], recv_sem.at[g, 1], *to)
    for g in range(3):
        p1 = place[g]
        wait_bytes(part1.at[g], recv_sem.at[g, 1])

        def put(rows, total, g=g):
            sum1[g, rows, :] = total

        add(
            QUARTER // 16,
            put,
            lambda rows, g=g, p1=p1: mine[g, p1, rows, :],
            *[lambda rows, g=g, k=k: part1[g, k, rows, :] for k in range(3)],
        )
        sum1[g, pl.ds(QUARTER, PADDED - QUARTER), :] = jnp.zeros((PADDED - QUARTER, WIDTH), BF16)
        for k in range(1, 4):
            d, to = peer((g + 1) % 3, k)
            rows = pl.ds(pl.multiple_of(d * 64, 64), 64)
            send(sum1.at[g, rows], part2.at[g, k - 1], send_sem.at[2], recv_sem.at[g, 2], *to)
    for g in range(3):
        first = place[(g + 1) % 3] * 64
        wait_bytes(part2.at[g], recv_sem.at[g, 2])
        rows = pl.ds(pl.multiple_of(first, 64), 64)
        total = sum1[g, rows, :].astype(F32)
        for k in range(3):
            total = total + part2[g, k].astype(F32)
        sum2[g] = total.astype(BF16)
        for k in range(1, 4):
            d, to = peer((g + 2) % 3, k)
            rows = pl.ds(pl.multiple_of(d * 16, 16), 16)
            send(sum2.at[g, rows], part3.at[g, k - 1], send_sem.at[3], recv_sem.at[g, 3], *to)
    for g in range(3):
        p1, p2, p3 = place[g], place[(g + 1) % 3], place[(g + 2) % 3]
        wait_bytes(part3.at[g], recv_sem.at[g, 3])
        total = sum2[g, pl.ds(pl.multiple_of(p3 * 16, 16), 16), :].astype(F32)
        for k in range(3):
            total = total + part3[g, k].astype(F32)
        rows = pl.ds(pl.multiple_of(p2 * 64 + p3 * 16, 16), 16)
        full[g, p1, rows, :] = total.astype(BF16)
        block = full.at[g, p1, rows]
        for k in range(1, 4):
            _, to = peer((g + 2) % 3, k)
            send(block, block, send_sem.at[4], recv_sem.at[g, 4], *to)
    for g in range(3):
        p1, p2 = place[g], place[(g + 1) % 3]
        wait_bytes(full.at[g, p1, pl.ds(0, 48)], recv_sem.at[g, 4])
        block = full.at[g, p1, pl.ds(pl.multiple_of(p2 * 64, 64), 64)]
        for k in range(1, 4):
            _, to = peer((g + 1) % 3, k)
            send(block, block, send_sem.at[5], recv_sem.at[g, 5], *to)
    for g in range(3):
        p1 = place[g]
        wait_bytes(full.at[g, p1, pl.ds(0, 192)], recv_sem.at[g, 5])
        block = full.at[g, p1, pl.ds(0, QUARTER)]
        for k in range(1, 4):
            _, to = peer(g, k)
            send(block, block, send_sem.at[6], recv_sem.at[g, 6], *to)
        send(block, other.at[g, p1], send_sem.at[7], recv_sem.at[g, 7], *partner)

    def unpack(source, g, c):
        wide = pl.ds(pl.multiple_of(g * 1024 + c * 512, 512), 512)
        narrow = pl.ds(pl.multiple_of(g * 256 + c * 128, 128), 128)

        @pl.loop(0, 4)
        def _(a):
            @pl.loop(0, 12)
            def _(r):
                rows = pl.ds(pl.multiple_of(r * 16, 16), 16)
                place_rows = pl.ds(pl.multiple_of(a * 192 + r * 16, 16), 16)
                in_sum[place_rows, wide] = source[g, a, rows, pl.ds(0, 512)]
                out_sum[place_rows, narrow] = source[g, a, rows, pl.ds(512, 128)]

            small_sum[pl.ds(pl.multiple_of(c * 64 + a * 16, 16), 16), pl.ds(g * WIDTH, WIDTH)] = source[
                g, a, pl.ds(192, 16), :
            ]

    for g in range(3):
        wait_bytes(full.at[g, pl.ds(0, 3), pl.ds(0, QUARTER)], recv_sem.at[g, 6])
        for k in range(1, 4):
            p1 = lax.rem(place[g] + k, 4)
            block = full.at[g, p1, pl.ds(0, QUARTER)]
            send(block, other.at[g, p1], send_sem.at[7], recv_sem.at[g, 7], *partner)
        unpack(full, g, core)
    for g in range(3):
        wait_bytes(other.at[g], recv_sem.at[g, 7])
        unpack(other, g, 1 - core)
    wait_bytes(theirs, send_sem.at[0])
    wait_bytes(part1, send_sem.at[1])
    wait_bytes(part2, send_sem.at[2])
    wait_bytes(part3, send_sem.at[3])
    wait_bytes(part3, send_sem.at[4])
    wait_bytes(part2, send_sem.at[5])
    wait_bytes(part1, send_sem.at[6])
    wait_bytes(theirs, send_sem.at[7])


def reduce_all(left_in, right_in, left_out, right_out, small, collective_id):
    chunk = (3, 4, QUARTER, WIDTH)
    return pl.pallas_call(
        reduce_kernel,
        out_shape=(
            jax.ShapeDtypeStruct((768, 3072), BF16),
            jax.ShapeDtypeStruct((768, 768), BF16),
            jax.ShapeDtypeStruct((128, 3 * WIDTH), BF16),
        ),
        in_specs=[pl.BlockSpec(memory_space=pltpu.VMEM)] * 5,
        out_specs=[pl.BlockSpec(memory_space=pltpu.VMEM)] * 3,
        scratch_shapes=[
            pltpu.VMEM((3, 4, PADDED, WIDTH), BF16),
            pltpu.VMEM(chunk, BF16),
            pltpu.VMEM(chunk, BF16),
            pltpu.VMEM(chunk, BF16),
            pltpu.VMEM(chunk, BF16),
            pltpu.VMEM((3, 3, QUARTER, WIDTH), BF16),
            pltpu.VMEM((3, PADDED, WIDTH), BF16),
            pltpu.VMEM((3, 3, 64, WIDTH), BF16),
            pltpu.VMEM((3, 64, WIDTH), BF16),
            pltpu.VMEM((3, 3, 16, WIDTH), BF16),
            pltpu.VMEM((3, 16, WIDTH), BF16),
            pltpu.SemaphoreType.DMA((8,)),
            pltpu.SemaphoreType.DMA((3, 8)),
        ],
        compiler_params=pltpu.CompilerParams(
            collective_id=collective_id, has_side_effects=True, vmem_limit_bytes=48 << 20
        ),
    )(left_in, right_in, left_out, right_out, small)


def norm_parts(values, axis):
    centered = values - jnp.mean(values, axis=axis, keepdims=True)
    inverse = lax.rsqrt(jnp.mean(centered * centered, axis=axis, keepdims=True) + EPSILON)
    return (centered * inverse, inverse)


def norm_back(normed, inverse, incoming_gradient, axis):
    first_mean = jnp.mean(incoming_gradient, axis=axis, keepdims=True)
    second_mean = jnp.mean(incoming_gradient * normed, axis=axis, keepdims=True)
    return (incoming_gradient - first_mean - normed * second_mean) * inverse


def silu_slope(values):
    sigmoid_part = jax.nn.sigmoid(values)
    return sigmoid_part * (1.0 + values * (1.0 - sigmoid_part))


def shards(
    pair,
    pair_mask,
    tri_in_w,
    tri_gate_w,
    tri_out_w,
    bias_w,
    atom_feats,
    atom_to_token,
    atom_w,
    tokens,
    attention_input_weight,
    attention_output_weight,
    cot_pair,
    token_output_cotangent,
):
    hidden = tri_in_w.shape[1] // 4
    token_width = attention_input_weight.shape[0]
    head_count = bias_w.shape[1]
    total_tokens = tokens.shape[1]
    pair_f = pair.astype(jnp.float32)
    normed_z, inverse_z = norm_parts(pair_f, 2)
    normed_zb = normed_z.astype(jnp.bfloat16)
    projected = jnp.einsum("ijz,zc->cij", normed_zb, tri_in_w, preferred_element_type=jnp.float32)
    mask_rows = pair_mask.astype(jnp.float32)[None]
    gate_left = jax.nn.sigmoid(projected[0:hidden])
    gate_right = jax.nn.sigmoid(projected[2 * hidden : 3 * hidden])
    rows, columns = pair_mask.shape
    blocks = (N_TILE, N_SAMPLE)
    following, bias_all, left_panel, right_panel, product, every_feat, every_atom = pair_forward(
        pair.reshape(-1, hidden),
        pair_mask.astype(F32).reshape(1, -1),
        tri_in_w.T,
        tri_gate_w,
        tri_out_w,
        bias_w.T,
        atom_feats,
        atom_to_token[None],
        0,
    )
    every_feat = every_feat.reshape(-1, atom_feats.shape[1])
    every_atom = every_atom.reshape(-1)
    product = product.reshape(hidden, rows, columns).astype(F32)
    normed_p, inverse_p = norm_parts(product, 0)
    normed_pb = normed_p.astype(jnp.bfloat16)
    linear = jnp.einsum("cij,cz->ijz", normed_pb, tri_out_w, preferred_element_type=jnp.float32)
    tri_gate = jax.nn.sigmoid(
        jnp.einsum("ijz,zy->ijy", normed_zb, tri_gate_w, preferred_element_type=jnp.float32)
    )
    pair_next = following.reshape(pair.shape)
    normed_n, inverse_n = norm_parts(pair_next, 2)
    normed_nb = normed_n.astype(jnp.bfloat16)
    atom_pre = jnp.dot(every_feat, atom_w, preferred_element_type=jnp.float32)
    atom_act = jax.nn.silu(atom_pre).astype(BF16)
    token_ids = jnp.arange(total_tokens, dtype=jnp.int32)
    one_hot = (token_ids[:, None] == every_atom[None, :]).astype(BF16)
    token_sums = jnp.dot(one_hot, atom_act, preferred_element_type=F32)
    token_counts = jnp.sum(one_hot.astype(F32), axis=1)
    token_cond = token_sums / token_counts[:, None]
    token_state_rows = tokens.astype(jnp.float32) + token_cond[None]
    normed_h, inverse_h = norm_parts(token_state_rows, 2)
    normalized_hidden_bfloat = normed_h.astype(jnp.bfloat16)
    hidden_t = normalized_hidden_bfloat.reshape(-1, token_width).T
    cot_rows = token_output_cotangent.reshape(-1, token_width)

    def project(block):
        weight = attention_input_weight[:, block * token_width : (block + 1) * token_width]
        return t_dot(weight, hidden_t)

    gated_t, d_every_t, bias_blocks = attention(
        project(0).astype(BF16),
        project(2).astype(BF16),
        project(3).astype(BF16),
        jax.nn.sigmoid(project(1)),
        dot_t(attention_output_weight, cot_rows),
        bias_all,
    )
    d_every_t = d_every_t.reshape(4 * token_width, -1)
    token_output_rows = token_state_rows + t_dot(gated_t, attention_output_weight).reshape(
        token_state_rows.shape
    )
    bias_grad = (
        scatter_sum(bias_blocks, 3)
        .reshape(head_count // GROUP, rows, GROUP, columns)
        .transpose(0, 2, 1, 3)
        .reshape(head_count, rows, columns)
    )
    normalized_hidden_gradient = lax.dot_general(
        d_every_t, attention_input_weight, (((0,), (1,)), ((), ())), preferred_element_type=F32
    ).reshape(token_state_rows.shape)
    grad_tokens = token_output_cotangent.astype(jnp.float32) + norm_back(
        normed_h, inverse_h, normalized_hidden_gradient, 2
    )
    cond_grad = (jnp.sum(grad_tokens, axis=0) / token_counts[:, None]).astype(BF16)
    d_act = lax.dot_general(
        one_hot, cond_grad, (((0,), (0,)), ((), ())), preferred_element_type=F32
    ) * silu_slope(atom_pre)
    grad_atom_w = lax.dot_general(
        every_feat, d_act.astype(BF16), (((0,), (0,)), ((), ())), preferred_element_type=F32
    )
    d_normed_n = jnp.einsum("hij,zh->ijz", bias_grad, bias_w.astype(jnp.float32), precision=HIGHEST)
    grad_bias_w = jnp.einsum(
        "ijz,hij->zh", normed_nb.astype(jnp.float32), bias_grad, precision=HIGHEST
    )
    d_next = cot_pair.astype(jnp.float32) + norm_back(normed_n, inverse_n, d_normed_n, 2)
    d_linear = (d_next * tri_gate).astype(jnp.bfloat16)
    d_gate_pre = (d_next * linear * tri_gate * (1.0 - tri_gate)).astype(jnp.bfloat16)
    grad_tri_out_w = jnp.einsum(
        "cij,ijz->cz", normed_pb, d_linear, preferred_element_type=jnp.float32
    )
    d_normed_p = jnp.einsum("ijz,cz->cij", d_linear, tri_out_w, preferred_element_type=jnp.float32)
    d_product = norm_back(normed_p, inverse_p, d_normed_p, 0).astype(jnp.bfloat16)

    def by_owner(values):
        return values.reshape((N_SAMPLE, N_TILE) + values.shape[1:]).swapaxes(0, 1)

    d_product_panel = (
        exchange(by_owner(d_product.astype(F32)).reshape(blocks + (4, 128)), 4)
        .reshape(blocks + (rows, columns))
        .astype(BF16)
        .transpose(0, 2, 1, 3)
        .reshape(N_TILE * rows, N_SAMPLE * columns)
    )
    d_left_panel = jnp.dot(d_product_panel, right_panel, preferred_element_type=F32)
    d_right_panel = jnp.dot(d_product_panel.T, left_panel, preferred_element_type=F32)
    d_halves = (
        jnp.stack([d_left_panel, d_right_panel])
        .reshape(2, N_TILE, rows, N_SAMPLE, columns)
        .transpose(1, 3, 0, 2, 4)
        .reshape(blocks + (8, 128))
    )
    d_halves = (
        exchange(d_halves, 5)
        .reshape(blocks + (2, rows, columns))
        .transpose(1, 0, 2, 3, 4)
        .reshape(hidden, 2, rows, columns)
    )
    d_left, d_right = d_halves[:, 0], d_halves[:, 1]
    d_proj = jnp.concatenate(
        [
            d_left * projected[hidden : 2 * hidden] * mask_rows * gate_left * (1.0 - gate_left),
            d_left * gate_left * mask_rows,
            d_right * projected[3 * hidden :] * mask_rows * gate_right * (1.0 - gate_right),
            d_right * gate_right * mask_rows,
        ],
        axis=0,
    ).astype(jnp.bfloat16)
    grad_tri_in_w = jnp.einsum("ijz,cij->zc", normed_zb, d_proj, preferred_element_type=jnp.float32)
    grad_tri_gate_w = jnp.einsum(
        "ijz,ijy->zy", normed_zb, d_gate_pre, preferred_element_type=jnp.float32
    )
    d_normed_z = jnp.einsum(
        "cij,zc->ijz", d_proj, tri_in_w, preferred_element_type=jnp.float32
    ) + jnp.einsum("ijy,zy->ijz", d_gate_pre, tri_gate_w, preferred_element_type=jnp.float32)
    grad_pair = d_next + norm_back(normed_z, inverse_z, d_normed_z, 2)
    small = jnp.concatenate(
        [
            grad_tri_in_w,
            grad_tri_gate_w,
            grad_tri_out_w,
            grad_bias_w,
            jnp.zeros((hidden, 128 - head_count), F32),
            grad_atom_w,
            jnp.zeros((hidden, 3 * WIDTH - 4 * hidden - 3 * 128 - token_width), F32),
        ],
        axis=1,
    ).astype(BF16)
    in_sum, out_sum, small_sum = reduce_all(hidden_t, d_every_t, gated_t, cot_rows, small, 6)
    small_sum = small_sum.astype(F32)
    at = 4 * hidden
    summed = (
        small_sum[:, :at],
        small_sum[:, at : at + 128],
        small_sum[:, at + 128 : at + 256],
        small_sum[:, at + 256 : at + 256 + head_count],
        small_sum[:, at + 384 : at + 384 + token_width],
        in_sum.astype(F32),
        out_sum.astype(F32),
    )
    return (pair_next, token_output_rows, grad_pair, grad_tokens) + summed


def solution(mesh):
    in_specs = (
        P("tile", "sample", None),
        P("tile", "sample"),
        P(),
        P(),
        P(),
        P(),
        P("tile", None),
        P("tile"),
        P(),
        P(("tile", "sample"), None, None),
        P(),
        P(),
        P("tile", "sample", None),
        P(("tile", "sample"), None, None),
    )
    out_specs = (
        P("tile", "sample", None),
        P(("tile", "sample"), None, None),
        P("tile", "sample", None),
        P(("tile", "sample"), None, None),
        P(),
        P(),
        P(),
        P(),
        P(),
        P(),
        P(),
    )
    return jax.shard_map(shards, mesh=mesh, in_specs=in_specs, out_specs=out_specs, check_vma=False)
```

profile of v0, /device:TPU:1, one launch (start us, length us, event | category | flops | bytes accessed | tf_op | source)
XLA Modules:
  0.0 296.6 jit_solution(8390636091845696102)
XLA Ops:
  7.1 52.2 %shard_map.221 = (f32[512,128]{1,0:T(8,128)S(1)}, bf16[8,2,8,4,16,128]{5,4,3,2,1,0:T(8,128)(2,1)S(1)}, bf16[256,256]{1,0:T(8,128)(2,1)S(1)}, bf16[256,256]{1,0:T...) custom-call(bf16[512,128]{1,0:T(8,128)(2,1)S(1)} %bitcast.160, ...), custom_call_target="tpu_custom_call" | custom-call | tf_op jit(solution)/shard_map/pallas_call | solution.py:283
  59.6 2.0 fusion.94
  61.7 2.2 fusion.31
  70.0 23.9 %shard_map.222 = (bf16[768,512]{1,0:T(8,128)(2,1)S(1)}, bf16[4,768,512]{2,1,0:T(8,128)(2,1)S(1)}, bf16[8,2,8,4,16,128]{5,4,3,2,1,0:T(8,128)(2,1)S(1)}) custom-call(bf16[768,512]{1,0:T(8,128)(2,1)S(1)} %fusion.10.q, bf16[768,512]{1,0:T(8,128)(2,1)S(1)} %fusion.11.k, bf16[768,512]{1,0:T(8,128)(2,1)S(1)} %fusion.12.v, f32[768,512]{1,0:T(8,128)S(1)} %divide_bitcast_fusion.gate, ...), custom_call_target="tpu_custom_call" | custom-call | tf_op jit(solution)/shard_map/pallas_call | solution.py:435
  93.9 1.6 copy-done.1
  95.6 23.8 %shard_map.223 = f32[4,16,128]{2,1,0:T(8,128)S(1)} custom-call(bf16[8,2,8,4,16,128]{5,4,3,2,1,0:T(8,128)(2,1)S(1)} %get-tuple-element.29.x), custom_call_target="tpu_custom_call" | custom-call | tf_op jit(solution)/shard_map/pallas_call | solution.py:356
  123.8 1.6 copy.124
  127.6 1.5 reshape.258
  129.2 16.8 %shard_map.224 = f32[16,8,4,128]{3,2,1,0:T(4,128)S(1)} custom-call(f32[16,8,4,128]{3,2,1,0:T(4,128)S(1)} %copy.150.x), custom_call_target="tpu_custom_call" | custom-call | tf_op jit(solution)/shard_map/pallas_call | solution.py:66
  152.1 1.6 copy.131
  153.7 2.0 reshape.235.x
  155.7 19.6 %shard_map.225 = f32[16,8,8,128]{3,2,1,0:T(8,128)S(1)} custom-call(f32[16,8,8,128]{3,2,1,0:T(8,128)S(1)} %reshape.235.x), custom_call_target="tpu_custom_call" | custom-call | tf_op jit(solution)/shard_map/pallas_call | solution.py:66
  175.3 1.8 reshape.236
  177.1 1.8 copy.132
  180.0 2.3 copy.154
  188.3 4.7 %copy.151 = bf16[512,3072]{1,0:T(8,128)(2,1)} copy(bf16[512,3072]{0,1:T(8,128)(2,1)} %bitcast.155) | data formatting | bytes 6291456 | tf_op jit(solution)/shard_map/dot_general | solution.py:779
  193.0 6.3 %fusion.86 = (f32[2,256]{1,0:T(2,128)S(1)}, f32[2,256]{1,0:T(2,128)S(1)}, f32[2,256,768]{2,1,0:T(8,128)S(1)}) fusion(f32[2,256]{1,0:T(2,128)S(1)} %add_rsqrt_fusion.3, f32[2,256]{1,0:T(2,128)S(1)} %broadcast_multiply_fusion.11, f32[256,768]{1,0:T(8,128)} %copy-done.23, bf16[2,256,768]{2,1,0:T(8,128)(2,1)S(1)} %copy-done.21, ...), kind=kOutput, calls=%fused_computation.142 | convolution fusion | flops 2418670592 | bytes 11018240 | tf_op jit(solution)/shard_map/dot_general | solution.py:779
  200.7 3.3 %fusion.90 = (f32[256,768]{1,0:T(8,128)}, f32[2,256,768]{2,1,0:T(8,128)}, f32[2,256,768]{2,1,0:T(8,128)}) fusion(f32[2,256]{1,0:T(2,128)S(1)} %get-tuple-element.124, f32[2,256]{1,0:T(2,128)S(1)} %add_rsqrt_fusion.3, f32[2,256]{1,0:T(2,128)S(1)} %broadcast_multiply_fusion.11, f32[256,768]{1,0:T(8,128)S(1)} %copy-done.24, ...), kind=kLoop, calls=%fused_computation.146 | loop fusion | flops 4521984 | bytes 9445376 | tf_op jit(solution)/shard_map/reduce_sum | solution.py:785
  204.0 6.7 %fusion.17 = bf16[128,768]{1,0:T(8,128)(2,1)} fusion(bf16[2048,128]{1,0:T(8,128)(2,1)S(1)} %bitcast.165, f32[2048,768]{1,0:T(8,128)} %copy-done.19, s32[2048]{0:T(1024)S(1)} %bitcast.172, f32[256,768]{1,0:T(8,128)} %get-tuple-element.100, f32[256]{0:T(256)S(1)} %convert_reduce_fusion), kind=kOutput, calls=%fused_computation.34 | convolution fusion | flops 1223131136 | bytes 7808000 | tf_op jit(solution)/shard_map/dot_general | solution.py:789
  211.7 1.9 concatenate.14.small
  213.5 1.4 copy.149
  217.1 65.2 %shard_map.226 = (bf16[768,3072]{1,0:T(8,128)(2,1)}, bf16[768,768]{1,0:T(8,128)(2,1)S(1)}, bf16[128,1920]{1,0:T(8,128)(2,1)S(1)}) custom-call(bf16[768,512]{1,0:T(8,128)(2,1)S(1)} %bitcast.161, bf16[3072,512]{1,0:T(8,128)(2,1)} %bitcast.156, bf16[768,512]{1,0:T(8,128)(2,1)S(1)} %copy-done.10, bf16[512,768]{1,0:T(8,128)(2,1)S(1)} %bitcast.163, ...), custom_call_target="tpu_custom_call" | custom-call | tf_op jit(solution)/shard_map/pallas_call | solution.py:645
  282.3 7.4 %convert_element_type.130 = f32[768,3072]{1,0:T(8,128)} convert(bf16[768,3072]{1,0:T(8,128)(2,1)} %get-tuple-element.35) | non-fusion elementwise | flops 2359296 | bytes 14155776 | tf_op jit(solution)/shard_map/convert_element_type | solution.py:868
  289.6 1.6 convert_element_type.131
  (179 shorter events, 42.0 us)
Async XLA Ops:
  0.6 68.3 %copy-start = (bf16[768,768]{1,0:T(8,128)(2,1)S(1)}, bf16[768,768]{1,0:T(8,128)(2,1)}, u32[]{:S(2)}) copy-start(bf16[768,768]{1,0:T(8,128)(2,1)} %param.25) | copy-start | bytes 3538948
  59.6 5.7 %slice-start = ((s8[4718592]{0:T(1024)(128)(4,1)}), s8[4194304]{0:T(1024)(128)(4,1)S(1)}, s32[]{:S(2)}) async-start(s8[4718592]{0:T(1024)(128)(4,1)} %bitcast.191), calls=%async_computation | async-start | bytes 8388608
  61.7 2.7 copy-start.19
  61.7 2.7 copy-start.20
  61.7 3.6 %slice-start.1 = ((s8[4718592]{0:T(1024)(128)(4,1)}), s8[524288]{0:T(1024)(128)(4,1)S(1)}, s32[]{:S(2)}) async-start(s8[4718592]{0:T(1024)(128)(4,1)} %bitcast.191), calls=%async_computation.1 | async-start | bytes 1048576
  65.3 2.8 copy-start.28
  95.6 23.9 %copy-start.8 = (bf16[768,512]{1,0:T(8,128)(2,1)}, bf16[768,512]{1,0:T(8,128)(2,1)S(1)}, u32[]{:S(2)}) copy-start(bf16[768,512]{1,0:T(8,128)(2,1)S(1)} %get-tuple-element.28.left_out) | copy-start | bytes 2359300
  95.6 24.5 %copy-start.17 = (bf16[128,16]{0,1:T(8,128)(2,1)S(1)}, bf16[128,16]{0,1:T(8,128)(2,1)}, u32[]{:S(2)}) copy-start(bf16[128,16]{0,1:T(8,128)(2,1)} %param.19) | copy-start | bytes 12292
  95.6 25.1 %copy-start.3 = (bf16[16,32,128]{2,1,0:T(8,128)(2,1)S(1)}, bf16[16,32,128]{2,1,0:T(8,128)(2,1)}, u32[]{:S(2)}) copy-start(bf16[16,32,128]{2,1,0:T(8,128)(2,1)} %param.14) | copy-start | bytes 393220
  119.5 2.8 copy-start.29
  122.3 3.5 %copy-start.45 = (bf16[16,32,128]{2,1,0:T(8,128)(2,1)}, bf16[16,32,128]{2,1,0:T(8,128)(2,1)S(1)}, u32[]{:S(2)}) copy-start(bf16[16,32,128]{2,1,0:T(8,128)(2,1)S(1)} %get-tuple-element.102) | copy-start | bytes 393220
  122.3 3.1 %copy-start.12 = (bf16[128,128]{1,0:T(8,128)(2,1)S(1)}, bf16[128,128]{1,0:T(8,128)(2,1)}, u32[]{:S(2)}) copy-start(bf16[128,128]{1,0:T(8,128)(2,1)} %out_w.1) | copy-start | bytes 98308
  125.5 3.7 %copy-start.25 = (f32[128,16,32]{0,2,1:T(8,128)}, f32[128,16,32]{0,2,1:T(8,128)S(1)}, u32[]{:S(2)}) copy-start(f32[128,16,32]{0,2,1:T(8,128)S(1)} %copy.124) | copy-start | bytes 786436
  188.3 4.7 %copy-start.21 = (bf16[2,256,768]{2,1,0:T(8,128)(2,1)S(1)}, bf16[2,256,768]{2,1,0:T(8,128)(2,1)}, u32[]{:S(2)}) copy-start(bf16[2,256,768]{2,1,0:T(8,128)(2,1)} %param.23) | copy-start | bytes 2359300
  193.0 6.3 %copy-start.9 = (bf16[768,512]{1,0:T(8,128)(2,1)S(1)}, bf16[768,512]{1,0:T(8,128)(2,1)}, u32[]{:S(2)}) copy-start(bf16[768,512]{1,0:T(8,128)(2,1)} %copy-done.8) | copy-start | bytes 2359300
  200.7 3.3 %copy-start.7 = (bf16[16,128,128]{2,1,0:T(8,128)(2,1)S(1)}, bf16[16,128,128]{2,1,0:T(8,128)(2,1)}, u32[]{:S(2)}) copy-start(bf16[16,128,128]{2,1,0:T(8,128)(2,1)} %copy-done.6) | copy-start | bytes 1572868
  204.0 6.7 %copy-start.46 = (bf16[16,32,128]{2,1,0:T(8,128)(2,1)S(1)}, bf16[16,32,128]{2,1,0:T(8,128)(2,1)}, u32[]{:S(2)}) copy-start(bf16[16,32,128]{2,1,0:T(8,128)(2,1)} %copy-done.45) | copy-start | bytes 393220
  204.0 7.3 %copy-start.30 = (f32[4,64,32]{2,1,0:T(8,128)S(1)}, f32[4,64,32]{2,1,0:T(8,128)}, u32[]{:S(2)}) copy-start(f32[4,64,32]{2,1,0:T(8,128)} %copy-done.29) | copy-start | bytes 98308
  291.2 2.9 copy-start.33
  291.2 2.9 copy-start.38
  291.2 2.9 copy-start.40
  291.2 2.9 copy-start.42
  291.2 2.9 copy-start.44
  292.0 2.4 copy-start.35
  (26 other events, 35.0 us)
where the time goes:
time: 298 us; the launch traced here: 297 us
  Pallas kernels  201 us (67%)
  local copies, waits for them, and re-layouts  44.9 us (15%)
  matrix products  30.5 us (10%)
  other arithmetic  18.3 us (6%)
    pallas_call x1, Pallas kernels, reduce_all(): pl.pallas_call(reduce_kernel, out_shape=(jax.ShapeDtypeStruct((768, 3072)...  65.2 us
    pallas_call x1, Pallas kernels, pair_forward(): pl.pallas_call(pair_forward_kernel, out_shape=[jax.ShapeDtypeStruct(pair....  52.2 us
    pallas_call x2, Pallas kernels, exchange(): pl.pallas_call(exchange_kernel, out_shape=jax.ShapeDtypeStruct(x.shape, x...  36.4 us
    pallas_call x1, Pallas kernels, attention(): pl.pallas_call(attention_kernel, grid=(width // block,), in_specs=[featur...  23.9 us
    pallas_call x1, Pallas kernels, scatter_sum(): pl.pallas_call(scatter_sum_kernel, out_shape=jax.ShapeDtypeStruct(block,...  23.8 us
    unnamed x105, local copies, waits for them, and re-layouts  16.8 us
    convert_element_type x1, other arithmetic, shards(): in_sum.astype(F32)  7.37 us
    dot_general x1, matrix products, shards(): lax.dot_general(every_feat, d_act.astype(BF16), (((0,), (0,)), ((), ())),...  6.65 us

commit v1 on v0

v1 whole, which is shorter than its diff:
```python
import functools
import math

import jax
import jax.numpy as jnp
from jax import lax
from jax.experimental import pallas as pl
from jax.experimental.pallas import tpu as pltpu
from jax.sharding import PartitionSpec as P

EPSILON = 1e-05
N_TILE = 16
N_SAMPLE = 8
N_CHIP = 8
MESH = pl.DeviceIdType.MESH
BF16 = jnp.bfloat16
F32 = jnp.float32
HIGHEST = lax.Precision.HIGHEST


def wait_bytes(ref, sem):
    pltpu.make_async_copy(ref, ref, sem).wait()


def send(src, dst, send_sem, recv_sem, t, s):
    pltpu.make_async_remote_copy(
        src, dst, send_sem, recv_sem, device_id=(t, s), device_id_type=MESH
    ).start()


def dot(a, b):
    return jnp.dot(a, b, preferred_element_type=F32)


def dot_t(a, b):
    return lax.dot_general(a, b, (((1,), (1,)), ((), ())), preferred_element_type=F32)


def t_dot(a, b):
    return lax.dot_general(a, b, (((0,), (0,)), ((), ())), preferred_element_type=F32)


HEAD = 48
GROUP = 4
LANES = 32


def place_lanes(parts, first):
    group_of = lax.broadcasted_iota(jnp.int32, parts[0].shape, 1) // LANES
    result = None
    for i in range(4):
        shift = (i - first) % 4 * LANES
        moved = pltpu.roll(parts[i], shift, 1) if shift else parts[i]
        result = moved if result is None else jnp.where(group_of == i, moved, result)
    return result


def panel_of(arrived, first, step, panel):
    for part in range(4):
        rows = [
            arrived[part, pl.ds(first + s * (step // 8), 16, stride=step), :] for s in range(8)
        ]
        for i in range(4):
            for half in range(2):
                panel[half, pl.ds(part * 4 + i, 16, stride=16), :] = place_lanes(
                    rows[half * 4 : half * 4 + 4], i
                )


def blocks_of(panel, store):
    for half in range(2):
        for part in range(4):
            rows = [panel[half, pl.ds(part * 4 + i, 16, stride=16), :] for i in range(4)]
            for q in range(4):
                store(half * 4 + q, pl.ds(part * 128, 128), place_lanes(rows, q))


def split_lanes(values, ref):
    for part in range(ref.shape[0]):
        ref[part] = values[:, part * 128 : part * 128 + 128]


def joined(ref):
    return jnp.concatenate([ref[0], ref[1]], axis=1)


def norm_rows(values, axis):
    centered = values - jnp.mean(values, axis=axis, keepdims=True)
    inverse = lax.rsqrt(jnp.mean(centered * centered, axis=axis, keepdims=True) + EPSILON)
    return centered * inverse, inverse


def sigmoid(values):
    return 1.0 / (1.0 + jnp.exp(-values))


def pair_forward_kernel(
    pair,
    mask,
    in_w_t,
    gate_w,
    out_w,
    bias_w_t,
    feats,
    atoms,
    pair_next,
    bias,
    left,
    right,
    product,
    every_feat,
    every_atom,
    x1,
    mid,
    mid_rows,
    x2,
    arrived,
    arrived_rows,
    panel,
    x3,
    back,
    back_rows,
    x4,
    packed,
    mine,
    send_sem,
    recv_sem,
):
    t, s = lax.axis_index("tile"), lax.axis_index("sample")
    m, c = t // 2, lax.rem(t, 2)
    barrier = pltpu.get_barrier_semaphore()
    tile_peers = [lax.rem(t + k, N_TILE) for k in range(1, N_TILE)]
    sample_peers = [lax.rem(s + k, N_SAMPLE) for k in range(1, N_SAMPLE)]
    for d in sample_peers:
        pl.semaphore_signal(barrier, inc=1, device_id=(t, d), device_id_type=MESH)
    for d in tile_peers:
        pl.semaphore_signal(barrier, inc=1, device_id=(d, s), device_id_type=MESH)

    normed_z = norm_rows(pair[...].astype(F32), 1)[0].astype(BF16)

    def project(block):
        return dot_t(in_w_t[pl.ds(block * 128, 128), :], normed_z)

    for side in range(2):
        value = (sigmoid(project(2 * side)) * project(2 * side + 1) * mask[...]).astype(BF16)
        for d in range(N_SAMPLE):
            x1[d, side] = value[d * 16 : d * 16 + 16]
    pl.semaphore_wait(barrier, N_SAMPLE + N_TILE - 2)
    for d in sample_peers:
        send(x1.at[d], mid.at[s], send_sem.at[0], recv_sem.at[0], t, d)
    for d in tile_peers:
        send(feats, every_feat.at[t], send_sem.at[1], recv_sem.at[1], d, s)
        send(atoms, every_atom.at[t], send_sem.at[2], recv_sem.at[2], d, s)
    every_feat[t] = feats[...]
    every_atom[t] = atoms[...]
    mid[s] = x1[s]
    tri_gate = sigmoid(dot(normed_z, gate_w[...]))
    wait_bytes(mid.at[pl.ds(0, N_SAMPLE - 1)], recv_sem.at[0])
    split_lanes(mid[...].reshape(256, 512).astype(F32), mid_rows)
    for d in range(N_TILE):
        for part in range(4):
            x2[d, :, pl.ds(part * 128, 128)] = mid_rows[part, pl.ds(d, 16, stride=16), :].astype(
                BF16
            )
    for d in tile_peers:
        send(x2.at[d], arrived.at[t], send_sem.at[3], recv_sem.at[3], d, s)
    arrived[t] = x2[t]
    wait_bytes(arrived.at[pl.ds(0, N_TILE - 1)], recv_sem.at[3])
    split_lanes(arrived[...].reshape(256, 512).astype(F32), arrived_rows)
    panel_of(arrived_rows, 0, 16, panel)
    left[...] = joined(panel).astype(BF16)
    panel_of(arrived_rows, 1, 16, panel)
    right[...] = joined(panel).astype(BF16)
    x3[...] = dot_t(left[...], right[...]).astype(BF16).reshape(N_TILE, 16, 256)
    for d in tile_peers:
        send(x3.at[d], back.at[t], send_sem.at[4], recv_sem.at[4], d, s)
    back[t] = x3[t]
    wait_bytes(back.at[pl.ds(0, N_TILE - 1)], recv_sem.at[4])
    split_lanes(back[...].reshape(256, 256).astype(F32), back_rows)

    def store(d, lanes, rows):
        x4[d, :, lanes] = rows.astype(BF16)

    blocks_of(back_rows, store)
    for d in sample_peers:
        send(x4.at[d], product.at[s], send_sem.at[5], recv_sem.at[5], t, d)
    product[s] = x4[s]
    wait_bytes(product.at[pl.ds(0, N_SAMPLE - 1)], recv_sem.at[5])
    normed_p = norm_rows(product[...].reshape(128, 512).astype(F32), 0)[0].astype(BF16)
    linear = t_dot(normed_p, out_w[...])
    following = pair[...].astype(F32) + tri_gate * linear
    pair_next[...] = following
    normed_n = norm_rows(following, 1)[0].astype(BF16)
    head_rows = dot_t(bias_w_t[...], normed_n)
    split_lanes(head_rows, packed)
    for part in range(4):
        rows = [packed[part, pl.ds(h, 4, stride=4), :] for h in range(4)]
        for i in range(4):
            mine[:, part * 4 + i] = place_lanes(rows, i)
    bias[m, c, s] = mine[...].astype(BF16)

    own = bias.at[m, c, s]
    for d in sample_peers:
        send(own, own, send_sem.at[6], recv_sem.at[6], t, d)
    wait_bytes(bias.at[m, c, pl.ds(0, N_SAMPLE - 1)], recv_sem.at[6])
    block = bias.at[m, c]
    other = m * 2 + 1 - c
    for k in range(1, N_CHIP):
        send(block, block, send_sem.at[7], recv_sem.at[7 + k], lax.rem(m + k, N_CHIP) * 2 + c, s)
    send(block, block, send_sem.at[8], recv_sem.at[7], other, s)
    for k in range(1, N_CHIP):
        came = bias.at[lax.rem(m + N_CHIP - k, N_CHIP), c]
        wait_bytes(came, recv_sem.at[7 + k])
        send(came, came, send_sem.at[8], recv_sem.at[7], other, s)
    wait_bytes(bias.at[:, 0], recv_sem.at[7])
    wait_bytes(every_feat.at[pl.ds(0, N_TILE - 1)], recv_sem.at[1])
    wait_bytes(every_atom.at[pl.ds(0, N_TILE - 1)], recv_sem.at[2])
    wait_bytes(mid.at[pl.ds(0, N_SAMPLE - 1)], send_sem.at[0])
    wait_bytes(every_feat.at[pl.ds(0, N_TILE - 1)], send_sem.at[1])
    wait_bytes(every_atom.at[pl.ds(0, N_TILE - 1)], send_sem.at[2])
    wait_bytes(arrived.at[pl.ds(0, N_TILE - 1)], send_sem.at[3])
    wait_bytes(back.at[pl.ds(0, N_TILE - 1)], send_sem.at[4])
    wait_bytes(product.at[pl.ds(0, N_SAMPLE - 1)], send_sem.at[5])
    wait_bytes(bias.at[m, c, pl.ds(0, N_SAMPLE - 1)], send_sem.at[6])
    wait_bytes(bias.at[pl.ds(0, N_CHIP - 1), 0], send_sem.at[7])
    wait_bytes(bias.at[:, 0], send_sem.at[8])


def pair_forward(pair, mask, in_w_t, gate_w, out_w, bias_w_t, feats, atoms, collective_id):
    vmem = pl.BlockSpec(memory_space=pltpu.VMEM)
    return pl.pallas_call(
        pair_forward_kernel,
        out_shape=[
            jax.ShapeDtypeStruct(pair.shape, F32),
            jax.ShapeDtypeStruct((N_CHIP, 2, N_SAMPLE, 4, 16, 128), BF16),
            jax.ShapeDtypeStruct((256, 256), BF16),
            jax.ShapeDtypeStruct((256, 256), BF16),
            jax.ShapeDtypeStruct((N_SAMPLE, 16, 512), BF16),
            jax.ShapeDtypeStruct((N_TILE,) + feats.shape, feats.dtype),
            jax.ShapeDtypeStruct((N_TILE,) + atoms.shape, atoms.dtype),
        ],
        in_specs=[vmem] * 8,
        out_specs=[vmem] * 7,
        scratch_shapes=[
            pltpu.VMEM((N_SAMPLE, 2, 16, 512), BF16),
            pltpu.VMEM((N_SAMPLE, 2, 16, 512), BF16),
            pltpu.VMEM((4, 256, 128), F32),
            pltpu.VMEM((N_TILE, 16, 512), BF16),
            pltpu.VMEM((N_TILE, 16, 512), BF16),
            pltpu.VMEM((4, 256, 128), F32),
            pltpu.VMEM((2, 256, 128), F32),
            pltpu.VMEM((N_TILE, 16, 256), BF16),
            pltpu.VMEM((N_TILE, 16, 256), BF16),
            pltpu.VMEM((2, 256, 128), F32),
            pltpu.VMEM((N_SAMPLE, 16, 512), BF16),
            pltpu.VMEM((4, 16, 128), F32),
            pltpu.VMEM((4, 16, 128), F32),
            pltpu.SemaphoreType.DMA((9,)),
            pltpu.SemaphoreType.DMA((15,)),
        ],
        compiler_params=pltpu.CompilerParams(
            collective_id=collective_id, has_side_effects=True, vmem_limit_bytes=40 << 20
        ),
    )(pair, mask, in_w_t, gate_w, out_w, bias_w_t, feats, atoms)


def attention_kernel(q, k, v, gate, up, bias, gated, d_every, d_bias, bias_rows, bias_total):
    tokens = bias_rows.shape[1]
    scale = 1.0 / math.sqrt(HEAD)
    group_of = lax.broadcasted_iota(jnp.int32, (tokens, 128), 1) // LANES

    for half in range(2):
        parts = [
            bias[:, :, half * 4 + i, 0].reshape(tokens, 128).astype(F32) for i in range(4)
        ]
        for h in range(GROUP):
            row = parts[0] if h == 0 else pltpu.roll(parts[0], (-h) % 4 * LANES, 1)
            for i in range(1, 4):
                shift = (i - h) % 4 * LANES
                moved = pltpu.roll(parts[i], shift, 1) if shift else parts[i]
                row = jnp.where(group_of == i, moved, row)
            bias_rows[h, :, pl.ds(half * 128, 128)] = row

    @pl.loop(0, GROUP)
    def _(h):
        rows = pl.ds(pl.multiple_of(h * HEAD, 16), HEAD)
        for sample in range(2):
            columns = pl.ds(sample * tokens, tokens)
            qh, kh, vh = q[rows, columns], k[rows, columns], v[rows, columns]
            scores = t_dot(qh, kh) * scale + bias_rows[h]
            weights = jnp.exp(scores - jnp.max(scores, axis=1, keepdims=True))
            probs = weights * (1.0 / jnp.sum(weights, axis=1, keepdims=True))
            probs_b = probs.astype(BF16)
            attended = dot_t(vh, probs_b)
            gate_h, up_h = gate[rows, columns], up[rows, columns]
            gated[rows, columns] = (gate_h * attended).astype(BF16)
            d_att = (up_h * gate_h).astype(BF16)
            d_every[1, rows, columns] = (up_h * attended * gate_h * (1.0 - gate_h)).astype(BF16)
            d_probs = t_dot(d_att, vh)
            inner = jnp.sum(probs * d_probs, axis=1, keepdims=True)
            d_scores = probs * (d_probs - inner)
            d_scores_b = d_scores.astype(BF16)
            d_every[0, rows, columns] = (dot_t(kh, d_scores_b) * scale).astype(BF16)
            d_every[2, rows, columns] = (dot(qh, d_scores_b) * scale).astype(BF16)
            d_every[3, rows, columns] = dot(d_att, probs_b).astype(BF16)
            if sample == 0:
                bias_total[h] = d_scores
            else:
                bias_total[h] = bias_total[h] + d_scores

    for half in range(2):
        parts = [bias_total[h, :, pl.ds(half * 128, 128)] for h in range(GROUP)]
        for i in range(4):
            row = parts[0] if i == 0 else pltpu.roll(parts[0], (-i) % 4 * LANES, 1)
            for h in range(1, GROUP):
                shift = (h - i) % 4 * LANES
                moved = pltpu.roll(parts[h], shift, 1) if shift else parts[h]
                row = jnp.where(group_of == h, moved, row)
            d_bias[:, :, half * 4 + i, 0] = row.astype(BF16).reshape(N_CHIP, 2, 16, 128)


def attention(q, k, v, gate, up, bias):
    width, columns = q.shape
    tokens = columns // 2
    block = GROUP * HEAD
    feature = pl.BlockSpec((block, columns), lambda i: (i, 0))
    of_bias = pl.BlockSpec((N_CHIP, 2, N_SAMPLE, 1, 16, 128), lambda i: (0, 0, 0, i, 0, 0))
    return pl.pallas_call(
        attention_kernel,
        grid=(width // block,),
        in_specs=[feature] * 5 + [of_bias],
        out_specs=[feature, pl.BlockSpec((4, block, columns), lambda i: (0, i, 0)), of_bias],
        out_shape=[
            jax.ShapeDtypeStruct((width, columns), BF16),
            jax.ShapeDtypeStruct((4, width, columns), BF16),
            jax.ShapeDtypeStruct(bias.shape, BF16),
        ],
        scratch_shapes=[
            pltpu.VMEM((GROUP, tokens, tokens), F32),
            pltpu.VMEM((GROUP, tokens, tokens), F32),
        ],
        compiler_params=pltpu.CompilerParams(vmem_limit_bytes=40 << 20),
    )(q, k, v, gate, up, bias)


ROWS = 192
WIDTH = 640
SMALL = 2048


def norm_back_rows(normed, inverse, incoming, axis):
    first = jnp.mean(incoming, axis=axis, keepdims=True)
    second = jnp.mean(incoming * normed, axis=axis, keepdims=True)
    return (incoming - first - normed * second) * inverse


def backward_kernel(
    d_bias,
    pair,
    mask,
    in_w_t,
    gate_w,
    out_w,
    bias_w_t,
    following,
    product,
    left,
    right,
    cot_pair,
    atom_grad,
    left_in,
    right_in,
    left_out,
    right_out,
    grad_pair,
    in_sum,
    out_sum,
    small_sum,
    pair_sum,
    by_chip,
    by_sample,
    bias_block,
    head_rows,
    coefficient,
    keep,
    keep_p,
    x1,
    mid,
    mid_rows,
    x2,
    arrived,
    arrived_rows,
    panel,
    x3,
    back,
    back_rows,
    x4,
    final,
    small,
    small_part,
    small_mid,
    small_last,
    theirs,
    mine,
    from_core,
    part1,
    sum1,
    part2,
    sum2,
    part3,
    full,
    other,
    send_sem,
    recv_sem,
    chip_sem,
    w_send,
    w_recv,
):
    t, s = lax.axis_index("tile"), lax.axis_index("sample")
    m, core = t // 2, lax.rem(t, 2)
    partner_t = m * 2 + 1 - core
    place = [lax.rem(s, 2) * 2 + t // 8, lax.rem(t // 2, 4), s // 2]
    tile_peers = [lax.rem(t + k, N_TILE) for k in range(1, N_TILE)]
    sample_peers = [lax.rem(s + k, N_SAMPLE) for k in range(1, N_SAMPLE)]

    def peer(axis, k):
        where = list(place)
        where[axis] = lax.rem(place[axis] + k, 4)
        x, y, z = where
        return where[axis], (lax.rem(x, 2) * 8 + y * 2 + core, z * 2 + x // 2)

    barrier = pltpu.get_barrier_semaphore()
    for d in sample_peers:
        pl.semaphore_signal(barrier, inc=1, device_id=(t, d), device_id_type=MESH)
    for d in tile_peers:
        pl.semaphore_signal(barrier, inc=1, device_id=(d, s), device_id_type=MESH)
    diagonal = (lax.rem(t + 8, N_TILE), s + 1 - 2 * lax.rem(s, 2))
    pl.semaphore_signal(barrier, inc=1, device_id=diagonal, device_id_type=MESH)

    def form(g, c, target):
        wide = pl.ds(pl.multiple_of(g * 1024 + c * 512, 512), 512)
        narrow = pl.ds(pl.multiple_of(g * 256 + c * 128, 128), 128)

        @pl.loop(0, 4)
        def _(a):
            rows = pl.ds(pl.multiple_of(a * ROWS, 64), ROWS)
            target[g, a, :, pl.ds(0, 512)] = dot_t(left_in[rows, :], right_in[wide, :]).astype(BF16)
            target[g, a, :, pl.ds(512, 128)] = dot(left_out[rows, :], right_out[:, narrow]).astype(
                BF16
            )

    def form_theirs(g):
        form(g, 1 - core, theirs)
        send(theirs.at[g], from_core.at[g], w_send.at[0], w_recv.at[g, 0], partner_t, s)

    def form_mine(g):
        form(g, core, mine)

    def add_cores(g):
        wait_bytes(from_core.at[g], w_recv.at[g, 0])

        @pl.loop(0, 4)
        def _(a):
            @pl.loop(0, ROWS // 16)
            def _(r):
                rows = pl.ds(pl.multiple_of(r * 16, 16), 16)
                total = mine[g, a, rows, :].astype(F32) + from_core[g, a, rows, :].astype(F32)
                mine[g, a, rows, :] = total.astype(BF16)

        for k in range(1, 4):
            d, to = peer(g, k)
            send(mine.at[g, d], part1.at[g, k - 1], w_send.at[1], w_recv.at[g, 1], *to)

    def add_first(g):
        p1 = place[g]
        wait_bytes(part1.at[g], w_recv.at[g, 1])

        @pl.loop(0, ROWS // 16)
        def _(r):
            rows = pl.ds(pl.multiple_of(r * 16, 16), 16)
            total = mine[g, p1, rows, :].astype(F32)
            for k in range(3):
                total = total + part1[g, k, rows, :].astype(F32)
            sum1[g, rows, :] = total.astype(BF16)

        for k in range(1, 4):
            d, to = peer((g + 1) % 3, k)
            rows = pl.ds(pl.multiple_of(d * 48, 16), 48)
            send(sum1.at[g, rows], part2.at[g, k - 1], w_send.at[2], w_recv.at[g, 2], *to)

    def add_second(g):
        p2, p3 = place[(g + 1) % 3], place[(g + 2) % 3]
        wait_bytes(part2.at[g], w_recv.at[g, 2])
        total = sum1[g, pl.ds(pl.multiple_of(p2 * 48, 16), 48), :].astype(F32)
        for k in range(3):
            total = total + part2[g, k].astype(F32)
        sum2[g] = total.astype(BF16)
        for k in range(1, 4):
            _, to = peer((g + 2) % 3, k)
            send(sum2.at[g], part3.at[g, p3], w_send.at[3], w_recv.at[g, 3], *to)
        part3[g, p3] = sum2[g]

    def add_third(g):
        p1, p2 = place[g], place[(g + 1) % 3]
        wait_bytes(part3.at[g, pl.ds(0, 3)], w_recv.at[g, 3])
        total = part3[g, 0].astype(F32)
        for k in range(1, 4):
            total = total + part3[g, k].astype(F32)
        rows = pl.ds(pl.multiple_of(p2 * 48, 16), 48)
        full[g, p1, rows, :] = total.astype(BF16)
        block = full.at[g, p1, rows]
        for k in range(1, 4):
            _, to = peer((g + 1) % 3, k)
            send(block, block, w_send.at[4], w_recv.at[g, 4], *to)

    def gather_second(g):
        p1 = place[g]
        wait_bytes(full.at[g, p1, pl.ds(0, 144)], w_recv.at[g, 4])
        block = full.at[g, p1]
        for k in range(1, 4):
            _, to = peer(g, k)
            send(block, block, w_send.at[5], w_recv.at[g, 5], *to)
        send(block, other.at[g, p1], w_send.at[6], w_recv.at[g, 6], partner_t, s)

    def unpack(source, g, c):
        wide = pl.ds(pl.multiple_of(g * 1024 + c * 512, 512), 512)
        narrow = pl.ds(pl.multiple_of(g * 256 + c * 128, 128), 128)

        @pl.loop(0, 4)
        def _(a):
            @pl.loop(0, ROWS // 16)
            def _(r):
                rows = pl.ds(pl.multiple_of(r * 16, 16), 16)
                to_rows = pl.ds(pl.multiple_of(a * ROWS + r * 16, 16), 16)
                in_sum[to_rows, wide] = source[g, a, rows, pl.ds(0, 512)]
                out_sum[to_rows, narrow] = source[g, a, rows, pl.ds(512, 128)]

    def gather_first(g):
        wait_bytes(full.at[g, pl.ds(0, 3)], w_recv.at[g, 5])
        for k in range(1, 4):
            p1 = lax.rem(place[g] + k, 4)
            send(full.at[g, p1], other.at[g, p1], w_send.at[6], w_recv.at[g, 6], partner_t, s)

    pl.semaphore_wait(barrier, N_SAMPLE + N_TILE - 1)
    for k in range(1, N_CHIP + 1):
        d = lax.rem(m + k, N_CHIP)
        send(d_bias.at[d, 1 - core], pair_sum.at[d], send_sem.at[0], chip_sem.at[k - 1], partner_t, s)

    keep[0], inverse_z = norm_rows(pair[...].astype(F32), 1)
    normed_z = keep[0].astype(BF16)

    def project(block):
        return dot_t(in_w_t[pl.ds(block * 128, 128), :], normed_z)

    for side in range(2):
        gate_side = sigmoid(project(2 * side))
        masked = gate_side * mask[...]
        coefficient[2 * side] = masked * (1.0 - gate_side) * project(2 * side + 1)
        coefficient[2 * side + 1] = masked
    keep[1] = sigmoid(dot(normed_z, gate_w[...]))
    keep_p[...], inverse_p = norm_rows(product[...].reshape(128, 512).astype(F32), 0)
    normed_p = keep_p[...].astype(BF16)
    keep[2] = t_dot(normed_p, out_w[...])
    keep[3], inverse_n = norm_rows(following[...], 1)
    normed_n = keep[3].astype(BF16)

    for k in range(1, N_CHIP + 1):
        d = lax.rem(m + k, N_CHIP)
        wait_bytes(pair_sum.at[d], chip_sem.at[k - 1])
        pair_sum[d] = (pair_sum[d].astype(F32) + d_bias[d, core].astype(F32)).astype(BF16)
        if k < N_CHIP:
            send(
                pair_sum.at[d],
                by_chip.at[k - 1],
                send_sem.at[1],
                chip_sem.at[N_CHIP + k - 1],
                d * 2 + core,
                s,
            )
    for g in range(3):
        form_theirs(g)
    form_mine(0)
    total = pair_sum[m].astype(F32)
    for k in range(1, N_CHIP):
        wait_bytes(by_chip.at[k - 1], chip_sem.at[N_CHIP + k - 1])
        total = total + by_chip[k - 1].astype(F32)
    pair_sum[m] = total.astype(BF16)
    for k in range(1, N_SAMPLE):
        send(
            pair_sum.at[m, sample_peers[k - 1]],
            by_sample.at[k - 1],
            send_sem.at[2],
            recv_sem.at[2],
            t,
            sample_peers[k - 1],
        )
    form_mine(1)
    wait_bytes(by_sample, recv_sem.at[2])
    bias_block[...] = pair_sum[m, s].astype(F32) + jnp.sum(by_sample[...].astype(F32), axis=0)

    for part in range(4):
        rows = [bias_block[:, part * 4 + i] for i in range(4)]
        for h in range(4):
            head_rows[part, pl.ds(h, 4, stride=4), :] = place_lanes(rows, h)
    d_heads = jnp.concatenate([head_rows[part] for part in range(4)], axis=1)
    high = d_heads.astype(BF16)
    low = (d_heads - high.astype(F32)).astype(BF16)
    d_normed_n = t_dot(high, bias_w_t[...]) + t_dot(low, bias_w_t[...])
    small[...] = jnp.zeros((128, SMALL), BF16)
    small[pl.ds(0, 16), pl.ds(1536, 128)] = (dot(high, normed_n) + dot(low, normed_n)).astype(BF16)
    small[:, pl.ds(768, 768)] = atom_grad[...]
    d_next = cot_pair[...].astype(F32) + norm_back_rows(keep[3], inverse_n, d_normed_n, 1)
    tri_gate = keep[1]
    d_linear = (d_next * tri_gate).astype(BF16)
    d_gate = (d_next * keep[2] * tri_gate * (1.0 - tri_gate)).astype(BF16)
    keep[4] = d_next
    d_product = norm_back_rows(keep_p[...], inverse_p, dot_t(out_w[...], d_linear), 0).astype(BF16)
    for d in range(N_SAMPLE):
        x1[d] = d_product[d * 16 : d * 16 + 16]
    for d in sample_peers:
        send(x1.at[d], mid.at[s], send_sem.at[3], recv_sem.at[3], t, d)
    mid[s] = x1[s]
    small[:, pl.ds(512, 128)] = t_dot(normed_z, d_gate).astype(BF16)
    small[:, pl.ds(640, 128)] = dot(normed_p, d_linear).astype(BF16)
    keep[5] = dot_t(d_gate, gate_w[...])
    add_cores(0)
    wait_bytes(mid.at[pl.ds(0, N_SAMPLE - 1)], recv_sem.at[3])
    split_lanes(mid[...].reshape(128, 512).astype(F32), mid_rows)
    for d in range(N_TILE):
        for part in range(4):
            x2[d, :, pl.ds(part * 128, 128)] = mid_rows[part, pl.ds(d, 8, stride=16), :]
    for d in tile_peers:
        send(x2.at[d], arrived.at[t], send_sem.at[4], recv_sem.at[4], d, s)
    arrived[t] = x2[t]
    add_cores(1)
    form_mine(2)
    wait_bytes(arrived.at[pl.ds(0, N_TILE - 1)], recv_sem.at[4])
    split_lanes(arrived[...].reshape(128, 512), arrived_rows)
    panel_of(arrived_rows, 0, 8, panel)
    d_panel = joined(panel).astype(BF16)
    x3[:, 0] = dot(d_panel, right[...]).astype(BF16).reshape(N_TILE, 16, 256)
    x3[:, 1] = t_dot(d_panel, left[...]).astype(BF16).reshape(N_TILE, 16, 256)
    for d in tile_peers:
        send(x3.at[d], back.at[t], send_sem.at[5], recv_sem.at[5], d, s)
    back[t] = x3[t]
    add_cores(2)
    wait_bytes(back.at[pl.ds(0, N_TILE - 1)], recv_sem.at[5])
    for side in range(2):
        split_lanes(back[:, side].reshape(256, 256).astype(F32), back_rows)

        def store(d, lanes, rows, side=side):
            x4[d, side, :, lanes] = rows.astype(BF16)

        blocks_of(back_rows, store)
    for d in sample_peers:
        send(x4.at[d], final.at[s], send_sem.at[6], recv_sem.at[6], t, d)
    final[s] = x4[s]
    add_first(0)
    wait_bytes(final.at[pl.ds(0, N_SAMPLE - 1)], recv_sem.at[6])
    d_normed_z = keep[5]
    for block in range(4):
        incoming = final[:, block // 2].reshape(128, 512).astype(F32)
        d_proj = (incoming * coefficient[block]).astype(BF16)
        small[:, pl.ds(block * 128, 128)] = dot(d_proj, normed_z).astype(BF16)
        d_normed_z = d_normed_z + t_dot(d_proj, in_w_t[pl.ds(block * 128, 128), :])
    for k in range(1, N_SAMPLE):
        d = sample_peers[k - 1]
        rows = pl.ds(pl.multiple_of(d * 16, 16), 16)
        send(small.at[rows], small_part.at[k - 1], send_sem.at[7], recv_sem.at[7], t, d)
    grad_pair[...] = keep[4] + norm_back_rows(keep[0], inverse_z, d_normed_z, 1)
    add_first(1)
    add_first(2)
    wait_bytes(small_part, recv_sem.at[7])
    own = pl.ds(pl.multiple_of(s * 16, 16), 16)
    total = small[own, :].astype(F32)
    for k in range(N_SAMPLE - 1):
        total = total + small_part[k].astype(F32)
    small_mid[...] = total.astype(BF16)
    for k in range(1, N_TILE):
        d = tile_peers[k - 1]
        lanes = pl.ds(pl.multiple_of(d * 128, 128), 128)
        send(small_mid.at[:, lanes], small_last.at[k - 1], send_sem.at[8], recv_sem.at[8], d, s)
    for g in range(3):
        add_second(g)
    wait_bytes(small_last, recv_sem.at[8])
    lanes = pl.ds(pl.multiple_of(t * 128, 128), 128)
    total = small_mid[:, lanes].astype(F32)
    for k in range(N_TILE - 1):
        total = total + small_last[k].astype(F32)
    small_sum[own, lanes] = total.astype(BF16)
    block = small_sum.at[own, lanes]
    for d in tile_peers:
        send(block, block, send_sem.at[9], recv_sem.at[9], d, s)
    for g in range(3):
        add_third(g)
    wait_bytes(small_last, recv_sem.at[9])
    block = small_sum.at[own]
    for d in sample_peers:
        send(block, block, send_sem.at[10], recv_sem.at[10], t, d)
    for g in range(3):
        gather_second(g)
    for g in range(3):
        gather_first(g)
        unpack(full, g, core)
    wait_bytes(small_part, recv_sem.at[10])
    for g in range(3):
        wait_bytes(other.at[g], w_recv.at[g, 6])
        unpack(other, g, 1 - core)

    wait_bytes(pair_sum, send_sem.at[0])
    wait_bytes(by_chip, send_sem.at[1])
    wait_bytes(by_sample, send_sem.at[2])
    wait_bytes(mid.at[pl.ds(0, N_SAMPLE - 1)], send_sem.at[3])
    wait_bytes(arrived.at[pl.ds(0, N_TILE - 1)], send_sem.at[4])
    wait_bytes(back.at[pl.ds(0, N_TILE - 1)], send_sem.at[5])
    wait_bytes(final.at[pl.ds(0, N_SAMPLE - 1)], send_sem.at[6])
    wait_bytes(small_part, send_sem.at[7])
    wait_bytes(small_last, send_sem.at[8])
    wait_bytes(small_last, send_sem.at[9])
    wait_bytes(small_part, send_sem.at[10])
    wait_bytes(theirs, w_send.at[0])
    wait_bytes(part1, w_send.at[1])
    wait_bytes(part2, w_send.at[2])
    wait_bytes(part3.at[:, pl.ds(0, 3)], w_send.at[3])
    wait_bytes(part2, w_send.at[4])
    wait_bytes(part1, w_send.at[5])
    wait_bytes(theirs, w_send.at[6])


def backward(collective_id, *operands):
    vmem = pl.BlockSpec(memory_space=pltpu.VMEM)
    chunk = (3, 4, ROWS, WIDTH)
    block = (4, 16, 128)
    return pl.pallas_call(
        backward_kernel,
        out_shape=[
            jax.ShapeDtypeStruct((512, 128), F32),
            jax.ShapeDtypeStruct((768, 3072), BF16),
            jax.ShapeDtypeStruct((768, 768), BF16),
            jax.ShapeDtypeStruct((128, SMALL), BF16),
        ],
        in_specs=[vmem] * len(operands),
        out_specs=[vmem] * 4,
        scratch_shapes=[
            pltpu.VMEM((N_CHIP, N_SAMPLE) + block, BF16),
            pltpu.VMEM((N_CHIP - 1, N_SAMPLE) + block, BF16),
            pltpu.VMEM((N_SAMPLE - 1,) + block, BF16),
            pltpu.VMEM(block, F32),
            pltpu.VMEM((4, 16, 128), F32),
            pltpu.VMEM((4, 128, 512), F32),
            pltpu.VMEM((6, 512, 128), F32),
            pltpu.VMEM((128, 512), F32),
            pltpu.VMEM((N_SAMPLE, 16, 512), BF16),
            pltpu.VMEM((N_SAMPLE, 16, 512), BF16),
            pltpu.VMEM((4, 128, 128), F32),
            pltpu.VMEM((N_TILE, 8, 512), F32),
            pltpu.VMEM((N_TILE, 8, 512), F32),
            pltpu.VMEM((4, 128, 128), F32),
            pltpu.VMEM((2, 256, 128), F32),
            pltpu.VMEM((N_TILE, 2, 16, 256), BF16),
            pltpu.VMEM((N_TILE, 2, 16, 256), BF16),
            pltpu.VMEM((2, 256, 128), F32),
            pltpu.VMEM((N_SAMPLE, 2, 16, 512), BF16),
            pltpu.VMEM((N_SAMPLE, 2, 16, 512), BF16),
            pltpu.VMEM((128, SMALL), BF16),
            pltpu.VMEM((N_SAMPLE - 1, 16, SMALL), BF16),
            pltpu.VMEM((16, SMALL), BF16),
            pltpu.VMEM((N_TILE - 1, 16, 128), BF16),
            pltpu.VMEM(chunk, BF16),
            pltpu.VMEM(chunk, BF16),
            pltpu.VMEM(chunk, BF16),
            pltpu.VMEM((3, 3, ROWS, WIDTH), BF16),
            pltpu.VMEM((3, ROWS, WIDTH), BF16),
            pltpu.VMEM((3, 3, 48, WIDTH), BF16),
            pltpu.VMEM((3, 48, WIDTH), BF16),
            pltpu.VMEM((3, 4, 48, WIDTH), BF16),
            pltpu.VMEM(chunk, BF16),
            pltpu.VMEM(chunk, BF16),
            pltpu.SemaphoreType.DMA((11,)),
            pltpu.SemaphoreType.DMA((11,)),
            pltpu.SemaphoreType.DMA((15,)),
            pltpu.SemaphoreType.DMA((7,)),
            pltpu.SemaphoreType.DMA((3, 7)),
        ],
        compiler_params=pltpu.CompilerParams(
            collective_id=collective_id, has_side_effects=True, vmem_limit_bytes=56 << 20
        ),
    )(*operands)


def norm_parts(values, axis):
    centered = values - jnp.mean(values, axis=axis, keepdims=True)
    inverse = lax.rsqrt(jnp.mean(centered * centered, axis=axis, keepdims=True) + EPSILON)
    return (centered * inverse, inverse)


def norm_back(normed, inverse, incoming_gradient, axis):
    first_mean = jnp.mean(incoming_gradient, axis=axis, keepdims=True)
    second_mean = jnp.mean(incoming_gradient * normed, axis=axis, keepdims=True)
    return (incoming_gradient - first_mean - normed * second_mean) * inverse


def silu_slope(values):
    sigmoid_part = jax.nn.sigmoid(values)
    return sigmoid_part * (1.0 + values * (1.0 - sigmoid_part))


def shards(
    pair,
    pair_mask,
    tri_in_w,
    tri_gate_w,
    tri_out_w,
    bias_w,
    atom_feats,
    atom_to_token,
    atom_w,
    tokens,
    attention_input_weight,
    attention_output_weight,
    cot_pair,
    token_output_cotangent,
):
    hidden = tri_in_w.shape[1] // 4
    token_width = attention_input_weight.shape[0]
    head_count = bias_w.shape[1]
    total_tokens = tokens.shape[1]
    pair_rows = pair.reshape(-1, hidden)
    mask_row = pair_mask.astype(F32).reshape(1, -1)
    in_w_t, bias_w_t = tri_in_w.T, bias_w.T
    following, bias_all, left_panel, right_panel, product, every_feat, every_atom = pair_forward(
        pair_rows,
        mask_row,
        in_w_t,
        tri_gate_w,
        tri_out_w,
        bias_w_t,
        atom_feats,
        atom_to_token[None],
        0,
    )
    every_feat = every_feat.reshape(-1, atom_feats.shape[1])
    every_atom = every_atom.reshape(-1)
    atom_pre = jnp.dot(every_feat, atom_w, preferred_element_type=jnp.float32)
    atom_act = jax.nn.silu(atom_pre).astype(BF16)
    token_ids = jnp.arange(total_tokens, dtype=jnp.int32)
    one_hot = (token_ids[:, None] == every_atom[None, :]).astype(BF16)
    token_sums = jnp.dot(one_hot, atom_act, preferred_element_type=F32)
    token_counts = jnp.sum(one_hot.astype(F32), axis=1)
    token_cond = token_sums / token_counts[:, None]
    token_state_rows = tokens.astype(jnp.float32) + token_cond[None]
    normed_h, inverse_h = norm_parts(token_state_rows, 2)
    normalized_hidden_bfloat = normed_h.astype(jnp.bfloat16)
    hidden_t = normalized_hidden_bfloat.reshape(-1, token_width).T
    cot_rows = token_output_cotangent.reshape(-1, token_width)

    def project(block):
        weight = attention_input_weight[:, block * token_width : (block + 1) * token_width]
        return t_dot(weight, hidden_t)

    gated_t, d_every_t, bias_blocks = attention(
        project(0).astype(BF16),
        project(2).astype(BF16),
        project(3).astype(BF16),
        jax.nn.sigmoid(project(1)),
        dot_t(attention_output_weight, cot_rows),
        bias_all,
    )
    d_every_t = d_every_t.reshape(4 * token_width, -1)
    token_output_rows = token_state_rows + t_dot(gated_t, attention_output_weight).reshape(
        token_state_rows.shape
    )
    normalized_hidden_gradient = lax.dot_general(
        d_every_t, attention_input_weight, (((0,), (1,)), ((), ())), preferred_element_type=F32
    ).reshape(token_state_rows.shape)
    grad_tokens = token_output_cotangent.astype(jnp.float32) + norm_back(
        normed_h, inverse_h, normalized_hidden_gradient, 2
    )
    cond_grad = (jnp.sum(grad_tokens, axis=0) / token_counts[:, None]).astype(BF16)
    d_act = lax.dot_general(
        one_hot, cond_grad, (((0,), (0,)), ((), ())), preferred_element_type=F32
    ) * silu_slope(atom_pre)
    grad_atom_w = lax.dot_general(
        every_feat, d_act.astype(BF16), (((0,), (0,)), ((), ())), preferred_element_type=F32
    )
    grad_pair, in_sum, out_sum, small_sum = backward(
        1,
        bias_blocks,
        pair_rows,
        mask_row,
        in_w_t,
        tri_gate_w,
        tri_out_w,
        bias_w_t,
        following,
        product,
        left_panel,
        right_panel,
        cot_pair.reshape(-1, hidden),
        grad_atom_w.astype(BF16),
        hidden_t,
        d_every_t,
        gated_t,
        cot_rows,
    )
    small_sum = small_sum.astype(F32)
    at = 4 * hidden
    summed = (
        small_sum[:, :at].reshape(hidden, 4, hidden).transpose(2, 1, 0).reshape(hidden, at),
        small_sum[:, at : at + hidden],
        small_sum[:, at + hidden : at + 2 * hidden],
        small_sum[:head_count, at + 2 * hidden + token_width :][:, :hidden].T,
        small_sum[:, at + 2 * hidden : at + 2 * hidden + token_width],
        in_sum.astype(F32),
        out_sum.astype(F32),
    )
    pair_next, grad_pair = following.reshape(pair.shape), grad_pair.reshape(pair.shape)
    return (pair_next, token_output_rows, grad_pair, grad_tokens) + summed


def solution(mesh):
    in_specs = (
        P("tile", "sample", None),
        P("tile", "sample"),
        P(),
        P(),
        P(),
        P(),
        P("tile", None),
        P("tile"),
        P(),
        P(("tile", "sample"), None, None),
        P(),
        P(),
        P("tile", "sample", None),
        P(("tile", "sample"), None, None),
    )
    out_specs = (
        P("tile", "sample", None),
        P(("tile", "sample"), None, None),
        P("tile", "sample", None),
        P(("tile", "sample"), None, None),
        P(),
        P(),
        P(),
        P(),
        P(),
        P(),
        P(),
    )
    return jax.shard_map(shards, mesh=mesh, in_specs=in_specs, out_specs=out_specs, check_vma=False)
```

time: 298 us -> 245 us (0.82)
  local copies, waits for them, and re-layouts: 44.9 us -> 20.7 us
  Pallas kernels: 201 us -> 187 us
  matrix products: 30.5 us -> 22 us
  other arithmetic: 18.3 us -> 13.5 us
    pallas_call x4 -> x1, Pallas kernels: 125 us -> 111 us  [backward(): pl.pallas_call(backward_kernel, out_shape=[jax.ShapeDtypeStruct((512, 128...]
    reshape x8 -> x2, local copies, waits for them, and re-layouts: 8.99 us -> 0.17 us  [the longest x1 0.09 us: shards(): small_sum[:, :at].reshape(hidden, 4, hidden).transpose(2, 1, 0)]
    dot_general x13 -> x0, matrix products: 8.14 us -> none  [the longest x1 1.28 us: shards(): jnp.dot(d_product_panel, right_panel, preferred_element_type=F32)]
    convert_element_type x4 -> x0, local copies, waits for them, and re-layouts: 5.06 us -> none  [the longest x2 2.84 us: shards(): product = product.reshape(hidden, rows, columns).astype(F32)]
    unnamed x105 -> x64, local copies, waits for them, and re-layouts: 16.8 us -> 12.3 us
where the time goes in v1:
time: 245 us; the launch traced here: 244 us
  Pallas kernels  187 us (76%)
  matrix products  22 us (9%)
  local copies, waits for them, and re-layouts  20.7 us (8%)
  other arithmetic  13.5 us (6%)
    pallas_call x1, Pallas kernels, backward(): pl.pallas_call(backward_kernel, out_shape=[jax.ShapeDtypeStruct((512, 128...  111 us
    pallas_call x1, Pallas kernels, pair_forward(): pl.pallas_call(pair_forward_kernel, out_shape=[jax.ShapeDtypeStruct(pair....  52.2 us
    pallas_call x1, Pallas kernels, attention(): pl.pallas_call(attention_kernel, grid=(width // block,), in_specs=[featur...  23.9 us
    unnamed x64, local copies, waits for them, and re-layouts  12.3 us
    convert_element_type x1, other arithmetic, shards(): in_sum.astype(F32)  7.47 us
    dot_general x1, matrix products, shards(): lax.dot_general(every_feat, d_act.astype(BF16), (((0,), (0,)), ((), ())),...  6.44 us
    dot_general x1, matrix products, shards(): lax.dot_general(d_every_t, attention_input_weight, (((0,), (1,)), ((), ()...  6.24 us
    dot_general x1, local copies, waits for them, and re-layouts, shards(): lax.dot_general(d_every_t, attention_input_weight, (((0,), (1,)), ((), ()...  4.92 us

profile of v1, /device:TPU:1, one launch (start us, length us, event | category | flops | bytes accessed | tf_op | source)
XLA Modules:
  0.0 244.0 jit_solution(8589599617752010898)
XLA Ops:
  0.7 1.1 copy.33
  2.6 0.9 copy-done.7
  3.5 0.8 copy-done.11
  7.1 52.2 %shard_map.221 = (f32[512,128]{1,0:T(8,128)S(1)}, bf16[8,2,8,4,16,128]{5,4,3,2,1,0:T(8,128)(2,1)S(1)}, bf16[256,256]{1,0:T(8,128)(2,1)S(1)}, bf16[256,256]{1,0:T...) custom-call(bf16[512,128]{1,0:T(8,128)(2,1)S(1)} %bitcast.58, ...), custom_call_target="tpu_custom_call" | custom-call | tf_op jit(solution)/shard_map/pallas_call | solution.py:231
  59.7 2.0 fusion.29
  61.8 2.2 fusion.21
  65.7 1.0 divide_bitcast_fusion.gate
  66.7 0.8 fusion.10.q
  67.6 0.8 fusion.11.k
  68.4 0.8 fusion.12.v
  69.5 0.8 fusion.30.up
  70.3 23.9 %shard_map.222 = (bf16[768,512]{1,0:T(8,128)(2,1)S(1)}, bf16[4,768,512]{2,1,0:T(8,128)(2,1)S(1)}, bf16[8,2,8,4,16,128]{5,4,3,2,1,0:T(8,128)(2,1)S(1)}) custom-call(bf16[768,512]{1,0:T(8,128)(2,1)S(1)} %fusion.10.q, bf16[768,512]{1,0:T(8,128)(2,1)S(1)} %fusion.11.k, bf16[768,512]{1,0:T(8,128)(2,1)S(1)} %fusion.12.v, f32[768,512]{1,0:T(8,128)S(1)} %divide_bitcast_fusion.gate, ...), custom_call_target="tpu_custom_call" | custom-call | tf_op jit(solution)/shard_map/pallas_call | solution.py:328
  94.3 1.6 copy-done.1
  95.9 1.3 copy-done.2
  97.2 4.9 %copy.46 = bf16[512,3072]{1,0:T(8,128)(2,1)} copy(bf16[512,3072]{0,1:T(8,128)(2,1)} %bitcast.50) | data formatting | bytes 6291456 | tf_op jit(solution)/shard_map/dot_general | solution.py:873
  102.2 6.2 %fusion.26 = (f32[2,256]{1,0:T(2,128)S(1)}, f32[2,256]{1,0:T(2,128)S(1)}, f32[2,256,768]{2,1,0:T(8,128)S(1)}) fusion(f32[2,256]{1,0:T(2,128)S(1)} %add_rsqrt_fusion, f32[2,256]{1,0:T(2,128)S(1)} %broadcast_multiply_fusion.2, f32[256,768]{1,0:T(8,128)} %copy-done.19, bf16[2,256,768]{2,1,0:T(8,128)(2,1)S(1)} %copy-done.18, ...), kind=kOutput, calls=%fused_computation.44 | convolution fusion | flops 2418670592 | bytes 11018240 | tf_op jit(solution)/shard_map/dot_general | solution.py:873
  108.4 0.8 fusion.31
  109.8 2.4 fusion.27
  112.2 6.4 %fusion.17.atom_grad = bf16[128,768]{1,0:T(8,128)(2,1)} fusion(bf16[2048,128]{1,0:T(8,128)(2,1)S(1)} %bitcast.53, f32[2048,768]{1,0:T(8,128)} %copy-done.17, s32[2048]{0:T(1024)S(1)} %bitcast.63, f32[256,768]{1,0:T(8,128)S(1)} %get-tuple-element.41, f32[256]{0:T(256)S(1)} %convert_reduce_fusion), kind=kOutput, calls=%fused_computation.30 | convolution fusion | flops 1223131136 | bytes 7808000 | tf_op jit(solution)/shard_map/dot_general | solution.py:883
  118.6 1.2 copy.45
  119.8 110.6 %shard_map.223 = (f32[512,128]{1,0:T(8,128)}, bf16[768,3072]{1,0:T(8,128)(2,1)}, bf16[768,768]{1,0:T(8,128)(2,1)}, bf16[128,2048]{1,0:T(8,128)(2,1)}) custom-call(bf16[8,2,8,4,16,128]{5,4,3,2,1,0:T(8,128)(2,1)} %copy-done.2, bf16[512,128]{1,0:T(8,128)(2,1)} %bitcast.57, f32[1,512]{1,0:T(1,128)} %copy-done.14, bf16[512,128]{1,0:T(8,128)(2,1)} %bitcast.55, ...), custom_call_target="tpu_custom_call" | custom-call | tf_op jit(solution)/shard_map/pallas_call | solution.py:734
  230.4 7.5 %convert_element_type.71 = f32[768,3072]{1,0:T(8,128)} convert(bf16[768,3072]{1,0:T(8,128)(2,1)} %get-tuple-element.37) | non-fusion elementwise | flops 2359296 | bytes 14155776 | tf_op jit(solution)/shard_map/convert_element_type | solution.py:914
  237.8 1.6 convert_element_type.72
  241.1 0.8 slice.42
  (75 shorter events, 10.2 us)
Async XLA Ops:
  0.6 68.6 %copy-start = (bf16[768,768]{1,0:T(8,128)(2,1)S(1)}, bf16[768,768]{1,0:T(8,128)(2,1)}, u32[]{:S(2)}) copy-start(bf16[768,768]{1,0:T(8,128)(2,1)} %param.25) | copy-start | bytes 3538948
  1.8 59.9 %copy-start.3 = (bf16[128,512]{0,1:T(8,128)(2,1)}, bf16[128,512]{0,1:T(8,128)(2,1)S(1)}, u32[]{:S(2)}) copy-start(bf16[128,512]{0,1:T(8,128)(2,1)S(1)} %copy.33) | copy-start | bytes 393220
  2.6 59.1 %copy-start.14 = (f32[1,512]{1,0:T(1,128)}, f32[1,512]{1,0:T(1,128)S(1)}, u32[]{:S(2)}) copy-start(f32[1,512]{1,0:T(1,128)S(1)} %reshape.84.mask) | copy-start | bytes 6148
  2.6 0.9 copy-start.7
  59.3 2.4 copy-start.4
  59.4 2.4 copy-start.8
  59.4 2.4 copy-start.9
  59.4 2.4 copy-start.10
  59.7 6.0 %slice-start = ((s8[4718592]{0:T(1024)(128)(4,1)}), s8[4194304]{0:T(1024)(128)(4,1)S(1)}, s32[]{:S(2)}) async-start(s8[4718592]{0:T(1024)(128)(4,1)} %bitcast.79), calls=%async_computation | async-start | bytes 8388608
  61.8 2.7 %copy-start.17 = (f32[2048,768]{1,0:T(8,128)}, f32[2048,768]{1,0:T(8,128)S(1)}, u32[]{:S(2)}) copy-start(f32[2048,768]{1,0:T(8,128)S(1)} %fusion.29) | copy-start | bytes 18874372
  61.8 2.7 %copy-start.18 = (bf16[2,256,768]{2,1,0:T(8,128)(2,1)S(1)}, bf16[2,256,768]{2,1,0:T(8,128)(2,1)}, u32[]{:S(2)}) copy-start(bf16[2,256,768]{2,1,0:T(8,128)(2,1)} %param.23) | copy-start | bytes 2359300
  61.8 3.9 %slice-start.1 = ((s8[4718592]{0:T(1024)(128)(4,1)}), s8[524288]{0:T(1024)(128)(4,1)S(1)}, s32[]{:S(2)}) async-start(s8[4718592]{0:T(1024)(128)(4,1)} %bitcast.79), calls=%async_computation.1 | async-start | bytes 1048576
  65.7 2.7 %copy-start.22 = (bf16[2,256,768]{2,1,0:T(8,128)(2,1)}, bf16[2,256,768]{2,1,0:T(8,128)(2,1)S(1)}, u32[]{:S(2)}) copy-start(bf16[2,256,768]{2,1,0:T(8,128)(2,1)S(1)} %fusion.8) | copy-start | bytes 2359300
  68.4 1.1 copy-start.24
  94.3 1.6 copy-start.1
  95.9 1.3 copy-start.2
  97.2 11.2 %copy-start.6 = (bf16[768,512]{1,0:T(8,128)(2,1)}, bf16[768,512]{1,0:T(8,128)(2,1)S(1)}, u32[]{:S(2)}) copy-start(bf16[768,512]{1,0:T(8,128)(2,1)S(1)} %get-tuple-element.29.left_out) | copy-start | bytes 2359300
  108.4 1.1 copy-start.20
  108.4 1.4 copy-start.25
  112.2 6.4 %copy-start.23 = (bf16[2,256,768]{2,1,0:T(8,128)(2,1)S(1)}, bf16[2,256,768]{2,1,0:T(8,128)(2,1)}, u32[]{:S(2)}) copy-start(bf16[2,256,768]{2,1,0:T(8,128)(2,1)} %copy-done.22) | copy-start | bytes 2359300
  230.4 7.5 %copy-start.26 = (bf16[768,768]{1,0:T(8,128)(2,1)S(1)}, bf16[768,768]{1,0:T(8,128)(2,1)}, u32[]{:S(2)}) copy-start(bf16[768,768]{1,0:T(8,128)(2,1)} %get-tuple-element.38) | copy-start | bytes 3538948
  237.8 1.6 copy-start.21
  240.1 2.5 %copy-start.5 = (f32[512,128]{1,0:T(8,128)S(1)}, f32[512,128]{1,0:T(8,128)}, u32[]{:S(2)}) copy-start(f32[512,128]{1,0:T(8,128)} %copy-done.4) | copy-start | bytes 786436
  240.2 3.1 %copy-start.27 = (f32[512,128]{1,0:T(8,128)S(1)}, f32[512,128]{1,0:T(8,128)}, u32[]{:S(2)}) copy-start(f32[512,128]{1,0:T(8,128)} %get-tuple-element.35) | copy-start | bytes 786436
  (6 other events, 4.5 us)

commit v2 on v1

--- a/solution.py
+++ b/solution.py
@@ -345,7 +345,7 @@
 
 ROWS = 192
 WIDTH = 640
-SMALL = 2048
+SMALL = 1152
 
 
 def norm_back_rows(normed, inverse, incoming, axis):
@@ -367,15 +367,22 @@
     left,
     right,
     cot_pair,
-    atom_grad,
     left_in,
     right_in,
     left_out,
     right_out,
+    in_w,
+    inverse_h,
+    counts,
+    feats,
+    atoms,
+    atom_w,
     grad_pair,
+    grad_tokens,
     in_sum,
     out_sum,
     small_sum,
+    tri_sum,
     pair_sum,
     by_chip,
     by_sample,
@@ -400,6 +407,9 @@
     small_part,
     small_mid,
     small_last,
+    tri,
+    tri_part,
+    tri_all,
     theirs,
     mine,
     from_core,
@@ -410,6 +420,9 @@
     part3,
     full,
     other,
+    d_hidden,
+    cond_grad,
+    atom_grad,
     send_sem,
     recv_sem,
     chip_sem,
@@ -541,10 +554,45 @@
             p1 = lax.rem(place[g] + k, 4)
             send(full.at[g, p1], other.at[g, p1], w_send.at[6], w_recv.at[g, 6], partner_t, s)
 
+    def token_product():
+        @pl.loop(0, 2)
+        def _(a):
+            rows = pl.ds(pl.multiple_of(a * 384, 128), 384)
+            d_hidden[rows, :] = dot(in_w[rows, :], right_in[...])
+
+    def token_norm():
+        @pl.loop(0, 4)
+        def _(a):
+            lanes = pl.ds(pl.multiple_of(a * 128, 128), 128)
+            back_t = norm_back_rows(
+                left_in[:, lanes].astype(F32), inverse_h[:, lanes], d_hidden[:, lanes], 0
+            )
+            grad_tokens[lanes, :] = right_out[lanes, :].astype(F32) + back_t.T
+
+        both = grad_tokens[pl.ds(0, 256), :] + grad_tokens[pl.ds(256, 256), :]
+        cond_grad[...] = (both / counts[...]).astype(BF16)
+
+    def atom_sums():
+        atom_grad[...] = jnp.zeros_like(atom_grad)
+
+        @pl.loop(0, atoms.shape[0])
+        def _(a):
+            feat = feats[a]
+            pre = dot(feat, atom_w[...])
+            part = sigmoid(pre)
+            token = lax.broadcasted_iota(jnp.int32, (256, atoms.shape[2]), 0)
+            one_hot = jnp.where(token == atoms[a], 1.0, 0.0).astype(BF16)
+            d_act = t_dot(one_hot, cond_grad[...]) * (part * (1.0 + pre * (1.0 - part)))
+            atom_grad[...] += t_dot(feat, d_act.astype(BF16))
+
+        small[:, pl.ds(0, 768)] = atom_grad[...].astype(BF16)
+
+    token_product()
     pl.semaphore_wait(barrier, N_SAMPLE + N_TILE - 1)
     for k in range(1, N_CHIP + 1):
         d = lax.rem(m + k, N_CHIP)
         send(d_bias.at[d, 1 - core], pair_sum.at[d], send_sem.at[0], chip_sem.at[k - 1], partner_t, s)
+    form_theirs(0)
 
     keep[0], inverse_z = norm_rows(pair[...].astype(F32), 1)
     normed_z = keep[0].astype(BF16)
@@ -557,13 +605,6 @@
         masked = gate_side * mask[...]
         coefficient[2 * side] = masked * (1.0 - gate_side) * project(2 * side + 1)
         coefficient[2 * side + 1] = masked
-    keep[1] = sigmoid(dot(normed_z, gate_w[...]))
-    keep_p[...], inverse_p = norm_rows(product[...].reshape(128, 512).astype(F32), 0)
-    normed_p = keep_p[...].astype(BF16)
-    keep[2] = t_dot(normed_p, out_w[...])
-    keep[3], inverse_n = norm_rows(following[...], 1)
-    normed_n = keep[3].astype(BF16)
-
     for k in range(1, N_CHIP + 1):
         d = lax.rem(m + k, N_CHIP)
         wait_bytes(pair_sum.at[d], chip_sem.at[k - 1])
@@ -577,9 +618,18 @@
                 d * 2 + core,
                 s,
             )
-    for g in range(3):
-        form_theirs(g)
+    form_theirs(1)
+    form_theirs(2)
+    keep[1] = sigmoid(dot(normed_z, gate_w[...]))
+    keep_p[...], inverse_p = norm_rows(product[...].reshape(128, 512).astype(F32), 0)
+    normed_p = keep_p[...].astype(BF16)
+    keep[2] = t_dot(normed_p, out_w[...])
+    keep[3], inverse_n = norm_rows(following[...], 1)
+    normed_n = keep[3].astype(BF16)
+    small[...] = jnp.zeros((128, SMALL), BF16)
+    small_mid[...] = jnp.zeros((16, N_TILE * 128), BF16)
     form_mine(0)
+    form_mine(1)
     total = pair_sum[m].astype(F32)
     for k in range(1, N_CHIP):
         wait_bytes(by_chip.at[k - 1], chip_sem.at[N_CHIP + k - 1])
@@ -594,7 +644,9 @@
             t,
             sample_peers[k - 1],
         )
-    form_mine(1)
+    add_cores(0)
+    form_mine(2)
+    add_cores(1)
     wait_bytes(by_sample, recv_sem.at[2])
     bias_block[...] = pair_sum[m, s].astype(F32) + jnp.sum(by_sample[...].astype(F32), axis=0)
 
@@ -606,24 +658,23 @@
     high = d_heads.astype(BF16)
     low = (d_heads - high.astype(F32)).astype(BF16)
     d_normed_n = t_dot(high, bias_w_t[...]) + t_dot(low, bias_w_t[...])
-    small[...] = jnp.zeros((128, SMALL), BF16)
-    small[pl.ds(0, 16), pl.ds(1536, 128)] = (dot(high, normed_n) + dot(low, normed_n)).astype(BF16)
-    small[:, pl.ds(768, 768)] = atom_grad[...]
     d_next = cot_pair[...].astype(F32) + norm_back_rows(keep[3], inverse_n, d_normed_n, 1)
     tri_gate = keep[1]
     d_linear = (d_next * tri_gate).astype(BF16)
-    d_gate = (d_next * keep[2] * tri_gate * (1.0 - tri_gate)).astype(BF16)
-    keep[4] = d_next
     d_product = norm_back_rows(keep_p[...], inverse_p, dot_t(out_w[...], d_linear), 0).astype(BF16)
     for d in range(N_SAMPLE):
         x1[d] = d_product[d * 16 : d * 16 + 16]
     for d in sample_peers:
         send(x1.at[d], mid.at[s], send_sem.at[3], recv_sem.at[3], t, d)
     mid[s] = x1[s]
-    small[:, pl.ds(512, 128)] = t_dot(normed_z, d_gate).astype(BF16)
-    small[:, pl.ds(640, 128)] = dot(normed_p, d_linear).astype(BF16)
+    d_gate = (d_next * keep[2] * tri_gate * (1.0 - tri_gate)).astype(BF16)
+    keep[4] = d_next
+    small[:, pl.ds(768, 128)] = t_dot(normed_z, d_gate).astype(BF16)
+    small[:, pl.ds(896, 128)] = dot(normed_p, d_linear).astype(BF16)
+    small[pl.ds(0, 16), pl.ds(1024, 128)] = (dot(high, normed_n) + dot(low, normed_n)).astype(BF16)
     keep[5] = dot_t(d_gate, gate_w[...])
-    add_cores(0)
+    add_cores(2)
+    token_norm()
     wait_bytes(mid.at[pl.ds(0, N_SAMPLE - 1)], recv_sem.at[3])
     split_lanes(mid[...].reshape(128, 512).astype(F32), mid_rows)
     for d in range(N_TILE):
@@ -632,8 +683,7 @@
     for d in tile_peers:
         send(x2.at[d], arrived.at[t], send_sem.at[4], recv_sem.at[4], d, s)
     arrived[t] = x2[t]
-    add_cores(1)
-    form_mine(2)
+    atom_sums()
     wait_bytes(arrived.at[pl.ds(0, N_TILE - 1)], recv_sem.at[4])
     split_lanes(arrived[...].reshape(128, 512), arrived_rows)
     panel_of(arrived_rows, 0, 8, panel)
@@ -643,7 +693,13 @@
     for d in tile_peers:
         send(x3.at[d], back.at[t], send_sem.at[5], recv_sem.at[5], d, s)
     back[t] = x3[t]
-    add_cores(2)
+    for k in range(1, N_SAMPLE):
+        d = sample_peers[k - 1]
+        rows = pl.ds(pl.multiple_of(d * 16, 16), 16)
+        send(small.at[rows], small_part.at[k - 1], send_sem.at[7], recv_sem.at[7], t, d)
+    own = pl.ds(pl.multiple_of(s * 16, 16), 16)
+    add_first(0)
+    add_first(1)
     wait_bytes(back.at[pl.ds(0, N_TILE - 1)], recv_sem.at[5])
     for side in range(2):
         split_lanes(back[:, side].reshape(256, 256).astype(F32), back_rows)
@@ -655,33 +711,31 @@
     for d in sample_peers:
         send(x4.at[d], final.at[s], send_sem.at[6], recv_sem.at[6], t, d)
     final[s] = x4[s]
-    add_first(0)
+    add_first(2)
+    wait_bytes(small_part, recv_sem.at[7])
+    total = small[own, :].astype(F32)
+    for k in range(N_SAMPLE - 1):
+        total = total + small_part[k].astype(F32)
+    small_mid[:, pl.ds(0, SMALL)] = total.astype(BF16)
+    for k in range(1, N_TILE):
+        d = tile_peers[k - 1]
+        lanes = pl.ds(pl.multiple_of(d * 128, 128), 128)
+        send(small_mid.at[:, lanes], small_last.at[k - 1], send_sem.at[8], recv_sem.at[8], d, s)
+    add_second(0)
+    add_second(1)
     wait_bytes(final.at[pl.ds(0, N_SAMPLE - 1)], recv_sem.at[6])
     d_normed_z = keep[5]
     for block in range(4):
         incoming = final[:, block // 2].reshape(128, 512).astype(F32)
         d_proj = (incoming * coefficient[block]).astype(BF16)
-        small[:, pl.ds(block * 128, 128)] = dot(d_proj, normed_z).astype(BF16)
+        tri[:, pl.ds(block * 128, 128)] = dot(d_proj, normed_z).astype(BF16)
         d_normed_z = d_normed_z + t_dot(d_proj, in_w_t[pl.ds(block * 128, 128), :])
     for k in range(1, N_SAMPLE):
         d = sample_peers[k - 1]
         rows = pl.ds(pl.multiple_of(d * 16, 16), 16)
-        send(small.at[rows], small_part.at[k - 1], send_sem.at[7], recv_sem.at[7], t, d)
+        send(tri.at[rows], tri_part.at[k - 1], send_sem.at[11], recv_sem.at[11], t, d)
+    add_second(2)
     grad_pair[...] = keep[4] + norm_back_rows(keep[0], inverse_z, d_normed_z, 1)
-    add_first(1)
-    add_first(2)
-    wait_bytes(small_part, recv_sem.at[7])
-    own = pl.ds(pl.multiple_of(s * 16, 16), 16)
-    total = small[own, :].astype(F32)
-    for k in range(N_SAMPLE - 1):
-        total = total + small_part[k].astype(F32)
-    small_mid[...] = total.astype(BF16)
-    for k in range(1, N_TILE):
-        d = tile_peers[k - 1]
-        lanes = pl.ds(pl.multiple_of(d * 128, 128), 128)
-        send(small_mid.at[:, lanes], small_last.at[k - 1], send_sem.at[8], recv_sem.at[8], d, s)
-    for g in range(3):
-        add_second(g)
     wait_bytes(small_last, recv_sem.at[8])
     lanes = pl.ds(pl.multiple_of(t * 128, 128), 128)
     total = small_mid[:, lanes].astype(F32)
@@ -691,18 +745,32 @@
     block = small_sum.at[own, lanes]
     for d in tile_peers:
         send(block, block, send_sem.at[9], recv_sem.at[9], d, s)
-    for g in range(3):
-        add_third(g)
+    add_third(0)
+    add_third(1)
+    wait_bytes(tri_part, recv_sem.at[11])
+    total = tri[own, :].astype(F32)
+    for k in range(N_SAMPLE - 1):
+        total = total + tri_part[k].astype(F32)
+    tri_all[t] = total.astype(BF16)
+    for d in tile_peers:
+        send(tri_all.at[t], tri_all.at[t], send_sem.at[12], recv_sem.at[12], d, s)
+    add_third(2)
+    gather_second(0)
+    gather_second(1)
+    wait_bytes(tri_all.at[pl.ds(0, N_TILE - 1)], recv_sem.at[12])
+    tri_sum[own, :] = jnp.sum(tri_all[...].astype(F32), axis=0).astype(BF16)
+    for d in sample_peers:
+        send(tri_sum.at[own], tri_sum.at[own], send_sem.at[13], recv_sem.at[13], t, d)
+    gather_second(2)
     wait_bytes(small_last, recv_sem.at[9])
-    block = small_sum.at[own]
+    known = small_sum.at[own, pl.ds(0, SMALL)]
     for d in sample_peers:
-        send(block, block, send_sem.at[10], recv_sem.at[10], t, d)
-    for g in range(3):
-        gather_second(g)
+        send(known, known, send_sem.at[10], recv_sem.at[10], t, d)
     for g in range(3):
         gather_first(g)
         unpack(full, g, core)
     wait_bytes(small_part, recv_sem.at[10])
+    wait_bytes(tri_part, recv_sem.at[13])
     for g in range(3):
         wait_bytes(other.at[g], w_recv.at[g, 6])
         unpack(other, g, 1 - core)
@@ -718,6 +786,9 @@
     wait_bytes(small_last, send_sem.at[8])
     wait_bytes(small_last, send_sem.at[9])
     wait_bytes(small_part, send_sem.at[10])
+    wait_bytes(tri_part, send_sem.at[11])
+    wait_bytes(tri_all.at[pl.ds(0, N_TILE - 1)], send_sem.at[12])
+    wait_bytes(tri_part, send_sem.at[13])
     wait_bytes(theirs, w_send.at[0])
     wait_bytes(part1, w_send.at[1])
     wait_bytes(part2, w_send.at[2])
@@ -735,12 +806,14 @@
         backward_kernel,
         out_shape=[
             jax.ShapeDtypeStruct((512, 128), F32),
+            jax.ShapeDtypeStruct((512, 768), F32),
             jax.ShapeDtypeStruct((768, 3072), BF16),
             jax.ShapeDtypeStruct((768, 768), BF16),
-            jax.ShapeDtypeStruct((128, SMALL), BF16),
+            jax.ShapeDtypeStruct((128, N_TILE * 128), BF16),
+            jax.ShapeDtypeStruct((128, 512), BF16),
         ],
         in_specs=[vmem] * len(operands),
-        out_specs=[vmem] * 4,
+        out_specs=[vmem] * 6,
         scratch_shapes=[
             pltpu.VMEM((N_CHIP, N_SAMPLE) + block, BF16),
             pltpu.VMEM((N_CHIP - 1, N_SAMPLE) + block, BF16),
@@ -764,8 +837,11 @@
             pltpu.VMEM((N_SAMPLE, 2, 16, 512), BF16),
             pltpu.VMEM((128, SMALL), BF16),
             pltpu.VMEM((N_SAMPLE - 1, 16, SMALL), BF16),
-            pltpu.VMEM((16, SMALL), BF16),
+            pltpu.VMEM((16, N_TILE * 128), BF16),
             pltpu.VMEM((N_TILE - 1, 16, 128), BF16),
+            pltpu.VMEM((128, 512), BF16),
+            pltpu.VMEM((N_SAMPLE - 1, 16, 512), BF16),
+            pltpu.VMEM((N_TILE, 16, 512), BF16),
             pltpu.VMEM(chunk, BF16),
             pltpu.VMEM(chunk, BF16),
             pltpu.VMEM(chunk, BF16),
@@ -776,14 +852,17 @@
             pltpu.VMEM((3, 4, 48, WIDTH), BF16),
             pltpu.VMEM(chunk, BF16),
             pltpu.VMEM(chunk, BF16),
-            pltpu.SemaphoreType.DMA((11,)),
-            pltpu.SemaphoreType.DMA((11,)),
+            pltpu.VMEM((768, 512), F32),
+            pltpu.VMEM((256, 768), BF16),
+            pltpu.VMEM((128, 768), F32),
+            pltpu.SemaphoreType.DMA((14,)),
+            pltpu.SemaphoreType.DMA((14,)),
             pltpu.SemaphoreType.DMA((15,)),
             pltpu.SemaphoreType.DMA((7,)),
             pltpu.SemaphoreType.DMA((3, 7)),
         ],
         compiler_params=pltpu.CompilerParams(
-            collective_id=collective_id, has_side_effects=True, vmem_limit_bytes=56 << 20
+            collective_id=collective_id, has_side_effects=True, vmem_limit_bytes=60 << 20
         ),
     )(*operands)
 
@@ -870,20 +949,7 @@
     token_output_rows = token_state_rows + t_dot(gated_t, attention_output_weight).reshape(
         token_state_rows.shape
     )
-    normalized_hidden_gradient = lax.dot_general(
-        d_every_t, attention_input_weight, (((0,), (1,)), ((), ())), preferred_element_type=F32
-    ).reshape(token_state_rows.shape)
-    grad_tokens = token_output_cotangent.astype(jnp.float32) + norm_back(
-        normed_h, inverse_h, normalized_hidden_gradient, 2
-    )
-    cond_grad = (jnp.sum(grad_tokens, axis=0) / token_counts[:, None]).astype(BF16)
-    d_act = lax.dot_general(
-        one_hot, cond_grad, (((0,), (0,)), ((), ())), preferred_element_type=F32
-    ) * silu_slope(atom_pre)
-    grad_atom_w = lax.dot_general(
-        every_feat, d_act.astype(BF16), (((0,), (0,)), ((), ())), preferred_element_type=F32
-    )
-    grad_pair, in_sum, out_sum, small_sum = backward(
+    grad_pair, grad_tokens, in_sum, out_sum, small_sum, tri_sum = backward(
         1,
         bias_blocks,
         pair_rows,
@@ -897,20 +963,29 @@
         left_panel,
         right_panel,
         cot_pair.reshape(-1, hidden),
-        grad_atom_w.astype(BF16),
         hidden_t,
         d_every_t,
         gated_t,
         cot_rows,
+        attention_input_weight,
+        inverse_h.reshape(1, -1),
+        token_counts[:, None],
+        every_feat.reshape(8, -1, every_feat.shape[1]),
+        every_atom.reshape(8, 1, -1),
+        atom_w,
     )
+    grad_tokens = grad_tokens.reshape(tokens.shape)
     small_sum = small_sum.astype(F32)
-    at = 4 * hidden
+    at = token_width
     summed = (
-        small_sum[:, :at].reshape(hidden, 4, hidden).transpose(2, 1, 0).reshape(hidden, at),
+        tri_sum.astype(F32)
+        .reshape(hidden, 4, hidden)
+        .transpose(2, 1, 0)
+        .reshape(hidden, 4 * hidden),
         small_sum[:, at : at + hidden],
         small_sum[:, at + hidden : at + 2 * hidden],
-        small_sum[:head_count, at + 2 * hidden + token_width :][:, :hidden].T,
-        small_sum[:, at + 2 * hidden : at + 2 * hidden + token_width],
+        small_sum[:head_count, at + 2 * hidden : at + 3 * hidden].T,
+        small_sum[:, :at],
         in_sum.astype(F32),
         out_sum.astype(F32),
     )

time: 245 us -> 226 us (0.922)
  Pallas kernels: 187 us -> 176 us
  matrix products: 22 us -> 11.2 us
  local copies, waits for them, and re-layouts: 20.7 us -> 23.6 us
    dot_general x3 -> x0, matrix products: 14.7 us -> none  [the longest x1 6.44 us: shards(): lax.dot_general(every_feat, d_act.astype(BF16), (((0,), (0,)), ((), ())),...]
    pallas_call x1, Pallas kernels: 111 us -> 99.8 us  [backward(): pl.pallas_call(backward_kernel, out_shape=[jax.ShapeDtypeStruct((512, 128...]
    unnamed x64 -> x72, local copies, waits for them, and re-layouts: 12.3 us -> 18 us
    dot_general x1 -> x0, local copies, waits for them, and re-layouts: 4.92 us -> none  [shards(): lax.dot_general(d_every_t, attention_input_weight, (((0,), (1,)), ((), ()...]
where the time goes in v2:
time: 226 us
  Pallas kernels  176 us (78%)
  local copies, waits for them, and re-layouts  23.6 us (10%)
  other arithmetic  13.9 us (6%)
  matrix products  11.2 us (5%)
    pallas_call x1, Pallas kernels, backward(): pl.pallas_call(backward_kernel, out_shape=[jax.ShapeDtypeStruct((512, 128...  99.8 us
    pallas_call x1, Pallas kernels, pair_forward(): pl.pallas_call(pair_forward_kernel, out_shape=[jax.ShapeDtypeStruct(pair....  52.2 us
    pallas_call x1, Pallas kernels, attention(): pl.pallas_call(attention_kernel, grid=(width // block,), in_specs=[featur...  23.9 us
    unnamed x72, local copies, waits for them, and re-layouts  18 us
    convert_element_type x1, other arithmetic, shards(): in_sum.astype(F32)  7.47 us
    dot_general x5, matrix products, t_dot(): lax.dot_general(a, b, (((0,), (0,)), ((), ())), preferred_element_type=F32)  6.01 us

profile of v2, /device:TPU:1, one launch (start us, length us, event | category | flops | bytes accessed | tf_op | source)
XLA Modules:
  0.0 225.5 jit_solution(13781875096077781436)
XLA Ops:
  0.7 1.1 copy.40
  2.6 0.9 copy-done.8
  7.1 52.2 %shard_map.221 = (f32[512,128]{1,0:T(8,128)S(1)}, bf16[8,2,8,4,16,128]{5,4,3,2,1,0:T(8,128)(2,1)S(1)}, bf16[256,256]{1,0:T(8,128)(2,1)S(1)}, bf16[256,256]{1,0:T...) custom-call(bf16[512,128]{1,0:T(8,128)(2,1)S(1)} %bitcast.52, ...), custom_call_target="tpu_custom_call" | custom-call | tf_op jit(solution)/shard_map/pallas_call | solution.py:231
  60.1 0.8 copy-done.9
  63.2 4.4 %fusion.15 = f32[256,768]{1,0:T(8,128)} fusion(bf16[2048,128]{1,0:T(8,128)(2,1)} %bitcast.53, bf16[128,768]{1,0:T(8,128)(2,1)} %atom_w.1, s32[2048]{0:T(1024)S(1)} %bitcast.56, f32[256]{0:T(256)S(1)} %convert_reduce_fusion), kind=kOutput, calls=%fused_computation.24 | convolution fusion | flops 1216544768 | bytes 1516544 | tf_op jit(solution)/shard_map/dot_general | solution.py:927
  67.6 1.7 fusion.6
  70.1 2.7 %divide_bitcast_fusion.gate = f32[768,512]{1,0:T(8,128)S(1)} fusion(bf16[512,768]{1,0:T(8,128)(2,1)S(1)} %bitcast.63, bf16[768,3072]{1,0:T(8,128)(2,1)} %in_w.1), kind=kOutput, calls=%fused_computation.6 | convolution fusion | flops 605159424 | bytes 3538944 | tf_op jit(solution)/shard_map/dot_general | solution.py:40
  72.9 0.8 fusion.7.q
  73.7 0.8 fusion.8.k
  74.6 0.8 fusion.9.v
  75.7 0.8 fusion.19.up
  76.5 23.9 %shard_map.222 = (bf16[768,512]{1,0:T(8,128)(2,1)S(1)}, bf16[4,768,512]{2,1,0:T(8,128)(2,1)S(1)}, bf16[8,2,8,4,16,128]{5,4,3,2,1,0:T(8,128)(2,1)S(1)}) custom-call(bf16[768,512]{1,0:T(8,128)(2,1)S(1)} %fusion.7.q, bf16[768,512]{1,0:T(8,128)(2,1)S(1)} %fusion.8.k, bf16[768,512]{1,0:T(8,128)(2,1)S(1)} %fusion.9.v, f32[768,512]{1,0:T(8,128)S(1)} %divide_bitcast_fusion.gate, ...), custom_call_target="tpu_custom_call" | custom-call | tf_op jit(solution)/shard_map/pallas_call | solution.py:328
  100.4 1.7 copy-done.1
  102.1 1.3 copy-done.2
  103.4 0.9 copy-done.6
  104.3 2.4 %copy.52 = bf16[512,768]{0,1:T(8,128)(2,1)} copy(bf16[512,768]{1,0:T(8,128)(2,1)} %bitcast.67) | data formatting | bytes 1572864 | tf_op jit(solution)/shard_map/reshape | solution.py:933
  107.3 0.8 copy.46.counts
  108.1 99.8 %shard_map.223 = (f32[512,128]{1,0:T(8,128)}, f32[512,768]{1,0:T(8,128)}, bf16[768,3072]{1,0:T(8,128)(2,1)}, bf16[768,768]{1,0:T(8,128)(2,1)}, bf16[128,2048]{1,0:T(8,128)(2,1)}, /*index=5*/bf16[128,512]{1,0:T(8,128)(2,1)}) custom-call(bf16[8,2,8,4,16,128]{5,4,3,2,1,0:T(8,128)(2,1)} %copy-done.2, bf16[512,128]{1,0:T(8,128)(2,1)} %bitcast.51, ...), custom_call_target="tpu_custom_call" | custom-call | tf_op jit(solution)/shard_map/pallas_call | solution.py:805
  207.9 7.5 %convert_element_type.56 = f32[768,3072]{1,0:T(8,128)} convert(bf16[768,3072]{1,0:T(8,128)(2,1)} %get-tuple-element.41) | non-fusion elementwise | flops 2359296 | bytes 14155776 | tf_op jit(solution)/shard_map/convert_element_type | solution.py:989
  215.4 1.6 convert_element_type.57
  218.8 0.8 slice.35
  220.3 0.8 fusion.20
  221.6 1.3 fusion.4
  224.4 1.1 copy.62
  (78 shorter events, 13.5 us)
Async XLA Ops:
  0.6 74.8 %copy-start = (bf16[768,768]{1,0:T(8,128)(2,1)S(1)}, bf16[768,768]{1,0:T(8,128)(2,1)}, u32[]{:S(2)}) copy-start(bf16[768,768]{1,0:T(8,128)(2,1)} %param.25) | copy-start | bytes 3538948
  1.8 65.8 %copy-start.3 = (bf16[128,512]{0,1:T(8,128)(2,1)}, bf16[128,512]{0,1:T(8,128)(2,1)S(1)}, u32[]{:S(2)}) copy-start(bf16[128,512]{0,1:T(8,128)(2,1)S(1)} %copy.40) | copy-start | bytes 393220
  2.6 65.0 %copy-start.17 = (f32[1,512]{1,0:T(1,128)}, f32[1,512]{1,0:T(1,128)S(1)}, u32[]{:S(2)}) copy-start(f32[1,512]{1,0:T(1,128)S(1)} %reshape.103.mask) | copy-start | bytes 6148
  2.6 0.9 copy-start.8
  60.0 0.9 copy-start.9
  62.9 4.7 %copy-start.15 = (s32[16,1,128]{2,1,0:T(1,128)}, s32[16,1,128]{2,1,0:T(1,128)S(1)}, u32[]{:S(2)}) copy-start(s32[16,1,128]{2,1,0:T(1,128)S(1)} %get-tuple-element.28) | copy-start | bytes 24580
  67.6 1.8 copy-start.20
  67.6 1.8 copy-start.22
  69.8 3.1 %slice-start = ((s8[4718592]{0:T(1024)(128)(4,1)}), s8[4194304]{0:T(1024)(128)(4,1)S(1)}, s32[]{:S(2)}) async-start(s8[4718592]{0:T(1024)(128)(4,1)} %bitcast.61), calls=%async_computation | async-start | bytes 8388608
  70.1 4.5 %copy-start.24 = (bf16[2,256,768]{2,1,0:T(8,128)(2,1)}, bf16[2,256,768]{2,1,0:T(8,128)(2,1)S(1)}, u32[]{:S(2)}) copy-start(bf16[2,256,768]{2,1,0:T(8,128)(2,1)S(1)} %multiply_convert_fusion.2) | copy-start | bytes 2359300
  70.1 2.8 %slice-start.1 = ((s8[4718592]{0:T(1024)(128)(4,1)}), s8[524288]{0:T(1024)(128)(4,1)S(1)}, s32[]{:S(2)}) async-start(s8[4718592]{0:T(1024)(128)(4,1)} %bitcast.61), calls=%async_computation.1 | async-start | bytes 1048576
  74.6 1.1 copy-start.28
  100.4 1.7 copy-start.1
  102.1 1.3 copy-start.2
  103.4 0.9 copy-start.6
  207.9 7.5 %copy-start.27 = (bf16[768,768]{1,0:T(8,128)(2,1)S(1)}, bf16[768,768]{1,0:T(8,128)(2,1)}, u32[]{:S(2)}) copy-start(bf16[768,768]{1,0:T(8,128)(2,1)} %get-tuple-element.42) | copy-start | bytes 3538948
  215.4 1.6 copy-start.25
  216.9 0.9 copy-start.30
  217.1 3.2 %copy-start.7 = (bf16[768,512]{1,0:T(8,128)(2,1)S(1)}, bf16[768,512]{1,0:T(8,128)(2,1)}, u32[]{:S(2)}) copy-start(bf16[768,512]{1,0:T(8,128)(2,1)} %copy-done.6) | copy-start | bytes 2359300
  220.3 1.1 copy-start.21
  220.3 1.4 copy-start.23
  221.6 1.3 copy-start.5
  221.6 2.0 copy-start.29
  221.6 2.7 %copy-start.26 = (f32[512,768]{1,0:T(8,128)S(1)}, f32[512,768]{1,0:T(8,128)}, u32[]{:S(2)}) copy-start(f32[512,768]{1,0:T(8,128)} %get-tuple-element.38) | copy-start | bytes 4718596
  (9 other events, 6.3 us)

commit v3 on v2

--- a/solution.py
+++ b/solution.py
@@ -43,6 +43,31 @@
 HEAD = 48
 GROUP = 4
 LANES = 32
+
+
+def fetching(kernel, count):
+    def run(*refs):
+        sources, rest, buffers, sem = refs[:count], refs[count : -count - 1], refs[-count - 1 : -1], refs[-1]
+        copies = [
+            pltpu.make_async_copy(source, buffer, sem.at[i])
+            for i, (source, buffer) in enumerate(zip(sources, buffers))
+        ]
+        for copy in copies:
+            copy.start()
+
+        def need(*which):
+            for i in which:
+                copies[i].wait()
+
+        kernel(need, *buffers, *rest)
+
+    return run
+
+
+def fetch_scratch(operands):
+    return [pltpu.VMEM(x.shape, x.dtype) for x in operands] + [
+        pltpu.SemaphoreType.DMA((len(operands),))
+    ]
 
 
 def place_lanes(parts, first):
@@ -94,15 +119,19 @@
     return 1.0 / (1.0 + jnp.exp(-values))
 
 
-def pair_forward_kernel(
+def forward_kernel(
+    need,
     pair,
+    in_w_t,
     mask,
-    in_w_t,
+    feats,
+    atoms,
     gate_w,
     out_w,
     bias_w_t,
-    feats,
-    atoms,
+    atom_w,
+    tokens,
+    in_w,
     pair_next,
     bias,
     left,
@@ -110,6 +139,14 @@
     product,
     every_feat,
     every_atom,
+    token_cond,
+    counts,
+    hidden_t,
+    inverse_h,
+    q,
+    k_out,
+    v,
+    gate,
     x1,
     mid,
     mid_rows,
@@ -136,7 +173,41 @@
     for d in tile_peers:
         pl.semaphore_signal(barrier, inc=1, device_id=(d, s), device_id_type=MESH)
 
+    def token_sums():
+        token_cond[...] = jnp.zeros_like(token_cond)
+        counts[...] = jnp.zeros_like(counts)
+
+        @pl.loop(0, N_TILE)
+        def _(a):
+            pre = dot(every_feat[a], atom_w[...])
+            token = lax.broadcasted_iota(jnp.int32, (256, 128), 0)
+            one_hot = jnp.where(token == every_atom[a], 1.0, 0.0)
+            token_cond[...] += dot(one_hot.astype(BF16), (pre * sigmoid(pre)).astype(BF16))
+            counts[...] += jnp.sum(one_hot, axis=1, keepdims=True)
+
+        token_cond[...] = token_cond[...] / counts[...]
+
+    def token_norm():
+        @pl.loop(0, 4)
+        def _(a):
+            lanes = pl.ds(pl.multiple_of(a * 128, 128), 128)
+            of_token = pl.ds(pl.multiple_of(lax.rem(a, 2) * 128, 128), 128)
+            state = tokens[lanes, :].astype(F32) + token_cond[of_token, :]
+            normed, inverse = norm_rows(state.T, 0)
+            hidden_t[:, lanes] = normed.astype(BF16)
+            inverse_h[:, lanes] = inverse
+
+    def token_project(block, out):
+        @pl.loop(0, 3)
+        def _(a):
+            rows = pl.ds(pl.multiple_of(a * 256, 256), 256)
+            columns = pl.ds(pl.multiple_of(block * 768 + a * 256, 256), 256)
+            result = t_dot(in_w[:, columns], hidden_t[...])
+            out[rows, :] = (sigmoid(result) if block == 1 else result).astype(out.dtype)
+
+    need(0)
     normed_z = norm_rows(pair[...].astype(F32), 1)[0].astype(BF16)
+    need(1, 2)
 
     def project(block):
         return dot_t(in_w_t[pl.ds(block * 128, 128), :], normed_z)
@@ -145,6 +216,7 @@
         value = (sigmoid(project(2 * side)) * project(2 * side + 1) * mask[...]).astype(BF16)
         for d in range(N_SAMPLE):
             x1[d, side] = value[d * 16 : d * 16 + 16]
+    need(3, 4)
     pl.semaphore_wait(barrier, N_SAMPLE + N_TILE - 2)
     for d in sample_peers:
         send(x1.at[d], mid.at[s], send_sem.at[0], recv_sem.at[0], t, d)
@@ -154,6 +226,7 @@
     every_feat[t] = feats[...]
     every_atom[t] = atoms[...]
     mid[s] = x1[s]
+    need(5, 6, 7, 8, 9, 10)
     tri_gate = sigmoid(dot(normed_z, gate_w[...]))
     wait_bytes(mid.at[pl.ds(0, N_SAMPLE - 1)], recv_sem.at[0])
     split_lanes(mid[...].reshape(256, 512).astype(F32), mid_rows)
@@ -165,6 +238,9 @@
     for d in tile_peers:
         send(x2.at[d], arrived.at[t], send_sem.at[3], recv_sem.at[3], d, s)
     arrived[t] = x2[t]
+    wait_bytes(every_feat.at[pl.ds(0, N_TILE - 1)], recv_sem.at[1])
+    wait_bytes(every_atom.at[pl.ds(0, N_TILE - 1)], recv_sem.at[2])
+    token_sums()
     wait_bytes(arrived.at[pl.ds(0, N_TILE - 1)], recv_sem.at[3])
     split_lanes(arrived[...].reshape(256, 512).astype(F32), arrived_rows)
     panel_of(arrived_rows, 0, 16, panel)
@@ -175,6 +251,7 @@
     for d in tile_peers:
         send(x3.at[d], back.at[t], send_sem.at[4], recv_sem.at[4], d, s)
     back[t] = x3[t]
+    token_norm()
     wait_bytes(back.at[pl.ds(0, N_TILE - 1)], recv_sem.at[4])
     split_lanes(back[...].reshape(256, 256).astype(F32), back_rows)
 
@@ -185,6 +262,7 @@
     for d in sample_peers:
         send(x4.at[d], product.at[s], send_sem.at[5], recv_sem.at[5], t, d)
     product[s] = x4[s]
+    token_project(0, q)
     wait_bytes(product.at[pl.ds(0, N_SAMPLE - 1)], recv_sem.at[5])
     normed_p = norm_rows(product[...].reshape(128, 512).astype(F32), 0)[0].astype(BF16)
     linear = t_dot(normed_p, out_w[...])
@@ -202,19 +280,20 @@
     own = bias.at[m, c, s]
     for d in sample_peers:
         send(own, own, send_sem.at[6], recv_sem.at[6], t, d)
+    token_project(2, k_out)
     wait_bytes(bias.at[m, c, pl.ds(0, N_SAMPLE - 1)], recv_sem.at[6])
     block = bias.at[m, c]
     other = m * 2 + 1 - c
     for k in range(1, N_CHIP):
         send(block, block, send_sem.at[7], recv_sem.at[7 + k], lax.rem(m + k, N_CHIP) * 2 + c, s)
     send(block, block, send_sem.at[8], recv_sem.at[7], other, s)
+    token_project(3, v)
+    token_project(1, gate)
     for k in range(1, N_CHIP):
         came = bias.at[lax.rem(m + N_CHIP - k, N_CHIP), c]
         wait_bytes(came, recv_sem.at[7 + k])
         send(came, came, send_sem.at[8], recv_sem.at[7], other, s)
     wait_bytes(bias.at[:, 0], recv_sem.at[7])
-    wait_bytes(every_feat.at[pl.ds(0, N_TILE - 1)], recv_sem.at[1])
-    wait_bytes(every_atom.at[pl.ds(0, N_TILE - 1)], recv_sem.at[2])
     wait_bytes(mid.at[pl.ds(0, N_SAMPLE - 1)], send_sem.at[0])
     wait_bytes(every_feat.at[pl.ds(0, N_TILE - 1)], send_sem.at[1])
     wait_bytes(every_atom.at[pl.ds(0, N_TILE - 1)], send_sem.at[2])
@@ -226,21 +305,30 @@
     wait_bytes(bias.at[:, 0], send_sem.at[8])
 
 
-def pair_forward(pair, mask, in_w_t, gate_w, out_w, bias_w_t, feats, atoms, collective_id):
+def forward(collective_id, *operands):
     vmem = pl.BlockSpec(memory_space=pltpu.VMEM)
+    feats, atoms = operands[3:5]
     return pl.pallas_call(
-        pair_forward_kernel,
+        fetching(forward_kernel, len(operands)),
         out_shape=[
-            jax.ShapeDtypeStruct(pair.shape, F32),
+            jax.ShapeDtypeStruct((512, 128), F32),
             jax.ShapeDtypeStruct((N_CHIP, 2, N_SAMPLE, 4, 16, 128), BF16),
             jax.ShapeDtypeStruct((256, 256), BF16),
             jax.ShapeDtypeStruct((256, 256), BF16),
             jax.ShapeDtypeStruct((N_SAMPLE, 16, 512), BF16),
             jax.ShapeDtypeStruct((N_TILE,) + feats.shape, feats.dtype),
             jax.ShapeDtypeStruct((N_TILE,) + atoms.shape, atoms.dtype),
+            jax.ShapeDtypeStruct((256, 768), F32),
+            jax.ShapeDtypeStruct((256, 1), F32),
+            jax.ShapeDtypeStruct((768, 512), BF16),
+            jax.ShapeDtypeStruct((1, 512), F32),
+            jax.ShapeDtypeStruct((768, 512), BF16),
+            jax.ShapeDtypeStruct((768, 512), BF16),
+            jax.ShapeDtypeStruct((768, 512), BF16),
+            jax.ShapeDtypeStruct((768, 512), F32),
         ],
-        in_specs=[vmem] * 8,
-        out_specs=[vmem] * 7,
+        in_specs=[pl.BlockSpec(memory_space=pl.ANY)] * len(operands),
+        out_specs=[vmem] * 15,
         scratch_shapes=[
             pltpu.VMEM((N_SAMPLE, 2, 16, 512), BF16),
             pltpu.VMEM((N_SAMPLE, 2, 16, 512), BF16),
@@ -257,11 +345,12 @@
             pltpu.VMEM((4, 16, 128), F32),
             pltpu.SemaphoreType.DMA((9,)),
             pltpu.SemaphoreType.DMA((15,)),
-        ],
+        ]
+        + fetch_scratch(operands),
         compiler_params=pltpu.CompilerParams(
             collective_id=collective_id, has_side_effects=True, vmem_limit_bytes=40 << 20
         ),
-    )(pair, mask, in_w_t, gate_w, out_w, bias_w_t, feats, atoms)
+    )(*operands)
 
 
 def attention_kernel(q, k, v, gate, up, bias, gated, d_every, d_bias, bias_rows, bias_total):
@@ -355,10 +444,16 @@
 
 
 def backward_kernel(
+    need,
     d_bias,
+    right_in,
+    in_w,
+    left_in,
+    left_out,
+    right_out,
     pair,
+    in_w_t,
     mask,
-    in_w_t,
     gate_w,
     out_w,
     bias_w_t,
@@ -367,11 +462,6 @@
     left,
     right,
     cot_pair,
-    left_in,
-    right_in,
-    left_out,
-    right_out,
-    in_w,
     inverse_h,
     counts,
     feats,
@@ -587,13 +677,17 @@
 
         small[:, pl.ds(0, 768)] = atom_grad[...].astype(BF16)
 
+    need(1, 2)
     token_product()
+    need(0)
     pl.semaphore_wait(barrier, N_SAMPLE + N_TILE - 1)
     for k in range(1, N_CHIP + 1):
         d = lax.rem(m + k, N_CHIP)
         send(d_bias.at[d, 1 - core], pair_sum.at[d], send_sem.at[0], chip_sem.at[k - 1], partner_t, s)
+    need(3, 4, 5)
     form_theirs(0)
 
+    need(*range(6, 22))
     keep[0], inverse_z = norm_rows(pair[...].astype(F32), 1)
     normed_z = keep[0].astype(BF16)
 
@@ -803,7 +897,7 @@
     chunk = (3, 4, ROWS, WIDTH)
     block = (4, 16, 128)
     return pl.pallas_call(
-        backward_kernel,
+        fetching(backward_kernel, len(operands)),
         out_shape=[
             jax.ShapeDtypeStruct((512, 128), F32),
             jax.ShapeDtypeStruct((512, 768), F32),
@@ -812,7 +906,7 @@
             jax.ShapeDtypeStruct((128, N_TILE * 128), BF16),
             jax.ShapeDtypeStruct((128, 512), BF16),
         ],
-        in_specs=[vmem] * len(operands),
+        in_specs=[pl.BlockSpec(memory_space=pl.ANY)] * len(operands),
         out_specs=[vmem] * 6,
         scratch_shapes=[
             pltpu.VMEM((N_CHIP, N_SAMPLE) + block, BF16),
@@ -860,28 +954,32 @@
             pltpu.SemaphoreType.DMA((15,)),
             pltpu.SemaphoreType.DMA((7,)),
             pltpu.SemaphoreType.DMA((3, 7)),
-        ],
+        ]
+        + fetch_scratch(operands),
         compiler_params=pltpu.CompilerParams(
             collective_id=collective_id, has_side_effects=True, vmem_limit_bytes=60 << 20
         ),
     )(*operands)
 
 
-def norm_parts(values, axis):
-    centered = values - jnp.mean(values, axis=axis, keepdims=True)
-    inverse = lax.rsqrt(jnp.mean(centered * centered, axis=axis, keepdims=True) + EPSILON)
-    return (centered * inverse, inverse)
-
-
-def norm_back(normed, inverse, incoming_gradient, axis):
-    first_mean = jnp.mean(incoming_gradient, axis=axis, keepdims=True)
-    second_mean = jnp.mean(incoming_gradient * normed, axis=axis, keepdims=True)
-    return (incoming_gradient - first_mean - normed * second_mean) * inverse
-
-
-def silu_slope(values):
-    sigmoid_part = jax.nn.sigmoid(values)
-    return sigmoid_part * (1.0 + values * (1.0 - sigmoid_part))
+def widen_kernel(wide, narrow, wide_out, narrow_out):
+    wide_out[...] = wide[...].astype(F32)
+    narrow_out[...] = narrow[...].astype(F32)
+
+
+def widen(wide, narrow):
+    steps = 6
+    specs = [
+        pl.BlockSpec((x.shape[0] // steps, x.shape[1]), lambda i: (i, 0)) for x in (wide, narrow)
+    ]
+    return pl.pallas_call(
+        widen_kernel,
+        grid=(steps,),
+        in_specs=specs,
+        out_specs=specs,
+        out_shape=[jax.ShapeDtypeStruct(x.shape, F32) for x in (wide, narrow)],
+        compiler_params=pltpu.CompilerParams(vmem_limit_bytes=32 << 20),
+    )(wide, narrow)
 
 
 def shards(
@@ -907,54 +1005,63 @@
     pair_rows = pair.reshape(-1, hidden)
     mask_row = pair_mask.astype(F32).reshape(1, -1)
     in_w_t, bias_w_t = tri_in_w.T, bias_w.T
-    following, bias_all, left_panel, right_panel, product, every_feat, every_atom = pair_forward(
+    token_rows = tokens.reshape(-1, token_width)
+    cot_rows = token_output_cotangent.reshape(-1, token_width)
+    (
+        following,
+        bias_all,
+        left_panel,
+        right_panel,
+        product,
+        every_feat,
+        every_atom,
+        token_cond,
+        token_counts,
+        hidden_t,
+        inverse_h,
+        queries,
+        keys_all,
+        values_all,
+        gate_values,
+    ) = forward(
+        0,
         pair_rows,
+        in_w_t,
         mask_row,
-        in_w_t,
+        atom_feats,
+        atom_to_token[None],
         tri_gate_w,
         tri_out_w,
         bias_w_t,
-        atom_feats,
-        atom_to_token[None],
-        0,
+        atom_w,
+        token_rows,
+        attention_input_weight,
     )
-    every_feat = every_feat.reshape(-1, atom_feats.shape[1])
-    every_atom = every_atom.reshape(-1)
-    atom_pre = jnp.dot(every_feat, atom_w, preferred_element_type=jnp.float32)
-    atom_act = jax.nn.silu(atom_pre).astype(BF16)
-    token_ids = jnp.arange(total_tokens, dtype=jnp.int32)
-    one_hot = (token_ids[:, None] == every_atom[None, :]).astype(BF16)
-    token_sums = jnp.dot(one_hot, atom_act, preferred_element_type=F32)
-    token_counts = jnp.sum(one_hot.astype(F32), axis=1)
-    token_cond = token_sums / token_counts[:, None]
-    token_state_rows = tokens.astype(jnp.float32) + token_cond[None]
-    normed_h, inverse_h = norm_parts(token_state_rows, 2)
-    normalized_hidden_bfloat = normed_h.astype(jnp.bfloat16)
-    hidden_t = normalized_hidden_bfloat.reshape(-1, token_width).T
-    cot_rows = token_output_cotangent.reshape(-1, token_width)
-
-    def project(block):
-        weight = attention_input_weight[:, block * token_width : (block + 1) * token_width]
-        return t_dot(weight, hidden_t)
-
     gated_t, d_every_t, bias_blocks = attention(
-        project(0).astype(BF16),
-        project(2).astype(BF16),
-        project(3).astype(BF16),
-        jax.nn.sigmoid(project(1)),
+        queries,
+        keys_all,
+        values_all,
+        gate_values,
         dot_t(attention_output_weight, cot_rows),
         bias_all,
     )
     d_every_t = d_every_t.reshape(4 * token_width, -1)
-    token_output_rows = token_state_rows + t_dot(gated_t, attention_output_weight).reshape(
-        token_state_rows.shape
+    token_output_rows = (
+        tokens.astype(F32)
+        + token_cond[None]
+        + t_dot(gated_t, attention_output_weight).reshape(tokens.shape)
     )
     grad_pair, grad_tokens, in_sum, out_sum, small_sum, tri_sum = backward(
         1,
         bias_blocks,
+        d_every_t,
+        attention_input_weight,
+        hidden_t,
+        gated_t,
+        cot_rows,
         pair_rows,
+        in_w_t,
         mask_row,
-        in_w_t,
         tri_gate_w,
         tri_out_w,
         bias_w_t,
@@ -963,15 +1070,10 @@
         left_panel,
         right_panel,
         cot_pair.reshape(-1, hidden),
-        hidden_t,
-        d_every_t,
-        gated_t,
-        cot_rows,
-        attention_input_weight,
-        inverse_h.reshape(1, -1),
-        token_counts[:, None],
-        every_feat.reshape(8, -1, every_feat.shape[1]),
-        every_atom.reshape(8, 1, -1),
+        inverse_h,
+        token_counts,
+        every_feat,
+        every_atom,
         atom_w,
     )
     grad_tokens = grad_tokens.reshape(tokens.shape)
@@ -986,8 +1088,7 @@
         small_sum[:, at + hidden : at + 2 * hidden],
         small_sum[:head_count, at + 2 * hidden : at + 3 * hidden].T,
         small_sum[:, :at],
-        in_sum.astype(F32),
-        out_sum.astype(F32),
+        *widen(in_sum, out_sum),
     )
     pair_next, grad_pair = following.reshape(pair.shape), grad_pair.reshape(pair.shape)
     return (pair_next, token_output_rows, grad_pair, grad_tokens) + summed

time: 226 us -> 221 us (0.978)
  Pallas kernels: 176 us -> 188 us
  other arithmetic: 13.9 us -> 2.2 us
  matrix products: 11.2 us -> 1.61 us
  local copies, waits for them, and re-layouts: 23.6 us -> 27.2 us
    pallas_call x2 -> x3, Pallas kernels: 152 us -> 165 us  [the longest x1 102 us: backward(): pl.pallas_call(fetching(backward_kernel, len(operands)), out_shape=[jax.S...]
    convert_element_type x3 -> x0, other arithmetic: 9.32 us -> none  [the longest x1 7.47 us: shards(): in_sum.astype(F32)]
    unnamed x72 -> x69, local copies, waits for them, and re-layouts: 18 us -> 23.2 us
    dot_general x5 -> x1, matrix products: 6.01 us -> 0.81 us  [t_dot(): lax.dot_general(a, b, (((0,), (0,)), ((), ())), preferred_element_type=F32)]
    dot_general x1 -> x0, matrix products: 4.4 us -> none  [shards(): token_sums = jnp.dot(one_hot, atom_act, preferred_element_type=F32)]
    reduce_sum x3 -> x0, other arithmetic: 2.39 us -> none  [the longest x1 1.72 us: norm_parts(): centered = values - jnp.mean(values, axis=axis, keepdims=True)]
    reshape x1 -> x0, local copies, waits for them, and re-layouts: 2.38 us -> none  [shards(): hidden_t = normalized_hidden_bfloat.reshape(-1, token_width).T]
where the time goes in v3:
time: 221 us; the launch traced here: 220 us
  Pallas kernels  188 us (85%)
  local copies, waits for them, and re-layouts  27.2 us (12%)
    pallas_call x1, Pallas kernels, backward(): pl.pallas_call(fetching(backward_kernel, len(operands)), out_shape=[jax.S...  102 us
    pallas_call x1, Pallas kernels, forward(): pl.pallas_call(fetching(forward_kernel, len(operands)), out_shape=[jax.Sh...  58 us
    pallas_call x1, Pallas kernels, attention(): pl.pallas_call(attention_kernel, grid=(width // block,), in_specs=[featur...  23.7 us
    unnamed x69, local copies, waits for them, and re-layouts  23.2 us
    pallas_call x1, Pallas kernels, widen(): pl.pallas_call(widen_kernel, grid=(steps,), in_specs=specs, out_specs=spe...  4.66 us

profile of v3, /device:TPU:1, one launch (start us, length us, event | category | flops | bytes accessed | tf_op | source)
XLA Modules:
  0.0 220.3 jit_solution(6466890863274429767)
XLA Ops:
  0.7 1.1 copy.25
  2.6 1.1 copy-done.2
  3.7 0.9 copy-done.10
  4.7 0.9 copy-done.14
  5.6 0.8 copy-done.20
  6.3 0.8 copy-done.21
  9.2 58.0 %shard_map.221 = (f32[512,128]{1,0:T(8,128)S(1)}, bf16[8,2,8,4,16,128]{5,4,3,2,1,0:T(8,128)(2,1)S(1)}, bf16[256,256]{1,0:T(8,128)(2,1)S(1)}, bf16[256,256]{1,0:T...) custom-call(bf16[512,128]{1,0:T(8,128)(2,1)S(1)} %bitcast.29, ...), custom_call_target="tpu_custom_call" | custom-call | tf_op jit(solution)/shard_map/pallas_call | solution.py:311
  67.9 0.9 copy-done.13
  70.7 0.8 fusion.1.up
  71.6 23.7 %shard_map.222 = (bf16[768,512]{1,0:T(8,128)(2,1)S(1)}, bf16[4,768,512]{2,1,0:T(8,128)(2,1)S(1)}, bf16[8,2,8,4,16,128]{5,4,3,2,1,0:T(8,128)(2,1)S(1)}) custom-call(bf16[768,512]{1,0:T(8,128)(2,1)S(1)} %get-tuple-element.39.q, bf16[768,512]{1,0:T(8,128)(2,1)S(1)} %get-tuple-element.40.k, bf16[768,512]{1,0:T(8,128)(2,1)S(1)} %get-tuple-element.41.v, ...), custom_call_target="tpu_custom_call" | custom-call | tf_op jit(solution)/shard_map/pallas_call | solution.py:417
  95.3 1.7 copy-done.4
  97.0 1.3 copy-done.5
  98.3 0.9 copy-done.11
  99.2 102.1 %shard_map.223 = (f32[512,128]{1,0:T(8,128)}, f32[512,768]{1,0:T(8,128)}, bf16[768,3072]{1,0:T(8,128)(2,1)}, bf16[768,768]{1,0:T(8,128)(2,1)}, bf16[128,2048]{1,0:T(8,128)(2,1)}, /*index=5*/bf16[128,512]{1,0:T(8,128)(2,1)}) custom-call(bf16[8,2,8,4,16,128]{5,4,3,2,1,0:T(8,128)(2,1)} %copy-done.5, bf16[3072,512]{1,0:T(8,128)(2,1)} %bitcast.24, ...), custom_call_target="tpu_custom_call" | custom-call | tf_op jit(solution)/shard_map/pallas_call | solution.py:899
  201.3 2.3 %copy-done.1 = bf16[768,3072]{1,0:T(8,128)(2,1)S(1)} copy-done((bf16[768,3072]{1,0:T(8,128)(2,1)S(1)}, bf16[768,3072]{1,0:T(8,128)(2,1)}, u32[]{:S(2)}) %copy-start.1) | copy-done | bytes 4718616
  203.6 1.3 copy-done.7
  204.9 4.7 %shard_map.224 = (f32[768,3072]{1,0:T(8,128)}, f32[768,768]{1,0:T(8,128)}) custom-call(bf16[768,3072]{1,0:T(8,128)(2,1)S(1)} %copy-done.1, bf16[768,768]{1,0:T(8,128)(2,1)S(1)} %copy-done.7), custom_call_target="tpu_custom_call" | custom-call | tf_op jit(solution)/shard_map/pallas_call | solution.py:975
  210.2 1.0 reshape.80
  211.2 0.8 copy.26
  212.1 1.7 copy.29
  213.7 0.8 slice.19
  215.2 0.8 fusion.2
  216.3 1.4 add_add_fusion
  219.1 1.1 copy.35
  (60 shorter events, 8.7 us)
Async XLA Ops:
  0.6 70.1 %copy-start = (bf16[768,768]{1,0:T(8,128)(2,1)S(1)}, bf16[768,768]{1,0:T(8,128)(2,1)}, u32[]{:S(2)}) copy-start(bf16[768,768]{1,0:T(8,128)(2,1)} %param.25) | copy-start | bytes 3538948
  1.8 65.4 %copy-start.6 = (bf16[128,512]{0,1:T(8,128)(2,1)}, bf16[128,512]{0,1:T(8,128)(2,1)S(1)}, u32[]{:S(2)}) copy-start(bf16[128,512]{0,1:T(8,128)(2,1)S(1)} %copy.25) | copy-start | bytes 393220
  2.6 64.6 %copy-start.23 = (f32[1,512]{1,0:T(1,128)}, f32[1,512]{1,0:T(1,128)S(1)}, u32[]{:S(2)}) copy-start(f32[1,512]{1,0:T(1,128)S(1)} %reshape.64.refs_2_.refs_8_) | copy-start | bytes 6148
  2.6 1.1 copy-start.2
  3.7 0.9 copy-start.10
  4.7 0.9 copy-start.14
  5.6 0.8 copy-start.20
  9.2 61.5 %copy-start.30 = (bf16[2,256,768]{2,1,0:T(8,128)(2,1)S(1)}, bf16[2,256,768]{2,1,0:T(8,128)(2,1)}, u32[]{:S(2)}) copy-start(bf16[2,256,768]{2,1,0:T(8,128)(2,1)} %param.27) | copy-start | bytes 2359300
  67.9 0.9 copy-start.13
  70.7 0.8 copy-start.15
  70.7 0.9 copy-start.17
  70.7 0.9 copy-start.18
  70.7 0.9 copy-start.25
  95.3 1.7 copy-start.4
  97.0 1.3 copy-start.5
  98.3 0.9 copy-start.11
  201.3 2.3 %copy-start.1 = (bf16[768,3072]{1,0:T(8,128)(2,1)S(1)}, bf16[768,3072]{1,0:T(8,128)(2,1)}, u32[]{:S(2)}) copy-start(bf16[768,3072]{1,0:T(8,128)(2,1)} %get-tuple-element.59.wide) | copy-start | bytes 14155780
  203.6 1.3 copy-start.7
  204.9 4.7 %copy-start.28 = (bf16[128,2048]{1,0:T(8,128)(2,1)S(1)}, bf16[128,2048]{1,0:T(8,128)(2,1)}, u32[]{:S(2)}) copy-start(bf16[128,2048]{1,0:T(8,128)(2,1)} %get-tuple-element.58) | copy-start | bytes 1572868
  209.6 5.6 %copy-start.12 = (bf16[768,512]{1,0:T(8,128)(2,1)S(1)}, bf16[768,512]{1,0:T(8,128)(2,1)}, u32[]{:S(2)}) copy-start(bf16[768,512]{1,0:T(8,128)(2,1)} %copy-done.11) | copy-start | bytes 2359300
  215.2 1.1 copy-start.3
  216.3 1.4 copy-start.9
  216.3 2.1 copy-start.31
  216.3 2.8 %copy-start.29 = (f32[512,768]{1,0:T(8,128)S(1)}, f32[512,768]{1,0:T(8,128)}, u32[]{:S(2)}) copy-start(f32[512,768]{1,0:T(8,128)} %get-tuple-element.56) | copy-start | bytes 4718596
  (8 other events, 5.4 us)

commit v4 on v3

--- a/solution.py
+++ b/solution.py
@@ -117,6 +117,61 @@
 
 def sigmoid(values):
     return 1.0 / (1.0 + jnp.exp(-values))
+
+
+def attend(group, q, k, v, gate, up, bias, gated, d_every, d_bias, bias_rows, bias_total):
+    tokens = bias_rows.shape[1]
+    scale = 1.0 / math.sqrt(HEAD)
+    group_of = lax.broadcasted_iota(jnp.int32, (tokens, 128), 1) // LANES
+
+    for half in range(2):
+        parts = [
+            bias[:, :, half * 4 + i, group].reshape(tokens, 128).astype(F32) for i in range(4)
+        ]
+        for h in range(GROUP):
+            row = parts[0] if h == 0 else pltpu.roll(parts[0], (-h) % 4 * LANES, 1)
+            for i in range(1, 4):
+                shift = (i - h) % 4 * LANES
+                moved = pltpu.roll(parts[i], shift, 1) if shift else parts[i]
+                row = jnp.where(group_of == i, moved, row)
+            bias_rows[h, :, pl.ds(half * 128, 128)] = row
+
+    @pl.loop(0, GROUP)
+    def _(h):
+        rows = pl.ds(pl.multiple_of(group * GROUP * HEAD + h * HEAD, 16), HEAD)
+        for sample in range(2):
+            columns = pl.ds(sample * tokens, tokens)
+            qh, kh, vh = q[rows, columns], k[rows, columns], v[rows, columns]
+            scores = t_dot(qh, kh) * scale + bias_rows[h]
+            weights = jnp.exp(scores - jnp.max(scores, axis=1, keepdims=True))
+            probs = weights * (1.0 / jnp.sum(weights, axis=1, keepdims=True))
+            probs_b = probs.astype(BF16)
+            attended = dot_t(vh, probs_b)
+            gate_h, up_h = gate[rows, columns], up[rows, columns]
+            gated[rows, columns] = (gate_h * attended).astype(BF16)
+            d_att = (up_h * gate_h).astype(BF16)
+            d_every[1, rows, columns] = (up_h * attended * gate_h * (1.0 - gate_h)).astype(BF16)
+            d_probs = t_dot(d_att, vh)
+            inner = jnp.sum(probs * d_probs, axis=1, keepdims=True)
+            d_scores = probs * (d_probs - inner)
+            d_scores_b = d_scores.astype(BF16)
+            d_every[0, rows, columns] = (dot_t(kh, d_scores_b) * scale).astype(BF16)
+            d_every[2, rows, columns] = (dot(qh, d_scores_b) * scale).astype(BF16)
+            d_every[3, rows, columns] = dot(d_att, probs_b).astype(BF16)
+            if sample == 0:
+                bias_total[h] = d_scores
+            else:
+                bias_total[h] = bias_total[h] + d_scores
+
+    for half in range(2):
+        parts = [bias_total[h, :, pl.ds(half * 128, 128)] for h in range(GROUP)]
+        for i in range(4):
+            row = parts[0] if i == 0 else pltpu.roll(parts[0], (-i) % 4 * LANES, 1)
+            for h in range(1, GROUP):
+                shift = (h - i) % 4 * LANES
+                moved = pltpu.roll(parts[h], shift, 1) if shift else parts[h]
+                row = jnp.where(group_of == h, moved, row)
+            d_bias[:, :, half * 4 + i, group] = row.astype(BF16).reshape(N_CHIP, 2, 16, 128)
 
 
 def forward_kernel(
@@ -132,8 +187,8 @@
     atom_w,
     tokens,
     in_w,
+    up,
     pair_next,
-    bias,
     left,
     right,
     product,
@@ -143,10 +198,9 @@
     counts,
     hidden_t,
     inverse_h,
-    q,
-    k_out,
-    v,
-    gate,
+    gated,
+    d_every,
+    bias_block,
     x1,
     mid,
     mid_rows,
@@ -160,8 +214,23 @@
     x4,
     packed,
     mine,
+    bias,
+    q,
+    keys,
+    v,
+    gate,
+    bias_rows,
+    bias_total,
+    d_bias,
+    pair_sum,
+    by_chip,
+    by_sample,
     send_sem,
     recv_sem,
+    chip_in,
+    core_in,
+    core_back,
+    chip_back,
 ):
     t, s = lax.axis_index("tile"), lax.axis_index("sample")
     m, c = t // 2, lax.rem(t, 2)
@@ -226,7 +295,7 @@
     every_feat[t] = feats[...]
     every_atom[t] = atoms[...]
     mid[s] = x1[s]
-    need(5, 6, 7, 8, 9, 10)
+    need(5, 6, 7, 8, 9, 10, 11)
     tri_gate = sigmoid(dot(normed_z, gate_w[...]))
     wait_bytes(mid.at[pl.ds(0, N_SAMPLE - 1)], recv_sem.at[0])
     split_lanes(mid[...].reshape(256, 512).astype(F32), mid_rows)
@@ -280,20 +349,74 @@
     own = bias.at[m, c, s]
     for d in sample_peers:
         send(own, own, send_sem.at[6], recv_sem.at[6], t, d)
-    token_project(2, k_out)
+    token_project(2, keys)
     wait_bytes(bias.at[m, c, pl.ds(0, N_SAMPLE - 1)], recv_sem.at[6])
-    block = bias.at[m, c]
     other = m * 2 + 1 - c
-    for k in range(1, N_CHIP):
-        send(block, block, send_sem.at[7], recv_sem.at[7 + k], lax.rem(m + k, N_CHIP) * 2 + c, s)
-    send(block, block, send_sem.at[8], recv_sem.at[7], other, s)
+    for g in range(4):
+        for k in range(1, N_CHIP):
+            d = lax.rem(m + k, N_CHIP) * 2 + c
+            send(bias.at[m, c, :, g], bias.at[m, c, :, g], send_sem.at[7], chip_in.at[g], d, s)
     token_project(3, v)
     token_project(1, gate)
-    for k in range(1, N_CHIP):
-        came = bias.at[lax.rem(m + N_CHIP - k, N_CHIP), c]
-        wait_bytes(came, recv_sem.at[7 + k])
-        send(came, came, send_sem.at[8], recv_sem.at[7], other, s)
-    wait_bytes(bias.at[:, 0], recv_sem.at[7])
+
+    def pass_bias(g):
+        wait_bytes(bias.at[pl.ds(0, N_CHIP - 1), 0, :, g], chip_in.at[g])
+        send(bias.at[:, c, :, g], bias.at[:, c, :, g], send_sem.at[8], core_in.at[g], other, s)
+
+    def add_cores(g):
+        wait_bytes(pair_sum.at[:, :, g], core_back.at[g])
+        for k in range(1, N_CHIP + 1):
+            d = lax.rem(m + k, N_CHIP)
+            total = pair_sum[d, :, g].astype(F32) + d_bias[d, c, :, g].astype(F32)
+            pair_sum[d, :, g] = total.astype(BF16)
+            if k < N_CHIP:
+                send(
+                    pair_sum.at[d, :, g],
+                    by_chip.at[k - 1, :, g],
+                    send_sem.at[10],
+                    chip_back.at[g],
+                    d * 2 + c,
+                    s,
+                )
+
+    def add_chips(g):
+        wait_bytes(by_chip.at[:, :, g], chip_back.at[g])
+        total = pair_sum[m, :, g].astype(F32)
+        for k in range(N_CHIP - 1):
+            total = total + by_chip[k, :, g].astype(F32)
+        pair_sum[m, :, g] = total.astype(BF16)
+        for k in range(1, N_SAMPLE):
+            d = sample_peers[k - 1]
+            send(
+                pair_sum.at[m, d, g], by_sample.at[k - 1, g], send_sem.at[11], recv_sem.at[7], t, d
+            )
+
+    pass_bias(0)
+    pass_bias(1)
+
+    @pl.loop(0, 4)
+    def _(g):
+        wait_bytes(bias.at[:, 0, :, g], core_in.at[g])
+        attend(g, q, keys, v, gate, up, bias, gated, d_every, d_bias, bias_rows, bias_total)
+        send(d_bias.at[:, 1 - c, :, g], pair_sum.at[:, :, g], send_sem.at[9], core_back.at[g], other, s)
+
+        @pl.when(g < 2)
+        def _():
+            pass_bias(g + 2)
+
+        @pl.when(g >= 1)
+        def _():
+            add_cores(g - 1)
+
+        @pl.when(g >= 2)
+        def _():
+            add_chips(g - 2)
+
+    add_cores(3)
+    add_chips(2)
+    add_chips(3)
+    wait_bytes(by_sample, recv_sem.at[7])
+    bias_block[...] = pair_sum[m, s].astype(F32) + jnp.sum(by_sample[...].astype(F32), axis=0)
     wait_bytes(mid.at[pl.ds(0, N_SAMPLE - 1)], send_sem.at[0])
     wait_bytes(every_feat.at[pl.ds(0, N_TILE - 1)], send_sem.at[1])
     wait_bytes(every_atom.at[pl.ds(0, N_TILE - 1)], send_sem.at[2])
@@ -303,6 +426,9 @@
     wait_bytes(bias.at[m, c, pl.ds(0, N_SAMPLE - 1)], send_sem.at[6])
     wait_bytes(bias.at[pl.ds(0, N_CHIP - 1), 0], send_sem.at[7])
     wait_bytes(bias.at[:, 0], send_sem.at[8])
+    wait_bytes(pair_sum, send_sem.at[9])
+    wait_bytes(by_chip, send_sem.at[10])
+    wait_bytes(by_sample, send_sem.at[11])
 
 
 def forward(collective_id, *operands):
@@ -312,7 +438,6 @@
         fetching(forward_kernel, len(operands)),
         out_shape=[
             jax.ShapeDtypeStruct((512, 128), F32),
-            jax.ShapeDtypeStruct((N_CHIP, 2, N_SAMPLE, 4, 16, 128), BF16),
             jax.ShapeDtypeStruct((256, 256), BF16),
             jax.ShapeDtypeStruct((256, 256), BF16),
             jax.ShapeDtypeStruct((N_SAMPLE, 16, 512), BF16),
@@ -323,12 +448,11 @@
             jax.ShapeDtypeStruct((768, 512), BF16),
             jax.ShapeDtypeStruct((1, 512), F32),
             jax.ShapeDtypeStruct((768, 512), BF16),
-            jax.ShapeDtypeStruct((768, 512), BF16),
-            jax.ShapeDtypeStruct((768, 512), BF16),
-            jax.ShapeDtypeStruct((768, 512), F32),
+            jax.ShapeDtypeStruct((4, 768, 512), BF16),
+            jax.ShapeDtypeStruct((4, 16, 128), F32),
         ],
         in_specs=[pl.BlockSpec(memory_space=pl.ANY)] * len(operands),
-        out_specs=[vmem] * 15,
+        out_specs=[vmem] * 13,
         scratch_shapes=[
             pltpu.VMEM((N_SAMPLE, 2, 16, 512), BF16),
             pltpu.VMEM((N_SAMPLE, 2, 16, 512), BF16),
@@ -343,93 +467,29 @@
             pltpu.VMEM((N_SAMPLE, 16, 512), BF16),
             pltpu.VMEM((4, 16, 128), F32),
             pltpu.VMEM((4, 16, 128), F32),
-            pltpu.SemaphoreType.DMA((9,)),
-            pltpu.SemaphoreType.DMA((15,)),
+            pltpu.VMEM((N_CHIP, 2, N_SAMPLE, 4, 16, 128), BF16),
+            pltpu.VMEM((768, 512), BF16),
+            pltpu.VMEM((768, 512), BF16),
+            pltpu.VMEM((768, 512), BF16),
+            pltpu.VMEM((768, 512), F32),
+            pltpu.VMEM((GROUP, 256, 256), F32),
+            pltpu.VMEM((GROUP, 256, 256), F32),
+            pltpu.VMEM((N_CHIP, 2, N_SAMPLE, 4, 16, 128), BF16),
+            pltpu.VMEM((N_CHIP, N_SAMPLE, 4, 16, 128), BF16),
+            pltpu.VMEM((N_CHIP - 1, N_SAMPLE, 4, 16, 128), BF16),
+            pltpu.VMEM((N_SAMPLE - 1, 4, 16, 128), BF16),
+            pltpu.SemaphoreType.DMA((12,)),
+            pltpu.SemaphoreType.DMA((8,)),
+            pltpu.SemaphoreType.DMA((4,)),
+            pltpu.SemaphoreType.DMA((4,)),
+            pltpu.SemaphoreType.DMA((4,)),
+            pltpu.SemaphoreType.DMA((4,)),
         ]
         + fetch_scratch(operands),
         compiler_params=pltpu.CompilerParams(
-            collective_id=collective_id, has_side_effects=True, vmem_limit_bytes=40 << 20
+            collective_id=collective_id, has_side_effects=True, vmem_limit_bytes=60 << 20
         ),
     )(*operands)
-
-
-def attention_kernel(q, k, v, gate, up, bias, gated, d_every, d_bias, bias_rows, bias_total):
-    tokens = bias_rows.shape[1]
-    scale = 1.0 / math.sqrt(HEAD)
-    group_of = lax.broadcasted_iota(jnp.int32, (tokens, 128), 1) // LANES
-
-    for half in range(2):
-        parts = [
-            bias[:, :, half * 4 + i, 0].reshape(tokens, 128).astype(F32) for i in range(4)
-        ]
-        for h in range(GROUP):
-            row = parts[0] if h == 0 else pltpu.roll(parts[0], (-h) % 4 * LANES, 1)
-            for i in range(1, 4):
-                shift = (i - h) % 4 * LANES
-                moved = pltpu.roll(parts[i], shift, 1) if shift else parts[i]
-                row = jnp.where(group_of == i, moved, row)
-            bias_rows[h, :, pl.ds(half * 128, 128)] = row
-
-    @pl.loop(0, GROUP)
-    def _(h):
-        rows = pl.ds(pl.multiple_of(h * HEAD, 16), HEAD)
-        for sample in range(2):
-            columns = pl.ds(sample * tokens, tokens)
-            qh, kh, vh = q[rows, columns], k[rows, columns], v[rows, columns]
-            scores = t_dot(qh, kh) * scale + bias_rows[h]
-            weights = jnp.exp(scores - jnp.max(scores, axis=1, keepdims=True))
-            probs = weights * (1.0 / jnp.sum(weights, axis=1, keepdims=True))
-            probs_b = probs.astype(BF16)
-            attended = dot_t(vh, probs_b)
-            gate_h, up_h = gate[rows, columns], up[rows, columns]
-            gated[rows, columns] = (gate_h * attended).astype(BF16)
-            d_att = (up_h * gate_h).astype(BF16)
-            d_every[1, rows, columns] = (up_h * attended * gate_h * (1.0 - gate_h)).astype(BF16)
-            d_probs = t_dot(d_att, vh)
-            inner = jnp.sum(probs * d_probs, axis=1, keepdims=True)
-            d_scores = probs * (d_probs - inner)
-            d_scores_b = d_scores.astype(BF16)
-            d_every[0, rows, columns] = (dot_t(kh, d_scores_b) * scale).astype(BF16)
-            d_every[2, rows, columns] = (dot(qh, d_scores_b) * scale).astype(BF16)
-            d_every[3, rows, columns] = dot(d_att, probs_b).astype(BF16)
-            if sample == 0:
-                bias_total[h] = d_scores
-            else:
-                bias_total[h] = bias_total[h] + d_scores
-
-    for half in range(2):
-        parts = [bias_total[h, :, pl.ds(half * 128, 128)] for h in range(GROUP)]
-        for i in range(4):
-            row = parts[0] if i == 0 else pltpu.roll(parts[0], (-i) % 4 * LANES, 1)
-            for h in range(1, GROUP):
-                shift = (h - i) % 4 * LANES
-                moved = pltpu.roll(parts[h], shift, 1) if shift else parts[h]
-                row = jnp.where(group_of == h, moved, row)
-            d_bias[:, :, half * 4 + i, 0] = row.astype(BF16).reshape(N_CHIP, 2, 16, 128)
-
-
-def attention(q, k, v, gate, up, bias):
-    width, columns = q.shape
-    tokens = columns // 2
-    block = GROUP * HEAD
-    feature = pl.BlockSpec((block, columns), lambda i: (i, 0))
-    of_bias = pl.BlockSpec((N_CHIP, 2, N_SAMPLE, 1, 16, 128), lambda i: (0, 0, 0, i, 0, 0))
-    return pl.pallas_call(
-        attention_kernel,
-        grid=(width // block,),
-        in_specs=[feature] * 5 + [of_bias],
-        out_specs=[feature, pl.BlockSpec((4, block, columns), lambda i: (0, i, 0)), of_bias],
-        out_shape=[
-            jax.ShapeDtypeStruct((width, columns), BF16),
-            jax.ShapeDtypeStruct((4, width, columns), BF16),
-            jax.ShapeDtypeStruct(bias.shape, BF16),
-        ],
-        scratch_shapes=[
-            pltpu.VMEM((GROUP, tokens, tokens), F32),
-            pltpu.VMEM((GROUP, tokens, tokens), F32),
-        ],
-        compiler_params=pltpu.CompilerParams(vmem_limit_bytes=40 << 20),
-    )(q, k, v, gate, up, bias)
 
 
 ROWS = 192
@@ -445,7 +505,7 @@
 
 def backward_kernel(
     need,
-    d_bias,
+    bias_block,
     right_in,
     in_w,
     left_in,
@@ -473,10 +533,6 @@
     out_sum,
     small_sum,
     tri_sum,
-    pair_sum,
-    by_chip,
-    by_sample,
-    bias_block,
     head_rows,
     coefficient,
     keep,
@@ -515,7 +571,6 @@
     atom_grad,
     send_sem,
     recv_sem,
-    chip_sem,
     w_send,
     w_recv,
 ):
@@ -679,70 +734,25 @@
 
     need(1, 2)
     token_product()
-    need(0)
     pl.semaphore_wait(barrier, N_SAMPLE + N_TILE - 1)
-    for k in range(1, N_CHIP + 1):
-        d = lax.rem(m + k, N_CHIP)
-        send(d_bias.at[d, 1 - core], pair_sum.at[d], send_sem.at[0], chip_sem.at[k - 1], partner_t, s)
     need(3, 4, 5)
     form_theirs(0)
-
-    need(*range(6, 22))
+    form_theirs(1)
+    form_theirs(2)
+
+    need(0, *range(6, 22))
     keep[0], inverse_z = norm_rows(pair[...].astype(F32), 1)
     normed_z = keep[0].astype(BF16)
 
     def project(block):
         return dot_t(in_w_t[pl.ds(block * 128, 128), :], normed_z)
 
-    for side in range(2):
-        gate_side = sigmoid(project(2 * side))
-        masked = gate_side * mask[...]
-        coefficient[2 * side] = masked * (1.0 - gate_side) * project(2 * side + 1)
-        coefficient[2 * side + 1] = masked
-    for k in range(1, N_CHIP + 1):
-        d = lax.rem(m + k, N_CHIP)
-        wait_bytes(pair_sum.at[d], chip_sem.at[k - 1])
-        pair_sum[d] = (pair_sum[d].astype(F32) + d_bias[d, core].astype(F32)).astype(BF16)
-        if k < N_CHIP:
-            send(
-                pair_sum.at[d],
-                by_chip.at[k - 1],
-                send_sem.at[1],
-                chip_sem.at[N_CHIP + k - 1],
-                d * 2 + core,
-                s,
-            )
-    form_theirs(1)
-    form_theirs(2)
     keep[1] = sigmoid(dot(normed_z, gate_w[...]))
     keep_p[...], inverse_p = norm_rows(product[...].reshape(128, 512).astype(F32), 0)
     normed_p = keep_p[...].astype(BF16)
     keep[2] = t_dot(normed_p, out_w[...])
     keep[3], inverse_n = norm_rows(following[...], 1)
     normed_n = keep[3].astype(BF16)
-    small[...] = jnp.zeros((128, SMALL), BF16)
-    small_mid[...] = jnp.zeros((16, N_TILE * 128), BF16)
-    form_mine(0)
-    form_mine(1)
-    total = pair_sum[m].astype(F32)
-    for k in range(1, N_CHIP):
-        wait_bytes(by_chip.at[k - 1], chip_sem.at[N_CHIP + k - 1])
-        total = total + by_chip[k - 1].astype(F32)
-    pair_sum[m] = total.astype(BF16)
-    for k in range(1, N_SAMPLE):
-        send(
-            pair_sum.at[m, sample_peers[k - 1]],
-            by_sample.at[k - 1],
-            send_sem.at[2],
-            recv_sem.at[2],
-            t,
-            sample_peers[k - 1],
-        )
-    add_cores(0)
-    form_mine(2)
-    add_cores(1)
-    wait_bytes(by_sample, recv_sem.at[2])
-    bias_block[...] = pair_sum[m, s].astype(F32) + jnp.sum(by_sample[...].astype(F32), axis=0)
 
     for part in range(4):
         rows = [bias_block[:, part * 4 + i] for i in range(4)]
@@ -761,14 +771,16 @@
     for d in sample_peers:
         send(x1.at[d], mid.at[s], send_sem.at[3], recv_sem.at[3], t, d)
     mid[s] = x1[s]
+    small[...] = jnp.zeros((128, SMALL), BF16)
+    small_mid[...] = jnp.zeros((16, N_TILE * 128), BF16)
     d_gate = (d_next * keep[2] * tri_gate * (1.0 - tri_gate)).astype(BF16)
     keep[4] = d_next
     small[:, pl.ds(768, 128)] = t_dot(normed_z, d_gate).astype(BF16)
     small[:, pl.ds(896, 128)] = dot(normed_p, d_linear).astype(BF16)
     small[pl.ds(0, 16), pl.ds(1024, 128)] = (dot(high, normed_n) + dot(low, normed_n)).astype(BF16)
     keep[5] = dot_t(d_gate, gate_w[...])
-    add_cores(2)
-    token_norm()
+    form_mine(0)
+    add_cores(0)
     wait_bytes(mid.at[pl.ds(0, N_SAMPLE - 1)], recv_sem.at[3])
     split_lanes(mid[...].reshape(128, 512).astype(F32), mid_rows)
     for d in range(N_TILE):
@@ -777,7 +789,15 @@
     for d in tile_peers:
         send(x2.at[d], arrived.at[t], send_sem.at[4], recv_sem.at[4], d, s)
     arrived[t] = x2[t]
-    atom_sums()
+    form_mine(1)
+    add_cores(1)
+    form_mine(2)
+    add_cores(2)
+    for side in range(2):
+        gate_side = sigmoid(project(2 * side))
+        masked = gate_side * mask[...]
+        coefficient[2 * side] = masked * (1.0 - gate_side) * project(2 * side + 1)
+        coefficient[2 * side + 1] = masked
     wait_bytes(arrived.at[pl.ds(0, N_TILE - 1)], recv_sem.at[4])
     split_lanes(arrived[...].reshape(128, 512), arrived_rows)
     panel_of(arrived_rows, 0, 8, panel)
@@ -787,13 +807,13 @@
     for d in tile_peers:
         send(x3.at[d], back.at[t], send_sem.at[5], recv_sem.at[5], d, s)
     back[t] = x3[t]
+    token_norm()
+    atom_sums()
     for k in range(1, N_SAMPLE):
         d = sample_peers[k - 1]
         rows = pl.ds(pl.multiple_of(d * 16, 16), 16)
         send(small.at[rows], small_part.at[k - 1], send_sem.at[7], recv_sem.at[7], t, d)
     own = pl.ds(pl.multiple_of(s * 16, 16), 16)
-    add_first(0)
-    add_first(1)
     wait_bytes(back.at[pl.ds(0, N_TILE - 1)], recv_sem.at[5])
     for side in range(2):
         split_lanes(back[:, side].reshape(256, 256).astype(F32), back_rows)
@@ -805,6 +825,8 @@
     for d in sample_peers:
         send(x4.at[d], final.at[s], send_sem.at[6], recv_sem.at[6], t, d)
     final[s] = x4[s]
+    add_first(0)
+    add_first(1)
     add_first(2)
     wait_bytes(small_part, recv_sem.at[7])
     total = small[own, :].astype(F32)
@@ -815,8 +837,6 @@
         d = tile_peers[k - 1]
         lanes = pl.ds(pl.multiple_of(d * 128, 128), 128)
         send(small_mid.at[:, lanes], small_last.at[k - 1], send_sem.at[8], recv_sem.at[8], d, s)
-    add_second(0)
-    add_second(1)
     wait_bytes(final.at[pl.ds(0, N_SAMPLE - 1)], recv_sem.at[6])
     d_normed_z = keep[5]
     for block in range(4):
@@ -828,6 +848,8 @@
         d = sample_peers[k - 1]
         rows = pl.ds(pl.multiple_of(d * 16, 16), 16)
         send(tri.at[rows], tri_part.at[k - 1], send_sem.at[11], recv_sem.at[11], t, d)
+    add_second(0)
+    add_second(1)
     add_second(2)
     grad_pair[...] = keep[4] + norm_back_rows(keep[0], inverse_z, d_normed_z, 1)
     wait_bytes(small_last, recv_sem.at[8])
@@ -839,8 +861,6 @@
     block = small_sum.at[own, lanes]
     for d in tile_peers:
         send(block, block, send_sem.at[9], recv_sem.at[9], d, s)
-    add_third(0)
-    add_third(1)
     wait_bytes(tri_part, recv_sem.at[11])
     total = tri[own, :].astype(F32)
     for k in range(N_SAMPLE - 1):
@@ -848,14 +868,14 @@
     tri_all[t] = total.astype(BF16)
     for d in tile_peers:
         send(tri_all.at[t], tri_all.at[t], send_sem.at[12], recv_sem.at[12], d, s)
-    add_third(2)
-    gather_second(0)
-    gather_second(1)
+    for g in range(3):
+        add_third(g)
+    for g in range(3):
+        gather_second(g)
     wait_bytes(tri_all.at[pl.ds(0, N_TILE - 1)], recv_sem.at[12])
     tri_sum[own, :] = jnp.sum(tri_all[...].astype(F32), axis=0).astype(BF16)
     for d in sample_peers:
         send(tri_sum.at[own], tri_sum.at[own], send_sem.at[13], recv_sem.at[13], t, d)
-    gather_second(2)
     wait_bytes(small_last, recv_sem.at[9])
     known = small_sum.at[own, pl.ds(0, SMALL)]
     for d in sample_peers:
@@ -869,9 +889,6 @@
         wait_bytes(other.at[g], w_recv.at[g, 6])
         unpack(other, g, 1 - core)
 
-    wait_bytes(pair_sum, send_sem.at[0])
-    wait_bytes(by_chip, send_sem.at[1])
-    wait_bytes(by_sample, send_sem.at[2])
     wait_bytes(mid.at[pl.ds(0, N_SAMPLE - 1)], send_sem.at[3])
     wait_bytes(arrived.at[pl.ds(0, N_TILE - 1)], send_sem.at[4])
     wait_bytes(back.at[pl.ds(0, N_TILE - 1)], send_sem.at[5])
@@ -895,7 +912,6 @@
 def backward(collective_id, *operands):
     vmem = pl.BlockSpec(memory_space=pltpu.VMEM)
     chunk = (3, 4, ROWS, WIDTH)
-    block = (4, 16, 128)
     return pl.pallas_call(
         fetching(backward_kernel, len(operands)),
         out_shape=[
@@ -909,10 +925,6 @@
         in_specs=[pl.BlockSpec(memory_space=pl.ANY)] * len(operands),
         out_specs=[vmem] * 6,
         scratch_shapes=[
-            pltpu.VMEM((N_CHIP, N_SAMPLE) + block, BF16),
-            pltpu.VMEM((N_CHIP - 1, N_SAMPLE) + block, BF16),
-            pltpu.VMEM((N_SAMPLE - 1,) + block, BF16),
-            pltpu.VMEM(block, F32),
             pltpu.VMEM((4, 16, 128), F32),
             pltpu.VMEM((4, 128, 512), F32),
             pltpu.VMEM((6, 512, 128), F32),
@@ -951,7 +963,6 @@
             pltpu.VMEM((128, 768), F32),
             pltpu.SemaphoreType.DMA((14,)),
             pltpu.SemaphoreType.DMA((14,)),
-            pltpu.SemaphoreType.DMA((15,)),
             pltpu.SemaphoreType.DMA((7,)),
             pltpu.SemaphoreType.DMA((3, 7)),
         ]
@@ -1009,7 +1020,6 @@
     cot_rows = token_output_cotangent.reshape(-1, token_width)
     (
         following,
-        bias_all,
         left_panel,
         right_panel,
         product,
@@ -1019,10 +1029,9 @@
         token_counts,
         hidden_t,
         inverse_h,
-        queries,
-        keys_all,
-        values_all,
-        gate_values,
+        gated_t,
+        d_every_t,
+        bias_block,
     ) = forward(
         0,
         pair_rows,
@@ -1036,14 +1045,7 @@
         atom_w,
         token_rows,
         attention_input_weight,
-    )
-    gated_t, d_every_t, bias_blocks = attention(
-        queries,
-        keys_all,
-        values_all,
-        gate_values,
         dot_t(attention_output_weight, cot_rows),
-        bias_all,
     )
     d_every_t = d_every_t.reshape(4 * token_width, -1)
     token_output_rows = (
@@ -1053,7 +1055,7 @@
     )
     grad_pair, grad_tokens, in_sum, out_sum, small_sum, tri_sum = backward(
         1,
-        bias_blocks,
+        bias_block,
         d_every_t,
         attention_input_weight,
         hidden_t,

time: 221 us -> 204 us (0.923)
  local copies, waits for them, and re-layouts: 27.2 us -> 12.6 us
  Pallas kernels: 188 us -> 185 us
  matrix products: 1.61 us -> 3.93 us
    pallas_call x1, Pallas kernels: 58 us -> 91.3 us  [forward(): pl.pallas_call(fetching(forward_kernel, len(operands)), out_shape=[jax.Sh...]
    pallas_call x1 -> x0, Pallas kernels: 23.7 us -> none  [attention(): pl.pallas_call(attention_kernel, grid=(width // block,), in_specs=[featur...]
    unnamed x69 -> x31, local copies, waits for them, and re-layouts: 23.2 us -> 9.66 us
    pallas_call x1, Pallas kernels: 102 us -> 89.5 us  [backward(): pl.pallas_call(fetching(backward_kernel, len(operands)), out_shape=[jax.S...]
    dot_general x1, matrix products: 0.8 us -> 3.12 us  [dot_t(): lax.dot_general(a, b, (((1,), (1,)), ((), ())), preferred_element_type=F32)]
where the time goes in v4:
time: 204 us
  Pallas kernels  185 us (91%)
  local copies, waits for them, and re-layouts  12.6 us (6%)
  matrix products  3.93 us (2%)
    pallas_call x1, Pallas kernels, forward(): pl.pallas_call(fetching(forward_kernel, len(operands)), out_shape=[jax.Sh...  91.3 us
    pallas_call x1, Pallas kernels, backward(): pl.pallas_call(fetching(backward_kernel, len(operands)), out_shape=[jax.S...  89.5 us
    unnamed x31, local copies, waits for them, and re-layouts  9.66 us
    pallas_call x1, Pallas kernels, widen(): pl.pallas_call(widen_kernel, grid=(steps,), in_specs=specs, out_specs=spe...  4.66 us

profile of v4, /device:TPU:1, one launch (start us, length us, event | category | flops | bytes accessed | tf_op | source)
XLA Modules:
  0.0 204.1 jit_solution(16993169819122999934)
XLA Ops:
  0.7 1.3 copy-done
  1.9 3.1 %fusion.1.refs_11_ = f32[768,512]{1,0:T(8,128)} fusion(bf16[768,768]{1,0:T(8,128)(2,1)S(1)} %copy-done, bf16[512,768]{1,0:T(8,128)(2,1)} %bitcast.32), kind=kOutput, calls=%fused_computation.4 | convolution fusion | flops 603979776 | bytes 3538944 | tf_op jit(solution)/shard_map/dot_general | solution.py:36
  5.0 0.8 copy.25
  5.8 0.7 reshape.64.refs_2_.refs_8_
  6.5 91.3 %shard_map.221 = (f32[512,128]{1,0:T(8,128)}, bf16[256,256]{1,0:T(8,128)(2,1)}, bf16[256,256]{1,0:T(8,128)(2,1)}, bf16[8,16,512]{2,1,0:T(8,128)(2,1)}, bf16[16,1...) custom-call(bf16[512,128]{1,0:T(8,128)(2,1)} %bitcast.34, ...), custom_call_target="tpu_custom_call" | custom-call | tf_op jit(solution)/shard_map/pallas_call | solution.py:437
  97.7 89.5 %shard_map.222 = (f32[512,128]{1,0:T(8,128)}, f32[512,768]{1,0:T(8,128)}, bf16[768,3072]{1,0:T(8,128)(2,1)}, bf16[768,768]{1,0:T(8,128)(2,1)}, bf16[128,2048]{1,0:T(8,128)(2,1)}, /*index=5*/bf16[128,512]{1,0:T(8,128)(2,1)}) custom-call(f32[4,16,128]{2,1,0:T(8,128)} %get-tuple-element.35.refs_0_, bf16[3072,512]{1,0:T(8,128)(2,1)} %bitcast.24, ...), custom_call_target="tpu_custom_call" | custom-call | tf_op jit(solution)/shard_map/pallas_call | solution.py:915
  187.2 2.3 %copy-done.1 = bf16[768,3072]{1,0:T(8,128)(2,1)S(1)} copy-done((bf16[768,3072]{1,0:T(8,128)(2,1)S(1)}, bf16[768,3072]{1,0:T(8,128)(2,1)}, u32[]{:S(2)}) %copy-start.1) | copy-done | bytes 4718616
  189.6 1.3 copy-done.2
  190.8 4.7 %shard_map.223 = (f32[768,3072]{1,0:T(8,128)}, f32[768,768]{1,0:T(8,128)}) custom-call(bf16[768,3072]{1,0:T(8,128)(2,1)S(1)} %copy-done.1, bf16[768,768]{1,0:T(8,128)(2,1)S(1)} %copy-done.2), custom_call_target="tpu_custom_call" | custom-call | tf_op jit(solution)/shard_map/pallas_call | solution.py:986
  195.5 0.1 convert_element_type.12
  195.6 0.6 slice_bitcast_fusion
  196.2 0.2 copy-done.10
  196.4 0.1 reshape.80
  196.5 0.2 copy.26
  196.6 0.7 copy.29
  197.4 0.8 slice.19
  198.1 0.7 fusion
  198.8 0.8 fusion.2
  199.6 0.3 copy-done.3
  199.9 0.2 copy-done.7
  200.2 1.3 add_add_fusion
  201.5 0.7 copy.33
  202.2 0.7 copy.34
  202.9 1.1 copy.35
  (21 shorter events, 0.0 us)
Async XLA Ops:
  0.6 1.3 copy-start
  1.9 3.1 %copy-start.11 = (bf16[128,512]{1,0:T(8,128)(2,1)S(1)}, bf16[128,512]{1,0:T(8,128)(2,1)}, u32[]{:S(2)}) copy-start(bf16[128,512]{1,0:T(8,128)(2,1)} %param.16) | copy-start | bytes 393220
  1.9 3.9 %copy-start.12 = (s32[16,32]{1,0:T(8,128)S(1)}, s32[16,32]{1,0:T(8,128)}, u32[]{:S(2)}) copy-start(s32[16,32]{1,0:T(8,128)} %param.15) | copy-start | bytes 6148
  187.2 2.3 %copy-start.1 = (bf16[768,3072]{1,0:T(8,128)(2,1)S(1)}, bf16[768,3072]{1,0:T(8,128)(2,1)}, u32[]{:S(2)}) copy-start(bf16[768,3072]{1,0:T(8,128)(2,1)} %get-tuple-element.49.wide) | copy-start | bytes 14155780
  189.6 1.3 copy-start.2
  190.8 4.7 %copy-start.4 = (bf16[128,2048]{1,0:T(8,128)(2,1)S(1)}, bf16[128,2048]{1,0:T(8,128)(2,1)}, u32[]{:S(2)}) copy-start(bf16[128,2048]{1,0:T(8,128)(2,1)} %get-tuple-element.48) | copy-start | bytes 1572868
  195.5 0.9 copy-start.10
  195.6 3.2 %copy-start.8 = (bf16[768,512]{1,0:T(8,128)(2,1)S(1)}, bf16[768,512]{1,0:T(8,128)(2,1)}, u32[]{:S(2)}) copy-start(bf16[768,512]{1,0:T(8,128)(2,1)} %get-tuple-element.34.refs_4_) | copy-start | bytes 2359300
  198.8 1.1 copy-start.3
  198.8 1.4 copy-start.7
  200.2 1.3 copy-start.6
  200.2 2.0 %copy-start.9 = (f32[512,128]{1,0:T(8,128)S(1)}, f32[512,128]{1,0:T(8,128)}, u32[]{:S(2)}) copy-start(f32[512,128]{1,0:T(8,128)} %get-tuple-element.45) | copy-start | bytes 786436
  200.2 2.7 %copy-start.5 = (f32[512,768]{1,0:T(8,128)S(1)}, f32[512,768]{1,0:T(8,128)}, u32[]{:S(2)}) copy-start(f32[512,768]{1,0:T(8,128)} %get-tuple-element.46) | copy-start | bytes 4718596

commit v5 on v4

--- a/solution.py
+++ b/solution.py
@@ -187,7 +187,8 @@
     atom_w,
     tokens,
     in_w,
-    up,
+    out_weight,
+    cot,
     pair_next,
     left,
     right,
@@ -201,6 +202,8 @@
     gated,
     d_every,
     bias_block,
+    grad_tokens,
+    atom_grad,
     x1,
     mid,
     mid_rows,
@@ -225,6 +228,10 @@
     pair_sum,
     by_chip,
     by_sample,
+    up,
+    d_hidden,
+    cond_grad,
+    atom_total,
     send_sem,
     recv_sem,
     chip_in,
@@ -274,6 +281,45 @@
             result = t_dot(in_w[:, columns], hidden_t[...])
             out[rows, :] = (sigmoid(result) if block == 1 else result).astype(out.dtype)
 
+    def token_upstream():
+        @pl.loop(0, 3)
+        def _(a):
+            rows = pl.ds(pl.multiple_of(a * 256, 256), 256)
+            up[rows, :] = dot_t(out_weight[rows, :], cot[...])
+
+    def back_product():
+        @pl.loop(0, 2)
+        def _(a):
+            rows = pl.ds(pl.multiple_of(a * 384, 128), 384)
+            d_hidden[rows, :] = dot(in_w[rows, :], d_every[...].reshape(3072, 512))
+
+    def back_norm():
+        @pl.loop(0, 4)
+        def _(a):
+            lanes = pl.ds(pl.multiple_of(a * 128, 128), 128)
+            back_t = norm_back_rows(
+                hidden_t[:, lanes].astype(F32), inverse_h[:, lanes], d_hidden[:, lanes], 0
+            )
+            grad_tokens[lanes, :] = cot[lanes, :].astype(F32) + back_t.T
+
+        both = grad_tokens[pl.ds(0, 256), :] + grad_tokens[pl.ds(256, 256), :]
+        cond_grad[...] = (both / counts[...]).astype(BF16)
+
+    def back_atoms():
+        atom_total[...] = jnp.zeros_like(atom_total)
+
+        @pl.loop(0, N_TILE)
+        def _(a):
+            feat = every_feat[a]
+            pre = dot(feat, atom_w[...])
+            part = sigmoid(pre)
+            token = lax.broadcasted_iota(jnp.int32, (256, 128), 0)
+            one_hot = jnp.where(token == every_atom[a], 1.0, 0.0).astype(BF16)
+            d_act = t_dot(one_hot, cond_grad[...]) * (part * (1.0 + pre * (1.0 - part)))
+            atom_total[...] += t_dot(feat, d_act.astype(BF16))
+
+        atom_grad[...] = atom_total[...].astype(BF16)
+
     need(0)
     normed_z = norm_rows(pair[...].astype(F32), 1)[0].astype(BF16)
     need(1, 2)
@@ -295,8 +341,9 @@
     every_feat[t] = feats[...]
     every_atom[t] = atoms[...]
     mid[s] = x1[s]
-    need(5, 6, 7, 8, 9, 10, 11)
+    need(5, 6, 7, 8, 9, 10, 11, 12)
     tri_gate = sigmoid(dot(normed_z, gate_w[...]))
+    token_upstream()
     wait_bytes(mid.at[pl.ds(0, N_SAMPLE - 1)], recv_sem.at[0])
     split_lanes(mid[...].reshape(256, 512).astype(F32), mid_rows)
     for d in range(N_TILE):
@@ -412,9 +459,12 @@
         def _():
             add_chips(g - 2)
 
+    back_product()
     add_cores(3)
     add_chips(2)
+    back_norm()
     add_chips(3)
+    back_atoms()
     wait_bytes(by_sample, recv_sem.at[7])
     bias_block[...] = pair_sum[m, s].astype(F32) + jnp.sum(by_sample[...].astype(F32), axis=0)
     wait_bytes(mid.at[pl.ds(0, N_SAMPLE - 1)], send_sem.at[0])
@@ -450,9 +500,11 @@
             jax.ShapeDtypeStruct((768, 512), BF16),
             jax.ShapeDtypeStruct((4, 768, 512), BF16),
             jax.ShapeDtypeStruct((4, 16, 128), F32),
+            jax.ShapeDtypeStruct((512, 768), F32),
+            jax.ShapeDtypeStruct((128, 768), BF16),
         ],
         in_specs=[pl.BlockSpec(memory_space=pl.ANY)] * len(operands),
-        out_specs=[vmem] * 13,
+        out_specs=[vmem] * 15,
         scratch_shapes=[
             pltpu.VMEM((N_SAMPLE, 2, 16, 512), BF16),
             pltpu.VMEM((N_SAMPLE, 2, 16, 512), BF16),
@@ -478,6 +530,10 @@
             pltpu.VMEM((N_CHIP, N_SAMPLE, 4, 16, 128), BF16),
             pltpu.VMEM((N_CHIP - 1, N_SAMPLE, 4, 16, 128), BF16),
             pltpu.VMEM((N_SAMPLE - 1, 4, 16, 128), BF16),
+            pltpu.VMEM((768, 512), F32),
+            pltpu.VMEM((768, 512), F32),
+            pltpu.VMEM((256, 768), BF16),
+            pltpu.VMEM((128, 768), F32),
             pltpu.SemaphoreType.DMA((12,)),
             pltpu.SemaphoreType.DMA((8,)),
             pltpu.SemaphoreType.DMA((4,)),
@@ -507,7 +563,6 @@
     need,
     bias_block,
     right_in,
-    in_w,
     left_in,
     left_out,
     right_out,
@@ -522,13 +577,8 @@
     left,
     right,
     cot_pair,
-    inverse_h,
-    counts,
-    feats,
-    atoms,
-    atom_w,
+    atom_grad,
     grad_pair,
-    grad_tokens,
     in_sum,
     out_sum,
     small_sum,
@@ -566,9 +616,6 @@
     part3,
     full,
     other,
-    d_hidden,
-    cond_grad,
-    atom_grad,
     send_sem,
     recv_sem,
     w_send,
@@ -606,10 +653,6 @@
             target[g, a, :, pl.ds(512, 128)] = dot(left_out[rows, :], right_out[:, narrow]).astype(
                 BF16
             )
-
-    def form_theirs(g):
-        form(g, 1 - core, theirs)
-        send(theirs.at[g], from_core.at[g], w_send.at[0], w_recv.at[g, 0], partner_t, s)
 
     def form_mine(g):
         form(g, core, mine)
@@ -699,48 +742,14 @@
             p1 = lax.rem(place[g] + k, 4)
             send(full.at[g, p1], other.at[g, p1], w_send.at[6], w_recv.at[g, 6], partner_t, s)
 
-    def token_product():
-        @pl.loop(0, 2)
-        def _(a):
-            rows = pl.ds(pl.multiple_of(a * 384, 128), 384)
-            d_hidden[rows, :] = dot(in_w[rows, :], right_in[...])
-
-    def token_norm():
-        @pl.loop(0, 4)
-        def _(a):
-            lanes = pl.ds(pl.multiple_of(a * 128, 128), 128)
-            back_t = norm_back_rows(
-                left_in[:, lanes].astype(F32), inverse_h[:, lanes], d_hidden[:, lanes], 0
-            )
-            grad_tokens[lanes, :] = right_out[lanes, :].astype(F32) + back_t.T
-
-        both = grad_tokens[pl.ds(0, 256), :] + grad_tokens[pl.ds(256, 256), :]
-        cond_grad[...] = (both / counts[...]).astype(BF16)
-
-    def atom_sums():
-        atom_grad[...] = jnp.zeros_like(atom_grad)
-
-        @pl.loop(0, atoms.shape[0])
-        def _(a):
-            feat = feats[a]
-            pre = dot(feat, atom_w[...])
-            part = sigmoid(pre)
-            token = lax.broadcasted_iota(jnp.int32, (256, atoms.shape[2]), 0)
-            one_hot = jnp.where(token == atoms[a], 1.0, 0.0).astype(BF16)
-            d_act = t_dot(one_hot, cond_grad[...]) * (part * (1.0 + pre * (1.0 - part)))
-            atom_grad[...] += t_dot(feat, d_act.astype(BF16))
-
-        small[:, pl.ds(0, 768)] = atom_grad[...].astype(BF16)
-
-    need(1, 2)
-    token_product()
+    need(1, 2, 3, 4)
+    for g in range(3):
+        form(g, 1 - core, theirs)
     pl.semaphore_wait(barrier, N_SAMPLE + N_TILE - 1)
-    need(3, 4, 5)
-    form_theirs(0)
-    form_theirs(1)
-    form_theirs(2)
-
-    need(0, *range(6, 22))
+    for g in range(3):
+        send(theirs.at[g], from_core.at[g], w_send.at[0], w_recv.at[g, 0], partner_t, s)
+
+    need(0, *range(5, 17))
     keep[0], inverse_z = norm_rows(pair[...].astype(F32), 1)
     normed_z = keep[0].astype(BF16)
 
@@ -772,6 +781,7 @@
         send(x1.at[d], mid.at[s], send_sem.at[3], recv_sem.at[3], t, d)
     mid[s] = x1[s]
     small[...] = jnp.zeros((128, SMALL), BF16)
+    small[:, pl.ds(0, 768)] = atom_grad[...]
     small_mid[...] = jnp.zeros((16, N_TILE * 128), BF16)
     d_gate = (d_next * keep[2] * tri_gate * (1.0 - tri_gate)).astype(BF16)
     keep[4] = d_next
@@ -807,8 +817,7 @@
     for d in tile_peers:
         send(x3.at[d], back.at[t], send_sem.at[5], recv_sem.at[5], d, s)
     back[t] = x3[t]
-    token_norm()
-    atom_sums()
+    add_first(0)
     for k in range(1, N_SAMPLE):
         d = sample_peers[k - 1]
         rows = pl.ds(pl.multiple_of(d * 16, 16), 16)
@@ -825,7 +834,6 @@
     for d in sample_peers:
         send(x4.at[d], final.at[s], send_sem.at[6], recv_sem.at[6], t, d)
     final[s] = x4[s]
-    add_first(0)
     add_first(1)
     add_first(2)
     wait_bytes(small_part, recv_sem.at[7])
@@ -916,14 +924,13 @@
         fetching(backward_kernel, len(operands)),
         out_shape=[
             jax.ShapeDtypeStruct((512, 128), F32),
-            jax.ShapeDtypeStruct((512, 768), F32),
             jax.ShapeDtypeStruct((768, 3072), BF16),
             jax.ShapeDtypeStruct((768, 768), BF16),
             jax.ShapeDtypeStruct((128, N_TILE * 128), BF16),
             jax.ShapeDtypeStruct((128, 512), BF16),
         ],
         in_specs=[pl.BlockSpec(memory_space=pl.ANY)] * len(operands),
-        out_specs=[vmem] * 6,
+        out_specs=[vmem] * 5,
         scratch_shapes=[
             pltpu.VMEM((4, 16, 128), F32),
             pltpu.VMEM((4, 128, 512), F32),
@@ -958,9 +965,6 @@
             pltpu.VMEM((3, 4, 48, WIDTH), BF16),
             pltpu.VMEM(chunk, BF16),
             pltpu.VMEM(chunk, BF16),
-            pltpu.VMEM((768, 512), F32),
-            pltpu.VMEM((256, 768), BF16),
-            pltpu.VMEM((128, 768), F32),
             pltpu.SemaphoreType.DMA((14,)),
             pltpu.SemaphoreType.DMA((14,)),
             pltpu.SemaphoreType.DMA((7,)),
@@ -989,7 +993,7 @@
         in_specs=specs,
         out_specs=specs,
         out_shape=[jax.ShapeDtypeStruct(x.shape, F32) for x in (wide, narrow)],
-        compiler_params=pltpu.CompilerParams(vmem_limit_bytes=32 << 20),
+        compiler_params=pltpu.CompilerParams(vmem_limit_bytes=62 << 20),
     )(wide, narrow)
 
 
@@ -1032,6 +1036,8 @@
         gated_t,
         d_every_t,
         bias_block,
+        grad_tokens,
+        atom_grad,
     ) = forward(
         0,
         pair_rows,
@@ -1045,7 +1051,8 @@
         atom_w,
         token_rows,
         attention_input_weight,
-        dot_t(attention_output_weight, cot_rows),
+        attention_output_weight,
+        cot_rows,
     )
     d_every_t = d_every_t.reshape(4 * token_width, -1)
     token_output_rows = (
@@ -1053,11 +1060,10 @@
         + token_cond[None]
         + t_dot(gated_t, attention_output_weight).reshape(tokens.shape)
     )
-    grad_pair, grad_tokens, in_sum, out_sum, small_sum, tri_sum = backward(
+    grad_pair, in_sum, out_sum, small_sum, tri_sum = backward(
         1,
         bias_block,
         d_every_t,
-        attention_input_weight,
         hidden_t,
         gated_t,
         cot_rows,
@@ -1072,11 +1078,7 @@
         left_panel,
         right_panel,
         cot_pair.reshape(-1, hidden),
-        inverse_h,
-        token_counts,
-        every_feat,
-        every_atom,
-        atom_w,
+        atom_grad,
     )
     grad_tokens = grad_tokens.reshape(tokens.shape)
     small_sum = small_sum.astype(F32)

time: 204 us -> 193 us (0.946)
  Pallas kernels: 185 us -> 179 us
  local copies, waits for them, and re-layouts: 12.6 us -> 8.61 us
  matrix products: 3.93 us -> 0.81 us
    pallas_call x1, Pallas kernels: 89.5 us -> 77.5 us  [backward(): pl.pallas_call(fetching(backward_kernel, len(operands)), out_shape=[jax.S...]
    unnamed x31 -> x23, local copies, waits for them, and re-layouts: 9.66 us -> 5.68 us
    dot_general x1 -> x0, matrix products: 3.12 us -> none  [dot_t(): lax.dot_general(a, b, (((1,), (1,)), ((), ())), preferred_element_type=F32)]
    pallas_call x1, Pallas kernels: 4.66 us -> 7.7 us  [widen(): pl.pallas_call(widen_kernel, grid=(steps,), in_specs=specs, out_specs=spe...]
    pallas_call x1, Pallas kernels: 91.3 us -> 93.7 us  [forward(): pl.pallas_call(fetching(forward_kernel, len(operands)), out_shape=[jax.Sh...]
where the time goes in v5:
time: 193 us; the launch traced here: 191 us
  Pallas kernels  179 us (93%)
  local copies, waits for them, and re-layouts  8.61 us (4%)
  other arithmetic  2.13 us (1%)
    pallas_call x1, Pallas kernels, forward(): pl.pallas_call(fetching(forward_kernel, len(operands)), out_shape=[jax.Sh...  93.7 us
    pallas_call x1, Pallas kernels, backward(): pl.pallas_call(fetching(backward_kernel, len(operands)), out_shape=[jax.S...  77.5 us
    pallas_call x1, Pallas kernels, widen(): pl.pallas_call(widen_kernel, grid=(steps,), in_specs=specs, out_specs=spe...  7.7 us
    unnamed x23, local copies, waits for them, and re-layouts  5.68 us

profile of v5, /device:TPU:1, one launch (start us, length us, event | category | flops | bytes accessed | tf_op | source)
XLA Modules:
  0.0 191.2 jit_solution(332577971252164107)
XLA Ops:
  0.6 1.7 copy.25
  2.3 0.7 convert_element_type.10
  3.0 0.7 reshape.64.refs_2_.refs_7_
  3.7 93.7 %shard_map.221 = (f32[512,128]{1,0:T(8,128)}, bf16[256,256]{1,0:T(8,128)(2,1)}, bf16[256,256]{1,0:T(8,128)(2,1)}, bf16[8,16,512]{2,1,0:T(8,128)(2,1)}, bf16[16,1...) custom-call(bf16[512,128]{1,0:T(8,128)(2,1)} %bitcast.32, ...), custom_call_target="tpu_custom_call" | custom-call | tf_op jit(solution)/shard_map/pallas_call | solution.py:487
  97.4 77.5 %shard_map.222 = (f32[512,128]{1,0:T(8,128)}, bf16[768,3072]{1,0:T(8,128)(2,1)}, bf16[768,768]{1,0:T(8,128)(2,1)}, bf16[128,2048]{1,0:T(8,128)(2,1)}, bf16[128,512]{1,0:T(8,128)(2,1)}) custom-call(f32[4,16,128]{2,1,0:T(8,128)} %get-tuple-element.32.refs_0_, bf16[3072,512]{1,0:T(8,128)(2,1)} %bitcast.22, bf16[768,512]{1,0:T(8,128)(2,1)} %get-tuple-element.34.refs_2_, ...), custom_call_target="tpu_custom_call" | custom-call | tf_op jit(solution)/shard_map/pallas_call | solution.py:923
  174.9 7.7 %shard_map.223 = (f32[768,3072]{1,0:T(8,128)}, f32[768,768]{1,0:T(8,128)}) custom-call(bf16[768,3072]{1,0:T(8,128)(2,1)} %get-tuple-element.43.wide, bf16[768,768]{1,0:T(8,128)(2,1)} %get-tuple-element.44.narrow), custom_call_target="tpu_custom_call" | custom-call | tf_op jit(solution)/shard_map/pallas_call | solution.py:990
  182.6 0.1 convert_element_type.12
  182.7 0.0 copy-start.3
  182.8 0.6 slice_bitcast_fusion
  183.4 0.2 copy-done.8
  183.5 0.1 reshape.80
  183.6 0.2 copy.26
  183.8 0.7 copy.29
  184.5 0.8 slice.19
  185.3 0.7 fusion
  185.9 0.0 copy-done.6
  185.9 0.8 fusion.1
  186.8 0.3 copy-done
  187.1 0.2 copy-done.5
  187.3 1.3 add_add_fusion
  188.7 0.7 copy.33
  189.4 0.0 copy-done.7
  189.4 0.7 copy.34
  190.1 1.1 copy.35
  (12 shorter events, 0.0 us)
Async XLA Ops:
  174.9 7.7 %copy-start.1 = (bf16[128,2048]{1,0:T(8,128)(2,1)S(1)}, bf16[128,2048]{1,0:T(8,128)(2,1)}, u32[]{:S(2)}) copy-start(bf16[128,2048]{1,0:T(8,128)(2,1)} %get-tuple-element.42) | copy-start | bytes 1572868
  182.6 0.9 copy-start.8
  182.7 3.2 %copy-start.3 = (bf16[768,768]{1,0:T(8,128)(2,1)S(1)}, bf16[768,768]{1,0:T(8,128)(2,1)}, u32[]{:S(2)}) copy-start(bf16[768,768]{1,0:T(8,128)(2,1)} %refs_11_.1) | copy-start | bytes 3538948
  182.7 3.2 %copy-start.6 = (bf16[768,512]{1,0:T(8,128)(2,1)S(1)}, bf16[768,512]{1,0:T(8,128)(2,1)}, u32[]{:S(2)}) copy-start(bf16[768,512]{1,0:T(8,128)(2,1)} %get-tuple-element.31.refs_3_) | copy-start | bytes 2359300
  185.9 1.1 copy-start
  185.9 1.4 copy-start.5
  187.3 1.3 copy-start.4
  187.3 2.0 %copy-start.7 = (f32[512,128]{1,0:T(8,128)S(1)}, f32[512,128]{1,0:T(8,128)}, u32[]{:S(2)}) copy-start(f32[512,128]{1,0:T(8,128)} %get-tuple-element.39) | copy-start | bytes 786436
  187.3 2.7 %copy-start.2 = (f32[512,768]{1,0:T(8,128)S(1)}, f32[512,768]{1,0:T(8,128)}, u32[]{:S(2)}) copy-start(f32[512,768]{1,0:T(8,128)} %get-tuple-element.40) | copy-start | bytes 4718596

commit v6 on v5

--- a/solution.py
+++ b/solution.py
@@ -404,7 +404,6 @@
             d = lax.rem(m + k, N_CHIP) * 2 + c
             send(bias.at[m, c, :, g], bias.at[m, c, :, g], send_sem.at[7], chip_in.at[g], d, s)
     token_project(3, v)
-    token_project(1, gate)
 
     def pass_bias(g):
         wait_bytes(bias.at[pl.ds(0, N_CHIP - 1), 0, :, g], chip_in.at[g])
@@ -439,6 +438,7 @@
             )
 
     pass_bias(0)
+    token_project(1, gate)
     pass_bias(1)
 
     @pl.loop(0, 4)
@@ -791,6 +791,7 @@
     keep[5] = dot_t(d_gate, gate_w[...])
     form_mine(0)
     add_cores(0)
+    form_mine(1)
     wait_bytes(mid.at[pl.ds(0, N_SAMPLE - 1)], recv_sem.at[3])
     split_lanes(mid[...].reshape(128, 512).astype(F32), mid_rows)
     for d in range(N_TILE):
@@ -799,7 +800,6 @@
     for d in tile_peers:
         send(x2.at[d], arrived.at[t], send_sem.at[4], recv_sem.at[4], d, s)
     arrived[t] = x2[t]
-    form_mine(1)
     add_cores(1)
     form_mine(2)
     add_cores(2)
@@ -818,6 +818,7 @@
         send(x3.at[d], back.at[t], send_sem.at[5], recv_sem.at[5], d, s)
     back[t] = x3[t]
     add_first(0)
+    add_first(1)
     for k in range(1, N_SAMPLE):
         d = sample_peers[k - 1]
         rows = pl.ds(pl.multiple_of(d * 16, 16), 16)
@@ -834,8 +835,8 @@
     for d in sample_peers:
         send(x4.at[d], final.at[s], send_sem.at[6], recv_sem.at[6], t, d)
     final[s] = x4[s]
-    add_first(1)
     add_first(2)
+    add_second(0)
     wait_bytes(small_part, recv_sem.at[7])
     total = small[own, :].astype(F32)
     for k in range(N_SAMPLE - 1):
@@ -856,7 +857,6 @@
         d = sample_peers[k - 1]
         rows = pl.ds(pl.multiple_of(d * 16, 16), 16)
         send(tri.at[rows], tri_part.at[k - 1], send_sem.at[11], recv_sem.at[11], t, d)
-    add_second(0)
     add_second(1)
     add_second(2)
     grad_pair[...] = keep[4] + norm_back_rows(keep[0], inverse_z, d_normed_z, 1)
@@ -869,6 +869,8 @@
     block = small_sum.at[own, lanes]
     for d in tile_peers:
         send(block, block, send_sem.at[9], recv_sem.at[9], d, s)
+    for g in range(3):
+        add_third(g)
     wait_bytes(tri_part, recv_sem.at[11])
     total = tri[own, :].astype(F32)
     for k in range(N_SAMPLE - 1):
@@ -876,8 +878,6 @@
     tri_all[t] = total.astype(BF16)
     for d in tile_peers:
         send(tri_all.at[t], tri_all.at[t], send_sem.at[12], recv_sem.at[12], d, s)
-    for g in range(3):
-        add_third(g)
     for g in range(3):
         gather_second(g)
     wait_bytes(tri_all.at[pl.ds(0, N_TILE - 1)], recv_sem.at[12])
@@ -977,24 +977,72 @@
     )(*operands)
 
 
-def widen_kernel(wide, narrow, wide_out, narrow_out):
+def finish_kernel(
+    wide,
+    narrow,
+    small,
+    tri,
+    gated,
+    weight,
+    tokens,
+    cond,
+    wide_out,
+    narrow_out,
+    tri_out,
+    gate_out,
+    linear_out,
+    bias_out,
+    atom_out,
+    token_out,
+):
+    step = pl.program_id(0)
     wide_out[...] = wide[...].astype(F32)
     narrow_out[...] = narrow[...].astype(F32)
 
-
-def widen(wide, narrow):
-    steps = 6
-    specs = [
+    @pl.when(step == 0)
+    def _():
+        for block in range(4):
+            lanes = pl.ds(block * 128, 128)
+            tri_out[:, lanes] = tri[:, lanes].astype(F32).T
+        atom_out[...] = small[:, pl.ds(0, 768)].astype(F32)
+        gate_out[...] = small[:, pl.ds(768, 128)].astype(F32)
+        linear_out[...] = small[:, pl.ds(896, 128)].astype(F32)
+        bias_out[...] = small[:, pl.ds(1024, 128)].astype(F32).T[:, 0 : bias_out.shape[1]]
+
+    @pl.when(lax.rem(step, 3) == 0)
+    def _():
+        token_out[...] = tokens[...].astype(F32) + cond[...] + t_dot(gated[...], weight[...])
+
+
+def finish(head_count, wide, narrow, small, tri, gated, weight, tokens, cond):
+    steps = 12
+    split = [
         pl.BlockSpec((x.shape[0] // steps, x.shape[1]), lambda i: (i, 0)) for x in (wide, narrow)
     ]
+
+    def whole(shape):
+        return pl.BlockSpec(shape, lambda i: (0, 0))
+
+    rows = pl.BlockSpec((128, 768), lambda i: (i // 3, 0))
+    one = [(128, 512), (128, 128), (128, 128), (128, head_count), (128, 768)]
     return pl.pallas_call(
-        widen_kernel,
+        finish_kernel,
         grid=(steps,),
-        in_specs=specs,
-        out_specs=specs,
-        out_shape=[jax.ShapeDtypeStruct(x.shape, F32) for x in (wide, narrow)],
-        compiler_params=pltpu.CompilerParams(vmem_limit_bytes=62 << 20),
-    )(wide, narrow)
+        in_specs=split
+        + [whole(small.shape), whole(tri.shape)]
+        + [
+            pl.BlockSpec((768, 128), lambda i: (0, i // 3)),
+            whole(weight.shape),
+            rows,
+            pl.BlockSpec((128, 768), lambda i: (lax.rem(i // 3, 2), 0)),
+        ],
+        out_specs=split + [whole(shape) for shape in one] + [rows],
+        out_shape=[
+            jax.ShapeDtypeStruct(shape, F32)
+            for shape in [wide.shape, narrow.shape] + one + [tokens.shape]
+        ],
+        compiler_params=pltpu.CompilerParams(vmem_limit_bytes=60 << 20),
+    )(wide, narrow, small, tri, gated, weight, tokens, cond)
 
 
 def shards(
@@ -1055,11 +1103,6 @@
         cot_rows,
     )
     d_every_t = d_every_t.reshape(4 * token_width, -1)
-    token_output_rows = (
-        tokens.astype(F32)
-        + token_cond[None]
-        + t_dot(gated_t, attention_output_weight).reshape(tokens.shape)
-    )
     grad_pair, in_sum, out_sum, small_sum, tri_sum = backward(
         1,
         bias_block,
@@ -1081,19 +1124,19 @@
         atom_grad,
     )
     grad_tokens = grad_tokens.reshape(tokens.shape)
-    small_sum = small_sum.astype(F32)
-    at = token_width
-    summed = (
-        tri_sum.astype(F32)
-        .reshape(hidden, 4, hidden)
-        .transpose(2, 1, 0)
-        .reshape(hidden, 4 * hidden),
-        small_sum[:, at : at + hidden],
-        small_sum[:, at + hidden : at + 2 * hidden],
-        small_sum[:head_count, at + 2 * hidden : at + 3 * hidden].T,
-        small_sum[:, :at],
-        *widen(in_sum, out_sum),
+    in_grad, out_grad, *others, token_output_rows = finish(
+        head_count,
+        in_sum,
+        out_sum,
+        small_sum,
+        tri_sum,
+        gated_t,
+        attention_output_weight,
+        token_rows,
+        token_cond,
     )
+    summed = (*others, in_grad, out_grad)
+    token_output_rows = token_output_rows.reshape(tokens.shape)
     pair_next, grad_pair = following.reshape(pair.shape), grad_pair.reshape(pair.shape)
     return (pair_next, token_output_rows, grad_pair, grad_tokens) + summed
 

time: 193 us -> 193 us (level)
  Pallas kernels: 179 us -> 185 us
  local copies, waits for them, and re-layouts: 8.61 us -> 6.39 us
    pallas_call x1, Pallas kernels: 7.7 us -> 13.6 us  [finish(): pl.pallas_call(finish_kernel, grid=(steps,), in_specs=split + [whole(smal...]
    unnamed x23 -> x11, local copies, waits for them, and re-layouts: 5.68 us -> 5.73 us
where the time goes in v6:
time: 193 us
  Pallas kernels  185 us (96%)
  local copies, waits for them, and re-layouts  6.39 us (3%)
    pallas_call x1, Pallas kernels, forward(): pl.pallas_call(fetching(forward_kernel, len(operands)), out_shape=[jax.Sh...  93.8 us
    pallas_call x1, Pallas kernels, backward(): pl.pallas_call(fetching(backward_kernel, len(operands)), out_shape=[jax.S...  77.4 us
    pallas_call x1, Pallas kernels, finish(): pl.pallas_call(finish_kernel, grid=(steps,), in_specs=split + [whole(smal...  13.6 us
    unnamed x11, local copies, waits for them, and re-layouts  5.73 us

profile of v6, /device:TPU:1, one launch (start us, length us, event | category | flops | bytes accessed | tf_op | source)
XLA Modules:
  0.0 192.6 jit_solution(10588018591886031170)
XLA Ops:
  0.6 0.7 convert_element_type.3
  1.3 0.7 reshape.53.refs_2_.refs_7_
  2.0 1.7 copy.25
  3.7 93.8 %shard_map.221 = (f32[512,128]{1,0:T(8,128)}, bf16[256,256]{1,0:T(8,128)(2,1)}, bf16[256,256]{1,0:T(8,128)(2,1)}, bf16[8,16,512]{2,1,0:T(8,128)(2,1)}, bf16[16,1...) custom-call(bf16[512,128]{1,0:T(8,128)(2,1)} %bitcast.21, ...), custom_call_target="tpu_custom_call" | custom-call | tf_op jit(solution)/shard_map/pallas_call | solution.py:487
  97.4 77.4 %shard_map.222 = (f32[512,128]{1,0:T(8,128)}, bf16[768,3072]{1,0:T(8,128)(2,1)}, bf16[768,768]{1,0:T(8,128)(2,1)}, bf16[128,2048]{1,0:T(8,128)(2,1)}, bf16[128,512]{1,0:T(8,128)(2,1)}) custom-call(f32[4,16,128]{2,1,0:T(8,128)} %get-tuple-element.36.refs_0_, bf16[3072,512]{1,0:T(8,128)(2,1)} %bitcast.14, bf16[768,512]{1,0:T(8,128)(2,1)} %get-tuple-element.38.refs_2_, ...), custom_call_target="tpu_custom_call" | custom-call | tf_op jit(solution)/shard_map/pallas_call | solution.py:923
  174.8 0.0 copy-start.1
  174.9 0.0 copy-start.2
  174.9 0.0 copy-start
  174.9 13.6 %shard_map.223 = (f32[768,3072]{1,0:T(8,128)}, f32[768,768]{1,0:T(8,128)}, f32[128,512]{1,0:T(8,128)}, f32[128,128]{1,0:T(8,128)}, f32[128,128]{1,0:T(8,128)}, /...) custom-call(bf16[768,3072]{1,0:T(8,128)(2,1)} %get-tuple-element.44.wide, ...), custom_call_target="tpu_custom_call" | custom-call | tf_op jit(solution)/shard_map/pallas_call | solution.py:1028
  188.5 1.5 copy.26
  190.0 0.0 copy-done.1
  190.0 0.7 copy.30
  190.7 0.0 copy-done.2
  190.7 0.7 copy.31
  191.4 0.0 copy-done
  191.4 1.1 copy.32
Async XLA Ops:
  174.8 15.2 %copy-start.1 = (f32[512,128]{1,0:T(8,128)S(1)}, f32[512,128]{1,0:T(8,128)}, u32[]{:S(2)}) copy-start(f32[512,128]{1,0:T(8,128)} %get-tuple-element.35.refs_11_) | copy-start | bytes 786436
  174.9 15.9 %copy-start.2 = (f32[512,128]{1,0:T(8,128)S(1)}, f32[512,128]{1,0:T(8,128)}, u32[]{:S(2)}) copy-start(f32[512,128]{1,0:T(8,128)} %get-tuple-element.50) | copy-start | bytes 786436
  174.9 16.6 %copy-start = (f32[512,768]{1,0:T(8,128)S(1)}, f32[512,768]{1,0:T(8,128)}, u32[]{:S(2)}) copy-start(f32[512,768]{1,0:T(8,128)} %get-tuple-element.51) | copy-start | bytes 4718596

commit v7 on v6

--- a/solution.py
+++ b/solution.py
@@ -1009,13 +1009,11 @@
         linear_out[...] = small[:, pl.ds(896, 128)].astype(F32)
         bias_out[...] = small[:, pl.ds(1024, 128)].astype(F32).T[:, 0 : bias_out.shape[1]]
 
-    @pl.when(lax.rem(step, 3) == 0)
-    def _():
-        token_out[...] = tokens[...].astype(F32) + cond[...] + t_dot(gated[...], weight[...])
+    token_out[...] = tokens[...].astype(F32) + cond[...] + t_dot(gated[...], weight[...])
 
 
 def finish(head_count, wide, narrow, small, tri, gated, weight, tokens, cond):
-    steps = 12
+    steps = 4
     split = [
         pl.BlockSpec((x.shape[0] // steps, x.shape[1]), lambda i: (i, 0)) for x in (wide, narrow)
     ]
@@ -1023,7 +1021,7 @@
     def whole(shape):
         return pl.BlockSpec(shape, lambda i: (0, 0))
 
-    rows = pl.BlockSpec((128, 768), lambda i: (i // 3, 0))
+    rows = pl.BlockSpec((128, 768), lambda i: (i, 0))
     one = [(128, 512), (128, 128), (128, 128), (128, head_count), (128, 768)]
     return pl.pallas_call(
         finish_kernel,
@@ -1031,10 +1029,10 @@
         in_specs=split
         + [whole(small.shape), whole(tri.shape)]
         + [
-            pl.BlockSpec((768, 128), lambda i: (0, i // 3)),
+            pl.BlockSpec((768, 128), lambda i: (0, i)),
             whole(weight.shape),
             rows,
-            pl.BlockSpec((128, 768), lambda i: (lax.rem(i // 3, 2), 0)),
+            pl.BlockSpec((128, 768), lambda i: (lax.rem(i, 2), 0)),
         ],
         out_specs=split + [whole(shape) for shape in one] + [rows],
         out_shape=[

time: 193 us -> 189 us (0.979)
  Pallas kernels: 185 us -> 181 us
    pallas_call x1, Pallas kernels: 13.6 us -> 9.87 us  [finish(): pl.pallas_call(finish_kernel, grid=(steps,), in_specs=split + [whole(smal...]
where the time goes in v7:
time: 189 us
  Pallas kernels  181 us (96%)
  local copies, waits for them, and re-layouts  6.39 us (3%)
    pallas_call x1, Pallas kernels, forward(): pl.pallas_call(fetching(forward_kernel, len(operands)), out_shape=[jax.Sh...  93.8 us
    pallas_call x1, Pallas kernels, backward(): pl.pallas_call(fetching(backward_kernel, len(operands)), out_shape=[jax.S...  77.4 us
    pallas_call x1, Pallas kernels, finish(): pl.pallas_call(finish_kernel, grid=(steps,), in_specs=split + [whole(smal...  9.87 us
    unnamed x11, local copies, waits for them, and re-layouts  5.73 us

profile of v7, /device:TPU:1, one launch (start us, length us, event | category | flops | bytes accessed | tf_op | source)
XLA Modules:
  0.0 188.8 jit_solution(5660562546687182788)
XLA Ops:
  0.6 0.7 convert_element_type.3
  1.3 0.7 reshape.53.refs_2_.refs_7_
  2.0 1.7 copy.25
  3.7 93.8 %shard_map.221 = (f32[512,128]{1,0:T(8,128)}, bf16[256,256]{1,0:T(8,128)(2,1)}, bf16[256,256]{1,0:T(8,128)(2,1)}, bf16[8,16,512]{2,1,0:T(8,128)(2,1)}, bf16[16,1...) custom-call(bf16[512,128]{1,0:T(8,128)(2,1)} %bitcast.21, ...), custom_call_target="tpu_custom_call" | custom-call | tf_op jit(solution)/shard_map/pallas_call | solution.py:487
  97.4 77.4 %shard_map.222 = (f32[512,128]{1,0:T(8,128)}, bf16[768,3072]{1,0:T(8,128)(2,1)}, bf16[768,768]{1,0:T(8,128)(2,1)}, bf16[128,2048]{1,0:T(8,128)(2,1)}, bf16[128,512]{1,0:T(8,128)(2,1)}) custom-call(f32[4,16,128]{2,1,0:T(8,128)} %get-tuple-element.36.refs_0_, bf16[3072,512]{1,0:T(8,128)(2,1)} %bitcast.14, bf16[768,512]{1,0:T(8,128)(2,1)} %get-tuple-element.38.refs_2_, ...), custom_call_target="tpu_custom_call" | custom-call | tf_op jit(solution)/shard_map/pallas_call | solution.py:923
  174.8 0.0 copy-start.1
  174.9 0.0 copy-start.2
  174.9 0.0 copy-start
  174.9 9.9 %shard_map.223 = (f32[768,3072]{1,0:T(8,128)}, f32[768,768]{1,0:T(8,128)}, f32[128,512]{1,0:T(8,128)}, f32[128,128]{1,0:T(8,128)}, f32[128,128]{1,0:T(8,128)}, /...) custom-call(bf16[768,3072]{1,0:T(8,128)(2,1)} %get-tuple-element.44.wide, ...), custom_call_target="tpu_custom_call" | custom-call | tf_op jit(solution)/shard_map/pallas_call | solution.py:1026
  184.7 1.5 copy.26
  186.2 0.0 copy-done.1
  186.2 0.7 copy.30
  187.0 0.0 copy-done.2
  187.0 0.7 copy.31
  187.7 0.0 copy-done
  187.7 1.1 copy.32
Async XLA Ops:
  174.8 11.4 %copy-start.1 = (f32[512,128]{1,0:T(8,128)S(1)}, f32[512,128]{1,0:T(8,128)}, u32[]{:S(2)}) copy-start(f32[512,128]{1,0:T(8,128)} %get-tuple-element.35.refs_11_) | copy-start | bytes 786436
  174.9 12.1 %copy-start.2 = (f32[512,128]{1,0:T(8,128)S(1)}, f32[512,128]{1,0:T(8,128)}, u32[]{:S(2)}) copy-start(f32[512,128]{1,0:T(8,128)} %get-tuple-element.50) | copy-start | bytes 786436
  174.9 12.8 %copy-start = (f32[512,768]{1,0:T(8,128)S(1)}, f32[512,768]{1,0:T(8,128)}, u32[]{:S(2)}) copy-start(f32[512,768]{1,0:T(8,128)} %get-tuple-element.51) | copy-start | bytes 4718596
